TPU v7x, 32 devices: a whole 2x2x4 slice. The times are simulated.
32 devices in a mesh: tm: 4 (over z), state: 4 (over y, x), outputs: 2 (over core).
Axes of the slice: x: 2, y: 2, z: 4, core: 2. Of those that a mesh axis runs over, the one named last changes fastest.
Arguments:
- observations: float32 [48, 512], P('tm', 'outputs'), may hold values from -6 to 6
- observed: int32 [48, 512], P('tm', 'outputs'), may hold values 0 or 1
- loadings: float32 [48, 512, 512], P('tm', 'outputs'), may hold values from -0.25 to 0.25
- noise_precision: float32 [512], P('outputs'), may hold values from 0.25 to 1
- blend_matrix: float32 [512, 512], replicated, may hold values from -0.02 to 0.1, as said below
- latent_rates: float32 [4], replicated, may hold values from 0.03 to 1
- pair_latent: int32 [256], replicated, may hold values from 0 to 3
- initial_mean: float32 [512], replicated, may hold values from -6 to 6
Outputs:
- states: float32 [48, 512], P('tm', 'state')
- predicted: float32 [48, 512], P('tm', 'outputs')
Inputs may be any that keep to these rules, and one draw needn't show every extreme that they name: `blend_matrix`: symmetric, positive definite.
All inputs are finite; a program needn't handle non-finite values. No bound on the sum of `observed` on one device may be relied on, other than what follows from the above.
Results may differ from a plain program's by a relative error of at most 0.0003.
Values sent between devices are 32-bit elements; how exact they have to be, the bound alone decides.
No kernel may reach another device: no remote copies, remote signals or barrier semaphores. Data moves between devices by JAX's collectives and lax.ppermute only.
A program may use at most 128 MiB of HBM per device.

v0:
```python
import jax
import jax.numpy as jnp
from jax import lax
from jax.sharding import PartitionSpec as P

HIGHEST_PRECISION = lax.Precision.HIGHEST


def from_behind(value, axis, steps):
    count = lax.axis_size(axis)
    initial, last = (max(0, -steps), min(count, count - steps))
    return lax.ppermute(value, axis, [(source, source + steps) for source in range(initial, last)])


def transition_parts(latent_rates, pair_latent):
    latent_ids = jnp.arange(latent_rates.shape[0], dtype=jnp.int32)
    one_hot = (pair_latent[:, None] == latent_ids[None, :]).astype(jnp.float32)
    pair_rate = jnp.sum(one_hot * latent_rates[None, :], axis=1)
    damping = jnp.exp(-pair_rate)
    diagonal_part = jnp.stack(
        [damping * (1.0 + pair_rate), damping * (1.0 - pair_rate)], axis=1
    ).reshape(-1)
    cross_part = jnp.stack([damping, -damping * pair_rate * pair_rate], axis=1).reshape(-1)
    return (diagonal_part, cross_part)


def right_transition(matrix, diagonal_part, cross_part):
    full_shape = matrix.shape
    swapped = matrix.reshape(full_shape[:-1] + (full_shape[-1] // 2, 2))[..., ::-1].reshape(
        full_shape
    )
    return matrix * diagonal_part + swapped * cross_part


def propagate(state_in, transit, shifts):

    def advance(current, inputs):
        step_transit, step_shift = inputs
        state_new = jnp.dot(current, step_transit, precision=HIGHEST_PRECISION) + step_shift
        return (state_new, state_new)

    return lax.scan(advance, state_in, (transit, shifts))


def per_device(
    observations,
    observed,
    loadings,
    noise_precision,
    blend_matrix,
    latent_rates,
    pair_latent,
    initial_mean,
):
    state_width = loadings.shape[2]
    row_share = state_width // lax.axis_size("state")
    row_start = lax.axis_index("state") * row_share
    diagonal_part, cross_part = transition_parts(latent_rates, pair_latent)
    weight = observed.astype(jnp.float32) * noise_precision[None, :]
    signal = weight * observations
    scaled = loadings * weight[:, :, None]
    own_columns = lax.dynamic_slice_in_dim(loadings, row_start, row_share, 2)
    info_rows = jnp.einsum(
        "kor,kot->krt",
        lax.dynamic_slice_in_dim(scaled, row_start, row_share, 2),
        loadings,
        precision=HIGHEST_PRECISION,
    )
    vector_rows = jnp.einsum("ko,kor->kr", signal, own_columns, precision=HIGHEST_PRECISION)
    info_rows, vector_rows = lax.psum((info_rows, vector_rows), "outputs")
    unit_rows = (
        jnp.arange(row_share, dtype=jnp.int32)[:, None] + row_start
        == jnp.arange(state_width, dtype=jnp.int32)[None, :]
    ).astype(jnp.float32)
    blended = jnp.einsum("krt,tu->kru", info_rows, blend_matrix, precision=HIGHEST_PRECISION)
    transit_rows = right_transition(unit_rows[None, :, :] - blended, diagonal_part, cross_part)
    transit, info_vector = (
        lax.all_gather(transit_rows, "state", axis=1, tiled=True),
        lax.all_gather(vector_rows, "state", axis=1, tiled=True),
    )
    shifts = right_transition(
        jnp.dot(info_vector, blend_matrix, precision=HIGHEST_PRECISION), diagonal_part, cross_part
    )
    position = lax.axis_index("tm")
    chain_length = lax.axis_size("tm")

    def round_body(round_index, loop_state):
        received = from_behind(loop_state[1], "tm", 1)
        entering = jnp.where(position == 0, initial_mean, received)
        leaving, _ = propagate(entering, transit, shifts)
        return (entering, leaving)

    state_in, _ = lax.fori_loop(0, chain_length, round_body, (initial_mean, initial_mean))
    _, trajectory = propagate(state_in, transit, shifts)
    own_states = lax.dynamic_slice_in_dim(trajectory, row_start, row_share, 1)
    predicted = jnp.einsum("ks,kos->ko", trajectory, loadings, precision=HIGHEST_PRECISION)
    return (own_states, predicted)


def solution(mesh):
    placed = (
        P("tm", "outputs"),
        P("tm", "outputs"),
        P("tm", "outputs", None),
        P("outputs"),
        P(),
        P(),
        P(),
        P(),
    )
    return jax.shard_map(
        per_device,
        mesh=mesh,
        in_specs=placed,
        out_specs=(P("tm", "state"), P("tm", "outputs")),
        check_vma=False,
    )
```

profile of v0, /device:TPU:24, one launch (start us, length us, event | category | flops | bytes accessed | tf_op | source)
XLA Modules:
  0.0 364.5 jit_solution(15939639057552873446)
XLA Ops:
  10.5 8.7 %fusion.8 = f32[12,128,512]{2,1,0:T(8,128)} fusion(f32[12,256,512]{2,1,0:T(8,128)} %param.16, f32[12,256,128]{1,2,0:T(8,128)} %copy.27, f32[12,256]{1,0:T(8,128)S(1)} %get-tuple-element.167), kind=kOutput, calls=%fused_computation.13 | convolution fusion | flops 2416312320 | bytes 11022336 | tf_op jit(solution)/shard_map/kor,kot->krt/dot_general | solution.py:63
  20.7 23.2 %all-reduce.2.cloned.1.call-done = f32[12,128,512]{2,1,0:T(8,128)} async-done(((f32[12,128,512]{2,1,0:T(8,128)}), f32[12,128,512]{2,1,0:T(8,128)}) %all-reduce.2.cloned.1.call-update) | async-done | bytes 3145744 | tf_op jit(solution)/shard_map/psum | solution.py:70
  43.9 7.9 %convolution_subtract_fusion = f32[12,128,512]{2,1,0:T(8,128)} fusion(f32[12,128,512]{2,1,0:T(8,128)} %all-reduce.2.cloned.1.call-done, f32[128,512]{1,0:T(8,128)S(1)} %fusion.12, f32[512,512]{1,0:T(8,128)S(1)} %copy-done), kind=kOutput, calls=%fused_computation.12 | convolution fusion | flops 4832624640 | bytes 7602176 | tf_op jit(solution)/shard_map/krt,tu->kru/dot_general | solution.py:75
  51.8 3.6 copy.18
  55.4 16.8 %rev.6 = f32[12,128,256,2]{1,3,2,0:T(2,128)} reverse(f32[12,128,256,2]{1,3,2,0:T(2,128)} %bitcast.61), dimensions={3} | reverse | bytes 6291456 | tf_op jit(solution)/shard_map/rev | solution.py:29
  72.2 3.5 copy.20
  75.7 5.3 %multiply_add_fusion = f32[12,128,512]{2,1,0:T(8,128)} fusion(f32[12,128,512]{2,1,0:T(8,128)} %copy.20, f32[12,128,512]{2,1,0:T(8,128)} %convolution_subtract_fusion, f32[512]{0:T(512)S(1)} %mul.120, f32[512]{0:T(512)S(1)} %mul.115), kind=kLoop, calls=%fused_computation.11 | loop fusion | flops 2359296 | bytes 9441280 | tf_op jit(solution)/shard_map/add | solution.py:32
  83.1 2.5 psum.15
  85.6 8.4 %all_gather.7 = f32[12,512]{1,0:T(8,128)S(1)} all-gather(f32[12,128]{1,0:T(8,128)S(1)} %psum.15), channel_id=1, replica_groups=mesh['tm'=4,'state'=4,'outputs'=2] {'state'}, dimensions={1}, use_global_device_ids=true | all-gather | bytes 30720 | tf_op jit(solution)/shard_map/all_gather | solution.py:79
  95.5 109.1 %all-gather.2.cloned.1.call-done = f32[12,512,512]{2,1,0:T(8,128)} async-done(((f32[12,128,512]{2,1,0:T(8,128)}), f32[12,512,512]{2,1,0:T(8,128)}) %all-gather.2.cloned.1.call-update) | async-done | bytes 12582928 | tf_op jit(solution)/shard_map/all_gather | solution.py:78
  204.6 114.1 %while.42 = (s32[]{:T(128)}, f32[512]{0:T(512)}, f32[512]{0:T(512)S(1)}, pred[]{:T(512)}, f32[512]{0:T(512)S(1)}, /*index=5*/f32[12,512,512]{2,1,0:T(8,128)}, f3...) while((s32[]{:T(128)}, f32[512]{0:T(512)}, f32[512]{0:T(512)S(1)}, pred[]{:T(512)}, f32[512]{0:T(512)S(1)}, ...), condition=%wide.region_6.7_spmd, body=%wide.region_3.6_spmd.sunk | while | flops 3146756 | bytes 1089831 | solution.py:93
  205.9 4.2 %collective-permute-done = f32[512]{0:T(512)S(1)} collective-permute-done((f32[512]{0:T(512)S(1)}, f32[512]{0:T(512)S(1)}, u32[]{:S(2)}, u32[]{:S(2)}) %collective-permute-start) | collective-permute-done | bytes 2080 | tf_op jit(solution)/shard_map/while/body/eval_jaxpr/ppermute | solution.py:12
  210.0 23.0 %while.44 = (s32[]{:T(128)}, f32[512]{0:T(512)S(1)}, f32[12,512,512]{2,1,0:T(8,128)}, f32[12,512]{1,0:T(8,128)S(1)}, s32[]{:T(128)}) while((s32[]{:T(128)}, f32[512]{0:T(512)S(1)}, f32[12,512,512]{2,1,0:T(8,128)}, f32[12,512]{1,0:T(8,128)S(1)}, s32[]{:T(128)}) %tuple.63), condition=%wide.region_5.5_spmd, body=%wide.region_4.4_spmd.sunk | while | flops 3146242 | bytes 1062989 | solution.py:42
  210.1 1.9 fusion.37
  212.0 1.9 fusion.37
  213.9 1.9 fusion.37
  215.8 1.9 fusion.37
  217.7 1.9 fusion.37
  219.7 1.9 fusion.37
  221.6 1.9 fusion.37
  223.5 1.9 fusion.37
  225.4 1.9 fusion.37
  227.3 1.9 fusion.37
  229.2 1.9 fusion.37
  231.2 1.9 fusion.37
  234.4 4.2 %collective-permute-done = f32[512]{0:T(512)S(1)} collective-permute-done((f32[512]{0:T(512)S(1)}, f32[512]{0:T(512)S(1)}, u32[]{:S(2)}, u32[]{:S(2)}) %collective-permute-start) | collective-permute-done | bytes 2080 | tf_op jit(solution)/shard_map/while/body/eval_jaxpr/ppermute | solution.py:12
  238.6 23.0 %while.44 = (s32[]{:T(128)}, f32[512]{0:T(512)S(1)}, f32[12,512,512]{2,1,0:T(8,128)}, f32[12,512]{1,0:T(8,128)S(1)}, s32[]{:T(128)}) while((s32[]{:T(128)}, f32[512]{0:T(512)S(1)}, f32[12,512,512]{2,1,0:T(8,128)}, f32[12,512]{1,0:T(8,128)S(1)}, s32[]{:T(128)}) %tuple.63), condition=%wide.region_5.5_spmd, body=%wide.region_4.4_spmd.sunk | while | flops 3146242 | bytes 1062989 | solution.py:42
  238.6 1.9 fusion.37
  240.5 1.9 fusion.37
  242.4 1.9 fusion.37
  244.4 1.9 fusion.37
  246.3 1.9 fusion.37
  248.2 1.9 fusion.37
  250.1 1.9 fusion.37
  252.0 1.9 fusion.37
  253.9 1.9 fusion.37
  255.9 1.9 fusion.37
  257.8 1.9 fusion.37
  259.7 1.9 fusion.37
  262.9 4.2 %collective-permute-done = f32[512]{0:T(512)S(1)} collective-permute-done((f32[512]{0:T(512)S(1)}, f32[512]{0:T(512)S(1)}, u32[]{:S(2)}, u32[]{:S(2)}) %collective-permute-start) | collective-permute-done | bytes 2080 | tf_op jit(solution)/shard_map/while/body/eval_jaxpr/ppermute | solution.py:12
  267.1 23.0 %while.44 = (s32[]{:T(128)}, f32[512]{0:T(512)S(1)}, f32[12,512,512]{2,1,0:T(8,128)}, f32[12,512]{1,0:T(8,128)S(1)}, s32[]{:T(128)}) while((s32[]{:T(128)}, f32[512]{0:T(512)S(1)}, f32[12,512,512]{2,1,0:T(8,128)}, f32[12,512]{1,0:T(8,128)S(1)}, s32[]{:T(128)}) %tuple.63), condition=%wide.region_5.5_spmd, body=%wide.region_4.4_spmd.sunk | while | flops 3146242 | bytes 1062989 | solution.py:42
  267.1 1.9 fusion.37
  269.1 1.9 fusion.37
  271.0 1.9 fusion.37
  272.9 1.9 fusion.37
  274.8 1.9 fusion.37
  276.7 1.9 fusion.37
  278.6 1.9 fusion.37
  280.6 1.9 fusion.37
  282.5 1.9 fusion.37
  288.2 1.9 fusion.37
  291.5 4.2 %collective-permute-done = f32[512]{0:T(512)S(1)} collective-permute-done((f32[512]{0:T(512)S(1)}, f32[512]{0:T(512)S(1)}, u32[]{:S(2)}, u32[]{:S(2)}) %collective-permute-start) | collective-permute-done | bytes 2080 | tf_op jit(solution)/shard_map/while/body/eval_jaxpr/ppermute | solution.py:12
  295.7 23.0 %while.44 = (s32[]{:T(128)}, f32[512]{0:T(512)S(1)}, f32[12,512,512]{2,1,0:T(8,128)}, f32[12,512]{1,0:T(8,128)S(1)}, s32[]{:T(128)}) while((s32[]{:T(128)}, f32[512]{0:T(512)S(1)}, f32[12,512,512]{2,1,0:T(8,128)}, f32[12,512]{1,0:T(8,128)S(1)}, s32[]{:T(128)}) %tuple.63), condition=%wide.region_5.5_spmd, body=%wide.region_4.4_spmd.sunk | while | flops 3146242 | bytes 1062989 | solution.py:42
  295.7 1.9 fusion.37
  301.4 1.9 fusion.37
  303.3 1.9 fusion.37
  307.2 1.9 fusion.37
  309.1 1.9 fusion.37
  311.0 1.9 fusion.37
  314.8 1.9 fusion.37
  316.8 1.9 fusion.37
  318.7 29.8 %while.43 = (s32[]{:T(128)}, f32[512]{0:T(512)}, f32[12,512]{1,0:T(8,128)S(1)}, f32[12,512,512]{2,1,0:T(8,128)}, f32[12,512]{1,0:T(8,128)S(1)}, /*index=5*/s32[]{:T(128)}, s32[]{:T(128)}) while((s32[]{:T(128)}, f32[512]{0:T(512)}, f32[12,512]{1,0:T(8,128)S(1)}, f32[12,512,512]{2,1,0:T(8,128)}, f32[12,512]{1,0:T(8,128)S(1)}, ...), condition=%wide.region_8.9_spmd, body=%wide.region_7.8_spmd.sunk | while | flops 3146242 | bytes 1075325 | solution.py:42
  318.7 1.9 fusion.34
  349.1 7.9 %fusion.13 = f32[12,1,256]{2,1,0:T(1,128)S(1)} fusion(f32[12,256,512]{2,1,0:T(8,128)} %param.16, f32[12,512,1]{1,0,2:T(8,128)S(1)} %bitcast.71), kind=kOutput, calls=%fused_computation.20 | convolution fusion | flops 18874368 | bytes 6328320 | tf_op jit(solution)/shard_map/ks,kos->ko/dot_general | solution.py:96
  (235 shorter events, 54.2 us)
Async XLA Ops:
  7.2 36.7 %copy-start = (f32[512,512]{1,0:T(8,128)S(1)}, f32[512,512]{1,0:T(8,128)}, u32[]{:S(2)}) copy-start(f32[512,512]{1,0:T(8,128)} %param.18) | copy-start | bytes 3145732
  7.2 36.7 %all-reduce.2.cloned.1.call-start = ((), (), s32[]{:S(2)}) async-start(), calls=%async_computation | async-start | bytes 6291456 | tf_op jit(solution)/shard_map/psum | solution.py:70
  7.2 3.3 copy-start.4
  7.2 3.2 copy-start.5
  7.3 3.2 copy-start.6
  19.2 0.7 copy-start.7
  19.2 0.7 copy-start.8
  19.2 185.3 %all-gather.2.cloned.1.call-start = ((), (), s32[]{:S(2)}) async-start(), calls=%async_computation.1 | async-start | bytes 15728640 | tf_op jit(solution)/shard_map/all_gather | solution.py:78
  81.0 0.7 copy-start.3
  204.6 5.5 %collective-permute-start = (f32[512]{0:T(512)S(1)}, f32[512]{0:T(512)S(1)}, u32[]{:S(2)}, u32[]{:S(2)}) collective-permute-start(f32[512]{0:T(512)S(1)} %get-tuple-element.309), channel_id=1, source_target_pairs={{0,8},{8,16},{16,24},{1,9},{9,17},{17,25},{2,10},{10,18},{18,26},{... | collective-permute-start | bytes 6152 | tf_op jit(solution)/shard_map/while/body/eval_jaxpr/ppermute | solution.py:12
  210.0 23.0 %copy-start.1 = (f32[512]{0:T(512)}, f32[512]{0:T(512)S(1)}, u32[]{:S(2)}) copy-start(f32[512]{0:T(512)S(1)} %broadcast_select_fusion.2) | copy-start | bytes 6148 | tf_op jit(solution)/shard_map/while
  233.1 5.5 %collective-permute-start = (f32[512]{0:T(512)S(1)}, f32[512]{0:T(512)S(1)}, u32[]{:S(2)}, u32[]{:S(2)}) collective-permute-start(f32[512]{0:T(512)S(1)} %get-tuple-element.309), channel_id=1, source_target_pairs={{0,8},{8,16},{16,24},{1,9},{9,17},{17,25},{2,10},{10,18},{18,26},{... | collective-permute-start | bytes 6152 | tf_op jit(solution)/shard_map/while/body/eval_jaxpr/ppermute | solution.py:12
  238.6 23.0 %copy-start.1 = (f32[512]{0:T(512)}, f32[512]{0:T(512)S(1)}, u32[]{:S(2)}) copy-start(f32[512]{0:T(512)S(1)} %broadcast_select_fusion.2) | copy-start | bytes 6148 | tf_op jit(solution)/shard_map/while
  261.6 5.5 %collective-permute-start = (f32[512]{0:T(512)S(1)}, f32[512]{0:T(512)S(1)}, u32[]{:S(2)}, u32[]{:S(2)}) collective-permute-start(f32[512]{0:T(512)S(1)} %get-tuple-element.309), channel_id=1, source_target_pairs={{0,8},{8,16},{16,24},{1,9},{9,17},{17,25},{2,10},{10,18},{18,26},{... | collective-permute-start | bytes 6152 | tf_op jit(solution)/shard_map/while/body/eval_jaxpr/ppermute | solution.py:12
  267.1 23.0 %copy-start.1 = (f32[512]{0:T(512)}, f32[512]{0:T(512)S(1)}, u32[]{:S(2)}) copy-start(f32[512]{0:T(512)S(1)} %broadcast_select_fusion.2) | copy-start | bytes 6148 | tf_op jit(solution)/shard_map/while
  290.2 5.5 %collective-permute-start = (f32[512]{0:T(512)S(1)}, f32[512]{0:T(512)S(1)}, u32[]{:S(2)}, u32[]{:S(2)}) collective-permute-start(f32[512]{0:T(512)S(1)} %get-tuple-element.309), channel_id=1, source_target_pairs={{0,8},{8,16},{16,24},{1,9},{9,17},{17,25},{2,10},{10,18},{18,26},{... | collective-permute-start | bytes 6152 | tf_op jit(solution)/shard_map/while/body/eval_jaxpr/ppermute | solution.py:12
  295.7 23.0 %copy-start.1 = (f32[512]{0:T(512)}, f32[512]{0:T(512)S(1)}, u32[]{:S(2)}) copy-start(f32[512]{0:T(512)S(1)} %broadcast_select_fusion.2) | copy-start | bytes 6148 | tf_op jit(solution)/shard_map/while
  320.6 0.6 copy-start.2
  323.1 0.6 copy-start.2
  325.6 0.6 copy-start.2
  328.1 0.6 copy-start.2
  330.5 0.6 copy-start.2
  333.0 0.6 copy-start.2
  335.5 0.6 copy-start.2
  338.0 0.6 copy-start.2
  340.5 0.6 copy-start.2
  342.9 0.6 copy-start.2
  345.4 0.6 copy-start.2
  347.9 0.6 copy-start.2
Sparse Core Ops, SparseCore 0:
  19.4 24.4 all-reduce.1
  81.1 123.4 all-gather.1
where the time goes:
time: 368 us; the launch traced here: 365 us
  waiting for transfers between devices  149 us (40%)
  matrix products  138 us (38%)
  local copies, waits for them, and re-layouts  39.1 us (11%)
  between operations  14.2 us (4%)
  blocking collectives  10.9 us (3%)
  other arithmetic  5.78 us (2%)
  starting transfers between devices  5.24 us (1%)
    dot_general x60, matrix products, advance(): jnp.dot(current, step_transit, precision=HIGHEST_PRECISION) + step_shift  112 us
    all_gather x1, waiting for transfers between devices, per_device(): lax.all_gather(transit_rows, 'state', axis=1, tiled=True)  109 us
    psum x1, waiting for transfers between devices, per_device(): info_rows, vector_rows = lax.psum((info_rows, vector_rows), 'outputs')  23.2 us
    rev x2, local copies, waits for them, and re-layouts, right_transition(): matrix.reshape(full_shape[:-1] + (full_shape[-1] // 2, 2))[..., ::-1]  17.4 us
    ppermute x4, waiting for transfers between devices, from_behind(): lax.ppermute(value, axis, [(source, source + steps) for source in range(i...  16.7 us
    dot_general x1, matrix products, per_device(): jnp.einsum('kor,kot->krt', lax.dynamic_slice_in_dim(scaled, row_start, ro...  8.71 us
    all_gather x1, blocking collectives, per_device(): lax.all_gather(vector_rows, 'state', axis=1, tiled=True)  8.36 us
    dot_general x1, matrix products, per_device(): jnp.einsum('ks,kos->ko', trajectory, loadings, precision=HIGHEST_PRECISION)  7.94 us
  transfers between devices with their start and end apart: 6, of which 6 were waited for; matrix products, arithmetic and copies ran while one was open for 1% of the time, Pallas kernels for 0%

commit v1 on v0

v1 whole, which is shorter than its diff:
```python
import functools

import jax
import jax.numpy as jnp
from jax import lax
from jax.experimental import pallas as pl
from jax.experimental.pallas import tpu as pltpu
from jax.sharding import PartitionSpec as P

F32, BF16 = jnp.float32, jnp.bfloat16
VMEM_LIMIT = 12 * 2**20
CHUNK = 3
WHOLE = pl.BlockSpec(memory_space=pltpu.VMEM)
SCALARS = pl.BlockSpec(memory_space=pltpu.SMEM)
FAR = pl.BlockSpec(memory_space=pltpu.HBM)


def call(kernel, name, outs, in_specs, scratch=(), flops=0, moved=0):
    return pl.pallas_call(
        kernel,
        out_shape=outs,
        in_specs=in_specs,
        out_specs=[WHOLE] * len(outs),
        scratch_shapes=scratch,
        compiler_params=pltpu.CompilerParams(vmem_limit_bytes=VMEM_LIMIT),
        cost_estimate=pl.CostEstimate(flops=flops, bytes_accessed=moved, transcendentals=0),
        name=name,
    )


def kept(*shape, dtype=F32):
    return pltpu.VMEM(shape, dtype)


def swap_pairs(x):
    width = x.shape[-1]
    lane = lax.broadcasted_iota(jnp.int32, x.shape, 1)
    return jnp.where(lane % 2 == 0, pltpu.roll(x, width - 1, 1), pltpu.roll(x, 1, 1))


def halves(x):
    high = x.astype(BF16)
    return high, (x - high.astype(F32)).astype(BF16)


def times_gain(scaled, gain_high, gain_low):
    high, low = halves(scaled)
    dot = functools.partial(jnp.dot, preferred_element_type=F32)
    return dot(high, gain_high) + (dot(high, gain_low) + dot(low, gain_high))


def gain_step(load, weight, reading, gain_high, gain_low):
    gained = times_gain(load * weight, gain_high, gain_low)
    return gained, jnp.sum(reading * gained, axis=0, keepdims=True)


def own_kernel(
    steps, rates, pairs, blend, columns, loads_far,
    loads, gained, shift, parts, gain_high, gain_low, sems,
):
    copies = [
        pltpu.make_async_copy(loads_far.at[k], loads.at[k], sems.at[k]) for k in range(steps)
    ]
    for copy in copies:
        copy.start()
    width = blend.shape[1]
    layout = pairs[...]
    rate = jnp.zeros(layout.shape, F32)
    for latent in range(rates.shape[0]):
        rate = jnp.where(layout == latent, rates[latent], rate)
    spread = lax.broadcasted_iota(jnp.int32, (layout.shape[1], width), 1) // 2
    spread = spread == lax.broadcasted_iota(jnp.int32, spread.shape, 0)
    rate = jnp.dot(
        jnp.broadcast_to(rate, (8, layout.shape[1])),
        spread.astype(F32),
        precision=lax.Precision.HIGHEST,
        preferred_element_type=F32,
    )
    even = lax.broadcasted_iota(jnp.int32, rate.shape, 1) % 2 == 0
    damping = jnp.exp(-rate)
    diagonal = jnp.where(even, damping * (1.0 + rate), damping * (1.0 - rate))
    cross = jnp.where(even, damping, -damping * rate * rate)
    parts[0] = diagonal
    parts[1] = cross
    gain = blend[...]
    gain = gain * diagonal[0:1] + swap_pairs(gain) * cross[0:1]
    high, low = halves(gain)
    gain_high[...] = high
    gain_low[...] = low
    for k in range(steps):
        copies[k].wait()
        gained[k], shift[k : k + 1, :] = gain_step(
            loads[k], columns[:, k : k + 1], columns[:, steps + k : steps + k + 1], high, low
        )


def advance(state, loads, gained, shift, diagonal, cross):
    width = state.shape[1]
    drift = shift
    for load, gain in zip(loads, gained):
        total = jnp.zeros_like(state)
        for row in range(0, load.shape[0], 8):
            product = load[row : row + 8, :] * state
            reading = jnp.sum(product, axis=1, keepdims=True)
            total = total + reading * gain[row : row + 8, :]
        drift = drift - jnp.sum(total, axis=0, keepdims=True)
    return state * diagonal + swap_pairs(state) * cross + drift


def part_kernel(
    first, count, steps, entering, loads_far, columns, loads_own, gained_own, shift_own, parts,
    gain_high, gain_low, loads, gained, shift, states, leaving, sems,
):
    copies = [
        pltpu.make_async_copy(loads_far.at[k], loads.at[k], sems.at[k]) for k in range(count)
    ]
    for copy in copies:
        copy.start()
    state = jnp.broadcast_to(entering[0:1, :], parts.shape[1:])
    high, low = gain_high[...], gain_low[...]
    for k in range(count):
        at = first + k
        copies[k].wait()
        gained[k], other = gain_step(
            loads[k], columns[:, at : at + 1], columns[:, steps + at : steps + at + 1], high, low
        )
        own = shift_own[at : at + 1, :]
        shift[k : k + 1, :] = own + other
        state = advance(
            state,
            (loads_own.at[at], loads.at[k]),
            (gained_own.at[at], gained.at[k]),
            own + other,
            parts[0],
            parts[1],
        )
        states[k : k + 1, :] = state[0:1, :]
    leaving[...] = state


def chain(entering, loads_own, gained_own, loads, gained, shifts, parts, states):
    state = jnp.broadcast_to(entering[0:1, :], parts.shape[1:])
    at = 0
    for load, gain, shift in zip(loads, gained, shifts):
        for k in range(load.shape[0]):
            state = advance(
                state,
                (loads_own.at[at], load.at[k]),
                (gained_own.at[at], gain.at[k]),
                shift[k : k + 1, :],
                parts[0],
                parts[1],
            )
            states[at : at + 1, :] = state[0:1, :]
            at += 1
    return state


def block_kernel(turn, count, position, before, entering, parts, loads_own, gained_own, *rest):
    loads, gained, shifts = rest[:count], rest[count : 2 * count], rest[2 * count : 3 * count]
    states, leaving = rest[3 * count :]

    @pl.when(position[0] == turn)
    def _():
        leaving[...] = chain(
            entering, loads_own, gained_own, loads, gained, shifts, parts, states
        )

    @pl.when(position[0] != turn)
    def _():
        states[...] = before[...]
        leaving[...] = jnp.zeros_like(leaving)


def last_kernel(turn, count, position, before, entering, parts, loads_own, gained_own, *rest):
    loads, gained, shifts = rest[:count], rest[count : 2 * count], rest[2 * count : 3 * count]
    own_states, predicted, states, columns = rest[3 * count :]

    @pl.when(position[0] == turn)
    def _():
        chain(entering, loads_own, gained_own, loads, gained, shifts, parts, states)

    @pl.when(position[0] != turn)
    def _():
        states[...] = before[...]

    share = own_states.shape[1]
    start = pl.multiple_of(position[1] * share, share)
    own_states[...] = states[:, pl.ds(start, share)]
    steps = states.shape[0]
    for k in range(steps):
        columns[:, k : k + 1] = jnp.sum(
            loads_own[k] * states[k : k + 1, :], axis=1, keepdims=True
        )
    predicted[...] = columns[...].T[:steps, :]


def per_device(
    observations, observed, loadings, noise_precision, blend_matrix, latent_rates, pair_latent,
    initial_mean,
):
    steps, outs, width = loadings.shape
    blocks = lax.axis_size("tm")
    share = width // lax.axis_size("state")
    other = functools.partial(lax.ppermute, axis_name="outputs", perm=[(0, 1), (1, 0)])
    weight = observed.astype(F32) * noise_precision[None, :]
    columns = jnp.concatenate([weight, observations], axis=0).T
    columns_far = other(columns)
    starts = range(0, steps, CHUNK)
    loads_far = [other(loadings[at : at + CHUNK]) for at in starts]
    initial = jnp.broadcast_to(initial_mean[None, :], (8, width))
    position = jnp.stack([lax.axis_index("tm"), lax.axis_index("state")]).astype(jnp.int32)

    half = 2 * 3 * outs * width * width
    loads_own, gained_own, shift_own, parts, gain_high, gain_low = call(
        functools.partial(own_kernel, steps),
        "own_half",
        [
            kept(steps, outs, width),
            kept(steps, outs, width),
            kept(steps, width),
            kept(2, 8, width),
            kept(width, width, dtype=BF16),
            kept(width, width, dtype=BF16),
        ],
        [SCALARS, WHOLE, WHOLE, WHOLE, FAR],
        [pltpu.SemaphoreType.DMA((steps,))],
        flops=steps * half,
        moved=4 * steps * outs * width,
    )(latent_rates, pair_latent[None, :], blend_matrix, columns, loadings)

    leaving = initial
    loads, gained, shifts, states = [], [], [], []
    for at, far in zip(starts, loads_far):
        count = far.shape[0]
        load, gain, shift, state, leaving = call(
            functools.partial(part_kernel, at, count, steps),
            "other_half",
            [
                kept(count, outs, width),
                kept(count, outs, width),
                kept(count, width),
                jax.ShapeDtypeStruct((count, width), F32),
                jax.ShapeDtypeStruct((8, width), F32),
            ],
            [WHOLE, FAR] + [WHOLE] * 7,
            [pltpu.SemaphoreType.DMA((count,))],
            flops=count * half,
            moved=4 * count * outs * width,
        )(
            leaving, far, columns_far, loads_own, gained_own, shift_own, parts, gain_high,
            gain_low,
        )
        loads.append(load)
        gained.append(gain)
        shifts.append(shift)
        states.append(state)
    states = jnp.concatenate(states, axis=0)
    parted = (*loads, *gained, *shifts)
    specs = [SCALARS] + [WHOLE] * (5 + len(parted))
    work = dict(flops=steps * half, moved=0)
    for turn in range(1, blocks):
        entering = lax.ppermute(leaving, "tm", [(turn - 1, turn)])
        operands = (position, states, entering, parts, loads_own, gained_own, *parted)
        if turn < blocks - 1:
            states, leaving = call(
                functools.partial(block_kernel, turn, len(loads)),
                "block_chain",
                [
                    jax.ShapeDtypeStruct((steps, width), F32),
                    jax.ShapeDtypeStruct((8, width), F32),
                ],
                specs,
                **work,
            )(*operands)
    if blocks == 1:
        operands = (position, states, initial, parts, loads_own, gained_own, *parted)
    return tuple(
        call(
            functools.partial(last_kernel, blocks - 1 if blocks > 1 else -1, len(loads)),
            "last_chain",
            [
                jax.ShapeDtypeStruct((steps, share), F32),
                jax.ShapeDtypeStruct((steps, outs), F32),
            ],
            specs,
            [pltpu.VMEM((steps, width), F32), pltpu.VMEM((outs, 128), F32)],
            **work,
        )(*operands)
    )


def solution(mesh):
    placed = (
        P("tm", "outputs"),
        P("tm", "outputs"),
        P("tm", "outputs", None),
        P("outputs"),
        P(),
        P(),
        P(),
        P(),
    )
    return jax.shard_map(
        per_device,
        mesh=mesh,
        in_specs=placed,
        out_specs=(P("tm", "state"), P("tm", "outputs")),
        check_vma=False,
    )
```

time: 368 us -> 55.1 us (0.15)
  matrix products: 138 us -> 0 us
  waiting for transfers between devices: 149 us -> 14.6 us
  local copies, waits for them, and re-layouts: 39.1 us -> 9.72 us
  Pallas kernels: 0 us -> 25.9 us
  between operations: 14.2 us -> 0.87 us
  blocking collectives: 10.9 us -> 0 us
  other arithmetic: 5.78 us -> 0.11 us
    dot_general x65 -> x0, matrix products: 138 us -> none  [the longest x60 112 us: advance(): jnp.dot(current, step_transit, precision=HIGHEST_PRECISION) + step_shift]
    all_gather x1 -> x0, waiting for transfers between devices: 109 us -> none  [per_device(): lax.all_gather(transit_rows, 'state', axis=1, tiled=True)]
    pallas_call x0 -> x8, Pallas kernels: none -> 25.9 us  [the longest x4 10.8 us: per_device(): call(functools.partial(part_kernel, at, count, steps), 'other_half', [kep...]
    psum x1 -> x0, waiting for transfers between devices: 23.2 us -> none  [per_device(): info_rows, vector_rows = lax.psum((info_rows, vector_rows), 'outputs')]
    rev x2 -> x0, local copies, waits for them, and re-layouts: 17.4 us -> none  [right_transition(): matrix.reshape(full_shape[:-1] + (full_shape[-1] // 2, 2))[..., ::-1]]
    all_gather x1 -> x0, blocking collectives: 8.36 us -> none  [per_device(): lax.all_gather(vector_rows, 'state', axis=1, tiled=True)]
    while x36 -> x0, local copies, waits for them, and re-layouts: 6.05 us -> none
    slice x0 -> x1, local copies, waits for them, and re-layouts: none -> 5.59 us  [per_device(): loads_far = [other(loadings[at:at + CHUNK]) for at in starts]]
  transfers between devices with their start and end apart: 6 -> 8, of which waited for: 6 -> 1; matrix products, arithmetic and copies ran while one was open for 1% -> 0% of each run, Pallas kernels for 0% -> 33%
where the time goes in v1:
time: 55.1 us; the launch traced here: 54.9 us
  Pallas kernels  25.9 us (47%)
  waiting for transfers between devices  14.6 us (26%)
  local copies, waits for them, and re-layouts  9.72 us (18%)
  starting transfers between devices  3.71 us (7%)
  between operations  0.87 us (2%)
    ppermute x3, waiting for transfers between devices, per_device(): entering = lax.ppermute(leaving, 'tm', [(turn - 1, turn)])  14.6 us
    pallas_call x4, Pallas kernels, per_device(): call(functools.partial(part_kernel, at, count, steps), 'other_half', [kep...  10.8 us
    pallas_call x1, Pallas kernels, per_device(): call(functools.partial(own_kernel, steps), 'own_half', [kept(steps, outs,...  9.81 us
    slice x1, local copies, waits for them, and re-layouts, per_device(): loads_far = [other(loadings[at:at + CHUNK]) for at in starts]  5.59 us
    pallas_call x1, Pallas kernels, per_device(): call(functools.partial(last_kernel, blocks - 1 if blocks > 1 else -1, len...  4.08 us
    unnamed x16, local copies, waits for them, and re-layouts  4.03 us
    ppermute x3, starting transfers between devices, per_device(): entering = lax.ppermute(leaving, 'tm', [(turn - 1, turn)])  2.62 us
    pallas_call x2, Pallas kernels, per_device(): call(functools.partial(block_kernel, turn, len(loads)), 'block_chain', [j...  1.14 us
  transfers between devices with their start and end apart: 8, of which 1 were waited for; matrix products, arithmetic and copies ran while one was open for 0% of the time, Pallas kernels for 33%

profile of v1, /device:TPU:24, one launch (start us, length us, event | category | flops | bytes accessed | tf_op | source)
XLA Modules:
  0.0 54.9 jit_solution(4876274288211012414)
XLA Ops:
  0.6 0.0 copy-start.7
  0.6 0.0 copy-start.5
  0.7 0.0 copy-start.4
  0.7 0.0 copy-start.2
  0.7 0.0 copy-start.3
  0.7 5.6 %fusion = (f32[3,256,512]{2,1,0:T(8,128)}, f32[3,256,512]{2,1,0:T(8,128)}, f32[3,256,512]{2,1,0:T(8,128)}, f32[3,256,512]{2,1,0:T(8,128)}) fusion(f32[12,256,512]{2,1,0:T(8,128)} %loads_far.1), kind=kLoop, calls=%fused_computation.4 | loop fusion | bytes 12582912 | tf_op jit(solution)/shard_map/slice | solution.py:210
  6.3 0.0 collective-permute-start
  6.3 0.5 collective-permute-start.2
  6.8 0.0 collective-permute-start.3
  6.8 0.5 collective-permute-start.4
  7.3 0.0 copy-done.7
  7.3 0.0 copy-done.5
  7.3 0.0 copy-done.4
  7.3 0.1 copy.13
  7.4 0.1 collective-permute-start.1
  7.5 0.0 copy-done.2
  7.5 0.0 copy-done.3
  7.5 0.0 copy-start
  7.5 2.8 %copy-done = f32[12,256,512]{2,1,0:T(8,128)S(1)} copy-done((f32[12,256,512]{2,1,0:T(8,128)S(1)}, f32[12,256,512]{2,1,0:T(8,128)}, u32[]{:S(2)}) %copy-start) | copy-done | bytes 6291480
  10.3 0.0 copy-start.1
  10.3 1.2 %copy-done.1 = f32[512,512]{1,0:T(8,128)S(1)} copy-done((f32[512,512]{1,0:T(8,128)S(1)}, f32[512,512]{1,0:T(8,128)}, u32[]{:S(2)}) %copy-start.1) | copy-done | bytes 1048600
  11.5 0.0 copy-start.6
  11.5 9.8 %own_half.1 = (f32[12,256,512]{2,1,0:T(8,128)S(1)}, f32[12,256,512]{2,1,0:T(8,128)S(1)}, f32[12,512]{1,0:T(8,128)S(1)}, f32[2,8,512]{2,1,0:T(8,128)S(1)}, bf16[5...) custom-call(f32[4]{0:T(128)S(1)} %copy-done.3, s32[1,256]{1,0:T(1,128)S(1)} %bitcast.6, f32[512,512]{1,0:T(8,128)S(1)} %copy-done.1, ...), custom_call_target="tpu_custom_call" | custom-call | flops 4831838208 | bytes 6291456 | tf_op jit(solution)/shard_map/own_half/pallas_call | solution.py:215
  21.4 0.1 pad_add_fusion.position
  21.4 0.0 collective-permute-done.1.columns
  21.4 0.0 collective-permute-done.loads_far
  21.4 0.0 copy-done.6
  21.5 3.1 %other_half.4 = (f32[3,256,512]{2,1,0:T(8,128)S(1)}, f32[3,256,512]{2,1,0:T(8,128)S(1)}, f32[3,512]{1,0:T(4,128)S(1)}, f32[3,512]{1,0:T(4,128)S(1)}, f32[8,512]{1,0:T(8,128)S(1)}) custom-call(f32[8,512]{1,0:T(8,128)S(1)} %broadcast_in_dim.4.entering, f32[3,256,512]{2,1,0:T(8,128)} %collective-permute-done.loads_far, ...), custom_call_target="tpu_custom_call" | custom-call | flops 1207959552 | bytes 1572864 | tf_op jit(solution)/shard_map/other_half/pallas_call | solution.py:236
  24.6 0.0 collective-permute-done.2.loads_far
  24.6 3.1 %other_half.5 = (f32[3,256,512]{2,1,0:T(8,128)S(1)}, f32[3,256,512]{2,1,0:T(8,128)S(1)}, f32[3,512]{1,0:T(4,128)S(1)}, f32[3,512]{1,0:T(4,128)S(1)}, f32[8,512]{1,0:T(8,128)S(1)}) custom-call(f32[8,512]{1,0:T(8,128)S(1)} %get-tuple-element.39.entering, f32[3,256,512]{2,1,0:T(8,128)} %collective-permute-done.2.loads_far, ...), custom_call_target="tpu_custom_call" | custom-call | flops 1207959552 | bytes 1572864 | tf_op jit(solution)/shard_map/other_half/pallas_call | solution.py:236
  27.7 0.0 collective-permute-done.3.loads_far
  27.7 2.2 %other_half.6 = (f32[3,256,512]{2,1,0:T(8,128)S(1)}, f32[3,256,512]{2,1,0:T(8,128)S(1)}, f32[3,512]{1,0:T(4,128)S(1)}, f32[3,512]{1,0:T(4,128)S(1)}, f32[8,512]{1,0:T(8,128)S(1)}) custom-call(f32[8,512]{1,0:T(8,128)S(1)} %get-tuple-element.41.entering, f32[3,256,512]{2,1,0:T(8,128)S(1)} %collective-permute-done.3.loads_far, ...), custom_call_target="tpu_custom_call" | custom-call | flops 1207959552 | bytes 1572864 | tf_op jit(solution)/shard_map/other_half/pallas_call | solution.py:236
  29.9 0.0 collective-permute-done.4.loads_far
  29.9 2.4 %other_half.7 = (f32[3,256,512]{2,1,0:T(8,128)S(1)}, f32[3,256,512]{2,1,0:T(8,128)S(1)}, f32[3,512]{1,0:T(4,128)S(1)}, f32[3,512]{1,0:T(4,128)S(1)}, f32[8,512]{1,0:T(8,128)S(1)}) custom-call(f32[8,512]{1,0:T(8,128)S(1)} %get-tuple-element.43.entering, f32[3,256,512]{2,1,0:T(8,128)S(1)} %collective-permute-done.4.loads_far, ...), custom_call_target="tpu_custom_call" | custom-call | flops 1207959552 | bytes 1572864 | tf_op jit(solution)/shard_map/other_half/pallas_call | solution.py:236
  32.4 0.7 %collective-permute-start.5 = (f32[8,512]{1,0:T(8,128)S(1)}, f32[8,512]{1,0:T(8,128)S(1)}, u32[]{:S(2)}, u32[]{:S(2)}) collective-permute-start(f32[8,512]{1,0:T(8,128)S(1)} %get-tuple-element.45), channel_id=1, source_target_pairs={{0,8},{1,9},{2,10},{3,11},{4,12},{5,13},{6,14},{7,15}} | collective-permute-start | bytes 49160 | tf_op jit(solution)/shard_map/ppermute | solution.py:263
  33.0 0.0 collective-permute-done.5.entering
  33.1 0.6 %block_chain.2 = (f32[12,512]{1,0:T(8,128)S(1)}, f32[8,512]{1,0:T(8,128)S(1)}) custom-call(s32[2]{0:T(128)S(1)} %pad_add_fusion.position, f32[12,512]{1,0:T(8,128)S(1)} %pad_maximum_fusion.before, f32[8,512]{1,0:T(8,128)S(1)} %collective-permute-done.5.entering, f32[2,8,512]{2,1,0:T(8,128)S(1)} %get-tuple-element.35.parts, ...), custom_call_target="tpu_custom_call" | custom-call | flops 4831838208 | tf_op jit(solution)/shard_map/block_chain/pallas_call | solution.py:266
  33.6 0.7 %collective-permute-start.6 = (f32[8,512]{1,0:T(8,128)S(1)}, f32[8,512]{1,0:T(8,128)S(1)}, u32[]{:S(2)}, u32[]{:S(2)}) collective-permute-start(f32[8,512]{1,0:T(8,128)S(1)} %get-tuple-element.59), channel_id=1, source_target_pairs={{8,16},{9,17},{10,18},{11,19},{12,20},{13,21},{14,22},{15,23}} | collective-permute-start | bytes 49160 | tf_op jit(solution)/shard_map/ppermute | solution.py:263
  34.3 0.0 collective-permute-done.6.entering
  34.3 0.6 %block_chain.3 = (f32[12,512]{1,0:T(8,128)S(1)}, f32[8,512]{1,0:T(8,128)S(1)}) custom-call(s32[2]{0:T(128)S(1)} %pad_add_fusion.position, f32[12,512]{1,0:T(8,128)S(1)} %get-tuple-element.58.before, f32[8,512]{1,0:T(8,128)S(1)} %collective-permute-done.6.entering, f32[2,8,512]{2,1,0:T(8,128)S(1)} %get-tuple-element.35.parts, ...), custom_call_target="tpu_custom_call" | custom-call | flops 4831838208 | tf_op jit(solution)/shard_map/block_chain/pallas_call | solution.py:266
  34.9 1.3 %collective-permute-start.7 = (f32[8,512]{1,0:T(8,128)S(1)}, f32[8,512]{1,0:T(8,128)S(1)}, u32[]{:S(2)}, u32[]{:S(2)}) collective-permute-start(f32[8,512]{1,0:T(8,128)S(1)} %get-tuple-element.61), channel_id=1, source_target_pairs={{16,24},{17,25},{18,26},{19,27},{20,28},{21,29},{22,30},{23,31}} | collective-permute-start | bytes 49160 | tf_op jit(solution)/shard_map/ppermute | solution.py:263
  36.2 14.6 %collective-permute-done.7.entering = f32[8,512]{1,0:T(8,128)S(1)} collective-permute-done((f32[8,512]{1,0:T(8,128)S(1)}, f32[8,512]{1,0:T(8,128)S(1)}, u32[]{:S(2)}, u32[]{:S(2)}) %collective-permute-start.7) | collective-permute-done | bytes 16416 | tf_op jit(solution)/shard_map/ppermute | solution.py:263
  50.8 4.1 %last_chain.1 = (f32[12,128]{1,0:T(8,128)}, f32[12,256]{1,0:T(8,128)}) custom-call(s32[2]{0:T(128)S(1)} %pad_add_fusion.position, f32[12,512]{1,0:T(8,128)S(1)} %get-tuple-element.60.before, f32[8,512]{1,0:T(8,128)S(1)} %collective-permute-done.7.entering, f32[2,8,512]{2,1,0:T(8,128)S(1)} %get-tuple-element.35.parts, ...), custom_call_target="tpu_custom_call" | custom-call | flops 4831838208 | tf_op jit(solution)/shard_map/last_chain/pallas_call | solution.py:279
  (4 shorter events, 0.0 us)
Async XLA Ops:
  0.6 6.7 %copy-start.7 = (f32[256]{0:T(256)S(1)}, f32[256]{0:T(256)}, u32[]{:S(2)}) copy-start(f32[256]{0:T(256)} %param.11) | copy-start | bytes 3076
  0.6 6.7 %copy-start.5 = (s32[12,256]{1,0:T(8,128)S(1)}, s32[12,256]{1,0:T(8,128)}, u32[]{:S(2)}) copy-start(s32[12,256]{1,0:T(8,128)} %param.9) | copy-start | bytes 36868
  0.7 6.7 %copy-start.4 = (f32[12,256]{1,0:T(8,128)S(1)}, f32[12,256]{1,0:T(8,128)}, u32[]{:S(2)}) copy-start(f32[12,256]{1,0:T(8,128)} %param.8) | copy-start | bytes 36868
  0.7 6.9 %copy-start.2 = (s32[256]{0:T(256)S(1)}, s32[256]{0:T(256)}, u32[]{:S(2)}) copy-start(s32[256]{0:T(256)} %param.14) | copy-start | bytes 3076
  0.7 6.9 %copy-start.3 = (f32[4]{0:T(128)S(1)}, f32[4]{0:T(128)}, u32[]{:S(2)}) copy-start(f32[4]{0:T(128)} %rates.1) | copy-start | bytes 52
  6.3 15.2 %collective-permute-start = (f32[3,256,512]{2,1,0:T(8,128)}, f32[3,256,512]{2,1,0:T(8,128)}, u32[]{:S(2)}, u32[]{:S(2)}) collective-permute-start(f32[3,256,512]{2,1,0:T(8,128)} %get-tuple-element.64), channel_id=1, source_target_pairs={{0,1},{1,0},{2,3},{3,2},{4,5},{5,4},{6,7},{7,6},{8,9},{9,8},{10,11... | collective-permute-start | bytes 4718600 | tf_op jit(solution)/shard_map/ppermute | solution.py:210
  6.3 18.3 %collective-permute-start.2 = (f32[3,256,512]{2,1,0:T(8,128)}, f32[3,256,512]{2,1,0:T(8,128)}, u32[]{:S(2)}, u32[]{:S(2)}) collective-permute-start(f32[3,256,512]{2,1,0:T(8,128)} %get-tuple-element.63), channel_id=1, source_target_pairs={{0,1},{1,0},{2,3},{3,2},{4,5},{5,4},{6,7},{7,6},{8,9},{9,8},{10,11... | collective-permute-start | bytes 4718600 | tf_op jit(solution)/shard_map/ppermute | solution.py:210
  6.8 20.9 %collective-permute-start.3 = (f32[3,256,512]{2,1,0:T(8,128)}, f32[3,256,512]{2,1,0:T(8,128)S(1)}, u32[]{:S(2)}, u32[]{:S(2)}) collective-permute-start(f32[3,256,512]{2,1,0:T(8,128)} %get-tuple-element.65), channel_id=1, source_target_pairs={{0,1},{1,0},{2,3},{3,2},{4,5},{5,4},{6,7},{7,6},{8,9},{9,8},{10,11... | collective-permute-start | bytes 4718600 | tf_op jit(solution)/shard_map/ppermute | solution.py:210
  6.8 23.2 %collective-permute-start.4 = (f32[3,256,512]{2,1,0:T(8,128)}, f32[3,256,512]{2,1,0:T(8,128)S(1)}, u32[]{:S(2)}, u32[]{:S(2)}) collective-permute-start(f32[3,256,512]{2,1,0:T(8,128)} %get-tuple-element.62), channel_id=1, source_target_pairs={{0,1},{1,0},{2,3},{3,2},{4,5},{5,4},{6,7},{7,6},{8,9},{9,8},{10,11... | collective-permute-start | bytes 4718600 | tf_op jit(solution)/shard_map/ppermute | solution.py:210
  7.4 14.0 %collective-permute-start.1 = (f32[256,24]{1,0:T(8,128)S(1)}, f32[256,24]{1,0:T(8,128)S(1)}, u32[]{:S(2)}, u32[]{:S(2)}) collective-permute-start(f32[256,24]{1,0:T(8,128)S(1)} %bitcast.4), channel_id=1, source_target_pairs={{0,1},{1,0},{2,3},{3,2},{4,5},{5,4},{6,7},{7,6},{8,9},{9,8},{10,11... | collective-permute-start | bytes 73736 | tf_op jit(solution)/shard_map/ppermute | solution.py:208
  7.5 2.8 %copy-start = (f32[12,256,512]{2,1,0:T(8,128)S(1)}, f32[12,256,512]{2,1,0:T(8,128)}, u32[]{:S(2)}) copy-start(f32[12,256,512]{2,1,0:T(8,128)} %loads_far.1) | copy-start | bytes 18874372
  10.3 1.2 %copy-start.1 = (f32[512,512]{1,0:T(8,128)S(1)}, f32[512,512]{1,0:T(8,128)}, u32[]{:S(2)}) copy-start(f32[512,512]{1,0:T(8,128)} %blend.1) | copy-start | bytes 3145732
  11.5 9.9 %copy-start.6 = (f32[512]{0:T(512)S(1)}, f32[512]{0:T(512)}, u32[]{:S(2)}) copy-start(f32[512]{0:T(512)} %param.15) | copy-start | bytes 6148
  32.4 0.7 %collective-permute-start.5 = (f32[8,512]{1,0:T(8,128)S(1)}, f32[8,512]{1,0:T(8,128)S(1)}, u32[]{:S(2)}, u32[]{:S(2)}) collective-permute-start(f32[8,512]{1,0:T(8,128)S(1)} %get-tuple-element.45), channel_id=1, source_target_pairs={{0,8},{1,9},{2,10},{3,11},{4,12},{5,13},{6,14},{7,15}} | collective-permute-start | bytes 49160 | tf_op jit(solution)/shard_map/ppermute | solution.py:263
  33.6 0.7 %collective-permute-start.6 = (f32[8,512]{1,0:T(8,128)S(1)}, f32[8,512]{1,0:T(8,128)S(1)}, u32[]{:S(2)}, u32[]{:S(2)}) collective-permute-start(f32[8,512]{1,0:T(8,128)S(1)} %get-tuple-element.59), channel_id=1, source_target_pairs={{8,16},{9,17},{10,18},{11,19},{12,20},{13,21},{14,22},{15,23}} | collective-permute-start | bytes 49160 | tf_op jit(solution)/shard_map/ppermute | solution.py:263
  34.9 15.9 %collective-permute-start.7 = (f32[8,512]{1,0:T(8,128)S(1)}, f32[8,512]{1,0:T(8,128)S(1)}, u32[]{:S(2)}, u32[]{:S(2)}) collective-permute-start(f32[8,512]{1,0:T(8,128)S(1)} %get-tuple-element.61), channel_id=1, source_target_pairs={{16,24},{17,25},{18,26},{19,27},{20,28},{21,29},{22,30},{23,31}} | collective-permute-start | bytes 49160 | tf_op jit(solution)/shard_map/ppermute | solution.py:263

commit v2 on v1

v2 whole, which is shorter than its diff:
```python
import functools

import jax
import jax.numpy as jnp
from jax import lax
from jax.experimental import pallas as pl
from jax.experimental.pallas import tpu as pltpu
from jax.sharding import PartitionSpec as P

F32, BF16 = jnp.float32, jnp.bfloat16
VMEM_LIMIT = 8 * 2**20
LAST_PART = 1
PARTS = 4
SECOND_GAINS = 5
WHOLE = pl.BlockSpec(memory_space=pltpu.VMEM)
FAR = pl.BlockSpec(memory_space=pl.ANY)


def call(kernel, name, outs, in_specs, scratch=(), flops=0, moved=0):
    return pl.pallas_call(
        kernel,
        out_shape=outs,
        in_specs=in_specs,
        out_specs=[WHOLE] * len(outs),
        scratch_shapes=scratch,
        compiler_params=pltpu.CompilerParams(vmem_limit_bytes=VMEM_LIMIT),
        cost_estimate=pl.CostEstimate(flops=flops, bytes_accessed=moved, transcendentals=0),
        name=name,
    )


def kept(*shape, dtype=F32):
    return pltpu.VMEM(shape, dtype)


def swap_pairs(x):
    width = x.shape[-1]
    lane = lax.broadcasted_iota(jnp.int32, x.shape, 1)
    return jnp.where(lane % 2 == 0, pltpu.roll(x, width - 1, 1), pltpu.roll(x, 1, 1))


def halves(x):
    high = x.astype(BF16)
    return high, (x - high.astype(F32)).astype(BF16)


def times_gain(scaled, gain_high, gain_low):
    high, low = halves(scaled)
    dot = functools.partial(jnp.dot, preferred_element_type=F32)
    return dot(high, gain_high) + (dot(high, gain_low) + dot(low, gain_high))


def part_sizes(steps):
    rest = steps - LAST_PART
    sizes = [rest // (PARTS - 1) + (i < rest % (PARTS - 1)) for i in range(PARTS - 1)]
    return sizes + [LAST_PART]


def copied(source, target, sem):
    copy = pltpu.make_async_copy(source, target, sem)
    copy.start()
    return copy


def fetched(loads_far, first, loads, sems):
    return [
        copied(loads_far.at[first + k], loads.at[k], sems.at[k]) for k in range(loads.shape[0])
    ]


def scale(copies, first, steps, loads, columns, scaled, sent):
    outs = loads.shape[1]
    for k, copy in enumerate(copies):
        at = first + k
        copy.wait()
        rows = loads[k] * columns[:, at : at + 1]
        tail = jnp.sum(columns[:, steps + at : steps + at + 1] * rows, axis=0, keepdims=True)
        tail = jnp.broadcast_to(tail, (8, tail.shape[1]))
        for target in (sent, scaled):
            target[k, :outs, :] = rows
            target[k, outs:, :] = tail


def stage_kernel(
    loads_far, observed_far, observations_far, noise_far, loads, scaled, sent, columns,
    observed, observations, noise, turned, sems, small_sems,
):
    small = [
        copied(source, target, small_sems.at[i])
        for i, (source, target) in enumerate(
            (
                (observed_far, observed),
                (observations_far, observations),
                (noise_far, noise),
            )
        )
    ]
    copies = fetched(loads_far, 0, loads, sems)
    turned[...] = jnp.zeros_like(turned)
    for copy in small:
        copy.wait()
    steps = observed.shape[0]
    root = jnp.sqrt(observed[...].astype(F32) * noise[...])
    turned[:steps, :] = root
    turned[steps : 2 * steps, :] = root * observations[...]
    columns[...] = turned[...].T
    scale(copies, 0, steps, loads, columns, scaled, sent)


def transition(rates, pairs, width):
    layout = pairs[...]
    rate = jnp.zeros(layout.shape, F32)
    for latent in range(rates.shape[1]):
        rate = jnp.where(layout == latent, rates[:, latent : latent + 1], rate)
    spread = lax.broadcasted_iota(jnp.int32, (layout.shape[1], width), 1) // 2
    spread = spread == lax.broadcasted_iota(jnp.int32, spread.shape, 0)
    rate = jnp.dot(
        jnp.broadcast_to(rate, (8, layout.shape[1])),
        spread.astype(F32),
        precision=lax.Precision.HIGHEST,
        preferred_element_type=F32,
    )
    even = lax.broadcasted_iota(jnp.int32, rate.shape, 1) % 2 == 0
    damping = jnp.exp(-rate)
    diagonal = jnp.where(even, damping * (1.0 + rate), damping * (1.0 - rate))
    cross = jnp.where(even, damping, -damping * rate * rate)
    return diagonal, cross


def gain_limit(block, steps):
    return (0, min(SECOND_GAINS, steps), steps)[min(block, 2)]


def by_block(work, steps):
    block = lax.axis_index("tm")
    for i in (1, 2):

        @pl.when(block == 1 if i == 1 else block > 1)
        def _():
            work(gain_limit(i, steps))


def fill_gains(limit, first, scaled, gain_high, gain_low, gained):
    rows = scaled.shape[1]
    for k in range(min(scaled.shape[0], limit - first)):
        block = jnp.concatenate([scaled[k], scaled[k, rows - 8 :, :]], axis=0)
        gained[k] = times_gain(block, gain_high[...], gain_low[...])[:rows]


def second_kernel(
    first, steps, loads_far, columns, rates, pairs, blend,
    loads, scaled, sent, parts, gain_high, gain_low, sems,
):
    copies = fetched(loads_far, first, loads, sems)
    diagonal, cross = transition(rates, pairs, blend.shape[1])
    parts[0] = diagonal
    parts[1] = cross

    @pl.when(lax.axis_index("tm") != 0)
    def _():
        gain = blend[...]
        gain = gain * diagonal[0:1] + swap_pairs(gain) * cross[0:1]
        gain_high[...], gain_low[...] = halves(gain)

    scale(copies, first, steps, loads, columns, scaled, sent)


def third_kernel(
    firsts, steps, loads_far, columns, scaled_first, gain_high, gain_low,
    gained_first, *rest,
):
    count = len(firsts)
    groups = [rest[3 * i : 3 * i + 3] for i in range(count)]
    sems = rest[3 * count :]
    copies = [
        fetched(loads_far, first, group[0], sem)
        for first, group, sem in zip(firsts, groups, sems)
    ]

    def work(limit):
        fill_gains(limit, 0, scaled_first, gain_high, gain_low, gained_first)

    by_block(work, steps)
    for first, group, copy in zip(firsts, groups, copies):
        loads, scaled, sent = group
        scale(copy, first, steps, loads, columns, scaled, sent)


def gain_kernel(firsts, steps, gain_high, gain_low, *rest):
    count = len(firsts)

    def work(limit):
        for first, scaled, gained in zip(firsts, rest[:count], rest[count:]):
            fill_gains(limit, first, scaled, gain_high, gain_low, gained)

    by_block(work, steps)


def reflected(state, pull, blend):
    pull = jnp.broadcast_to(pull, state.shape)
    place = lax.broadcasted_iota(jnp.int32, (8, 128), 1) - lax.broadcasted_iota(
        jnp.int32, (8, 128), 0
    )
    turned = []
    for start in range(0, state.shape[1], 128):
        total = jnp.zeros((8, 128), F32)
        for row in range(0, 128, 8):
            blended = blend[start + row : start + row + 8, :] * pull
            total = total + jnp.where(
                place == row, jnp.sum(blended, axis=1, keepdims=True), 0.0
            )
        turned.append(jnp.sum(total, axis=0, keepdims=True))
    return state - jnp.concatenate(turned, axis=1)


def advance(state, scaled, gained, parts, blend=None):
    pull = 0.0
    for rows, gains in zip(scaled, gained):
        outs = rows.shape[0] - 8
        total = jnp.zeros_like(state)
        for row in range(0, outs, 8):
            block = rows[row : row + 8, :]
            reading = jnp.sum(block * state, axis=1, keepdims=True)
            total = total + reading * (block if blend is not None else gains[row : row + 8, :])
        pull += jnp.sum(total, axis=0, keepdims=True) - gains[outs : outs + 1, :]
    if blend is not None:
        state, pull = reflected(state, pull, blend), 0.0
    return state * parts[0] + swap_pairs(state) * parts[1] - pull


def part_kernel(
    first, steps, entering, scaled_far, scaled_own, parts, blend, gain_high, gain_low,
    scaled, gained, states, leaving, sem,
):
    copied(scaled_far, scaled, sem).wait()
    block = lax.axis_index("tm")

    @pl.when(block == 0)
    def _():
        state = jnp.broadcast_to(entering[0:1, :], parts.shape[1:])
        for k in range(scaled.shape[0]):
            pair = (scaled_own.at[k], scaled.at[k])
            state = advance(state, pair, pair, parts, blend)
            states[k : k + 1, :] = state[0:1, :]
        leaving[...] = state

    def work(limit):
        fill_gains(limit, first, scaled, gain_high, gain_low, gained)

    by_block(work, steps)


def chain(limit, entering, parts, blend, operands, states):
    state = jnp.broadcast_to(entering[0:1, :], parts.shape[1:])
    at = 0
    for _, own, gained_own, scaled, gained in operands:
        for k in range(own.shape[0]):
            pair = (own.at[k], scaled.at[k])
            if at < limit:
                state = advance(state, pair, (gained_own.at[k], gained.at[k]), parts)
            else:
                state = advance(state, pair, pair, parts, blend)
            states[at : at + 1, :] = state[0:1, :]
            at += 1
    return state


def grouped(refs, count):
    return [refs[5 * i : 5 * i + 5] for i in range(count)], refs[5 * count :]


def block_kernel(turn, count, before, entering, parts, blend, *refs):
    operands, (states, leaving) = grouped(refs, count)
    block = lax.axis_index("tm")

    @pl.when(block == turn)
    def _():
        limit = gain_limit(turn, states.shape[0])
        leaving[...] = chain(limit, entering, parts, blend, operands, states)

    @pl.when(block != turn)
    def _():
        states[...] = before[...]
        leaving[...] = jnp.zeros_like(leaving)


def last_kernel(turn, count, before, entering, parts, blend, *refs):
    operands, (own_states, predicted, states, readings) = grouped(refs, count)
    block = lax.axis_index("tm")

    @pl.when(block == turn)
    def _():
        limit = gain_limit(turn, states.shape[0])
        chain(limit, entering, parts, blend, operands, states)

    @pl.when(block != turn)
    def _():
        states[...] = before[...]

    share = own_states.shape[1]
    start = pl.multiple_of(lax.axis_index("state") * share, share)
    own_states[...] = states[:, pl.ds(start, share)]
    at = 0
    for loads, *_ in operands:
        for k in range(loads.shape[0]):
            readings[:, at : at + 1] = jnp.sum(
                loads[k] * states[at : at + 1, :], axis=1, keepdims=True
            )
            at += 1
    predicted[...] = readings[...].T[:at, :]


def per_device(
    observations, observed, loadings, noise_precision, blend_matrix, latent_rates, pair_latent,
    initial_mean,
):
    steps, outs, width = loadings.shape
    blocks = lax.axis_size("tm")
    share = width // lax.axis_size("state")
    other = functools.partial(lax.ppermute, axis_name="outputs", perm=[(0, 1), (1, 0)])
    in_hbm = functools.partial(
        pltpu.with_memory_space_constraint, memory_space=pltpu.HBM
    )
    loadings = in_hbm(loadings)
    sizes = part_sizes(steps)
    count = len(sizes)
    firsts = [sum(sizes[:i]) for i in range(count)]
    initial = jnp.broadcast_to(initial_mean[None, :], (8, width))

    half = 2 * 3 * outs * width * width
    vector, gain_type = kept(8, width), kept(width, width, dtype=BF16)
    sems = pltpu.SemaphoreType.DMA

    def matrices(size):
        return kept(size, outs + 8, width)

    def chunk(size):
        return [kept(size, outs, width), matrices(size), matrices(size)]

    small = (steps, outs)
    *first_chunk, columns = call(
        stage_kernel,
        "stage",
        chunk(sizes[0]) + [kept(outs, 128)],
        [FAR] * 4,
        [
            pltpu.VMEM(small, observed.dtype),
            pltpu.VMEM(small, F32),
            pltpu.VMEM((1, outs), F32),
            pltpu.VMEM((128, outs), F32),
            sems((sizes[0],)),
            sems((3,)),
        ],
        moved=8 * sizes[0] * outs * width,
    )(loadings, in_hbm(observed), in_hbm(observations), in_hbm(noise_precision[None, :]))
    *second_chunk, parts, gain_high, gain_low = call(
        functools.partial(second_kernel, firsts[1], steps),
        "second_part",
        chunk(sizes[1]) + [kept(2, 8, width), gain_type, gain_type],
        [FAR] + [WHOLE] * 4,
        [sems((sizes[1],))],
        moved=8 * sizes[1] * outs * width,
    )(loadings, columns, latent_rates[None, :], pair_latent[None, :], blend_matrix)
    gained_first, *later = call(
        functools.partial(third_kernel, firsts[2:], steps),
        "later_parts",
        [matrices(sizes[0])] + sum([chunk(size) for size in sizes[2:]], []),
        [FAR] + [WHOLE] * 4,
        [sems((size,)) for size in sizes[2:]],
        flops=sizes[0] * half,
        moved=8 * sum(sizes[2:]) * outs * width,
    )(loadings, columns, first_chunk[1], gain_high, gain_low)
    chunks = [first_chunk, second_chunk] + [later[i : i + 3] for i in range(0, len(later), 3)]
    loads_own, scaled_own, sent = zip(*chunks)
    gained_own = [gained_first] + list(
        call(
            functools.partial(gain_kernel, firsts[1:], steps),
            "own_gains",
            [matrices(size) for size in sizes[1:]],
            [WHOLE] * (1 + count),
            flops=sum(sizes[1:]) * half,
        )(gain_high, gain_low, *scaled_own[1:])
    )

    leaving = initial
    operands, states = [], []
    for i in range(count):
        scaled, gained, state, leaving = call(
            functools.partial(part_kernel, firsts[i], steps),
            "other_part",
            [matrices(sizes[i]), matrices(sizes[i]), kept(sizes[i], width), vector],
            [WHOLE, FAR] + [WHOLE] * 5,
            [sems],
            flops=sizes[i] * half,
            moved=8 * sizes[i] * outs * width,
        )(
            leaving, other(sent[i]), scaled_own[i], parts, blend_matrix, gain_high, gain_low
        )
        operands += [loads_own[i], scaled_own[i], gained_own[i], scaled, gained]
        states.append(state)
    states = jnp.concatenate(states, axis=0)

    specs = [WHOLE] * (4 + len(operands))
    entering = leaving
    for turn in range(1, blocks):
        entering = lax.ppermute(leaving, "tm", [(turn - 1, turn)])
        if turn < blocks - 1:
            states, leaving = call(
                functools.partial(block_kernel, turn, count),
                "block_chain",
                [kept(steps, width), vector],
                specs,
                flops=steps * half,
            )(states, entering, parts, blend_matrix, *operands)
    return tuple(
        call(
            functools.partial(last_kernel, blocks - 1 if blocks > 1 else -1, count),
            "last_chain",
            [
                jax.ShapeDtypeStruct((steps, share), F32),
                jax.ShapeDtypeStruct((steps, outs), F32),
            ],
            specs,
            [pltpu.VMEM((steps, width), F32), pltpu.VMEM((outs, 128), F32)],
            flops=steps * half,
        )(states, entering, parts, blend_matrix, *operands)
    )


def solution(mesh):
    placed = (
        P("tm", "outputs"),
        P("tm", "outputs"),
        P("tm", "outputs", None),
        P("outputs"),
        P(),
        P(),
        P(),
        P(),
    )
    return jax.shard_map(
        per_device,
        mesh=mesh,
        in_specs=placed,
        out_specs=(P("tm", "state"), P("tm", "outputs")),
        check_vma=False,
    )
```

time: 55.1 us -> 35.3 us (0.64)
  local copies, waits for them, and re-layouts: 9.72 us -> 0.02 us
  Pallas kernels: 25.9 us -> 20.5 us
  waiting for transfers between devices: 14.6 us -> 9.9 us
    slice x1 -> x0, local copies, waits for them, and re-layouts: 5.59 us -> none  [per_device(): loads_far = [other(loadings[at:at + CHUNK]) for at in starts]]
    pallas_call x8 -> x11, Pallas kernels: 25.9 us -> 20.5 us  [the longest x4 6.86 us: per_device(): call(functools.partial(part_kernel, firsts[i], steps), 'other_part', [mat...]
    ppermute x3, waiting for transfers between devices: 14.6 us -> 9.88 us  [per_device(): entering = lax.ppermute(leaving, 'tm', [(turn - 1, turn)])]
    unnamed x16 -> x8, local copies, waits for them, and re-layouts: 4.03 us -> 0.02 us
    ppermute x5 -> x4, starting transfers between devices: 1.09 us -> 1.18 us  [per_device(): other(sent[i])]
  transfers between devices with their start and end apart: 8 -> 7, of which waited for: 1 -> 1; matrix products, arithmetic and copies ran while one was open for 0% -> 0% of each run, Pallas kernels for 33% -> 41%
where the time goes in v2:
time: 35.3 us; the launch traced here: 35.1 us
  Pallas kernels  20.5 us (58%)
  waiting for transfers between devices  9.9 us (28%)
  starting transfers between devices  3.8 us (11%)
  between operations  0.86 us (2%)
    ppermute x3, waiting for transfers between devices, per_device(): entering = lax.ppermute(leaving, 'tm', [(turn - 1, turn)])  9.88 us
    pallas_call x4, Pallas kernels, per_device(): call(functools.partial(part_kernel, firsts[i], steps), 'other_part', [mat...  6.86 us
    pallas_call x1, Pallas kernels, per_device(): call(functools.partial(gain_kernel, firsts[1:], steps), 'own_gains', [mat...  3.61 us
    pallas_call x1, Pallas kernels, per_device(): call(functools.partial(last_kernel, blocks - 1 if blocks > 1 else -1, cou...  3.32 us
    ppermute x3, starting transfers between devices, per_device(): entering = lax.ppermute(leaving, 'tm', [(turn - 1, turn)])  2.62 us
    pallas_call x1, Pallas kernels, per_device(): call(functools.partial(third_kernel, firsts[2:], steps), 'later_parts', [...  2.6 us
    pallas_call x1, Pallas kernels, per_device(): call(stage_kernel, 'stage', chunk(sizes[0]) + [kept(outs, 128)], [FAR] *...  2.13 us
    pallas_call x1, Pallas kernels, per_device(): call(functools.partial(second_kernel, firsts[1], steps), 'second_part', c...  1.9 us
  transfers between devices with their start and end apart: 7, of which 1 were waited for; matrix products, arithmetic and copies ran while one was open for 0% of the time, Pallas kernels for 41%

profile of v2, /device:TPU:24, one launch (start us, length us, event | category | flops | bytes accessed | tf_op | source)
XLA Modules:
  0.0 35.1 jit_solution(16176196612803405937)
XLA Ops:
  0.6 0.0 copy-start
  0.6 0.0 copy-start.1
  0.7 0.0 copy-start.2
  0.7 2.1 %stage.1 = (f32[4,256,512]{2,1,0:T(8,128)S(1)}, f32[4,264,512]{2,1,0:T(8,128)S(1)}, f32[4,264,512]{2,1,0:T(8,128)S(1)}, f32[256,128]{1,0:T(8,128)S(1)}) custom-call(f32[12,256,512]{2,1,0:T(8,128)} %loads_far.5, s32[12,256]{1,0:T(8,128)} %observed_far.1, f32[12,256]{1,0:T(8,128)} %observations_far.1, f32[1,256]{1,0:T(1,128)} %bitcast.5), custom_call_target="tpu_custom_call" | custom-call | bytes 4194304 | tf_op jit(solution)/shard_map/stage/pallas_call | solution.py:341
  2.8 0.1 collective-permute-start
  2.9 0.0 copy-done
  2.9 0.0 copy-done.1
  2.9 0.0 copy-done.2
  2.9 1.9 %second_part.1 = (f32[4,256,512]{2,1,0:T(8,128)S(1)}, f32[4,264,512]{2,1,0:T(8,128)S(1)}, f32[4,264,512]{2,1,0:T(8,128)S(1)}, f32[2,8,512]{2,1,0:T(8,128)S(1)}, ...) custom-call(f32[12,256,512]{2,1,0:T(8,128)} %loads_far.5, f32[256,128]{1,0:T(8,128)S(1)} %get-tuple-element.44.columns, ...), custom_call_target="tpu_custom_call" | custom-call | bytes 4194304 | tf_op jit(solution)/shard_map/second_part/pallas_call | solution.py:356
  4.8 0.5 %collective-permute-start.1 = (f32[4,264,512]{2,1,0:T(8,128)S(1)}, f32[4,264,512]{2,1,0:T(8,128)S(1)}, u32[]{:S(2)}, u32[]{:S(2)}) collective-permute-start(f32[4,264,512]{2,1,0:T(8,128)S(1)} %get-tuple-element.50), channel_id=1, source_target_pairs={{0,1},{1,0},{2,3},{3,2},{4,5},{5,4},{6,7},{7,6},{8,9},{9,8},{10,11... | collective-permute-start | bytes 6488072 | tf_op jit(solution)/shard_map/ppermute | solution.py:397
  5.4 2.6 %later_parts.1 = (f32[4,264,512]{2,1,0:T(8,128)S(1)}, f32[3,256,512]{2,1,0:T(8,128)S(1)}, f32[3,264,512]{2,1,0:T(8,128)S(1)}, f32[3,264,512]{2,1,0:T(8,128)S(1)}...) custom-call(f32[12,256,512]{2,1,0:T(8,128)} %loads_far.5, ...), custom_call_target="tpu_custom_call" | custom-call | flops 1610612736 | bytes 4194304 | tf_op jit(solution)/shard_map/later_parts/pallas_call | solution.py:364
  8.0 0.1 collective-permute-start.2
  8.1 0.5 %collective-permute-start.3 = (f32[1,264,512]{2,1,0:T(8,128)S(1)}, f32[1,264,512]{2,1,0:T(8,128)S(1)}, u32[]{:S(2)}, u32[]{:S(2)}) collective-permute-start(f32[1,264,512]{2,1,0:T(8,128)S(1)} %get-tuple-element.58), channel_id=1, source_target_pairs={{0,1},{1,0},{2,3},{3,2},{4,5},{5,4},{6,7},{7,6},{8,9},{9,8},{10,11... | collective-permute-start | bytes 1622024 | tf_op jit(solution)/shard_map/ppermute | solution.py:397
  8.5 0.0 copy-start.3
  8.5 3.6 %own_gains.1 = (f32[4,264,512]{2,1,0:T(8,128)S(1)}, f32[3,264,512]{2,1,0:T(8,128)S(1)}, f32[1,264,512]{2,1,0:T(8,128)S(1)}) custom-call(bf16[512,512]{1,0:T(8,128)(2,1)S(1)} %get-tuple-element.46.gain_high, bf16[512,512]{1,0:T(8,128)(2,1)S(1)} %get-tuple-element.47.gain_low, f32[4,264,512]{2,1,0:T(8,128)S(1)} %get-tuple-element.51.scaled_own.rest_0_.refs_6_, ...), custom_call_target="tpu_custom_call" | custom-call | flops 3221225472 | tf_op jit(solution)/shard_map/own_gains/pallas_call | solution.py:376
  12.2 0.0 collective-permute-done.scaled_far
  12.2 0.0 copy-done.3
  12.2 2.2 %other_part.4 = (f32[4,264,512]{2,1,0:T(8,128)S(1)}, f32[4,264,512]{2,1,0:T(8,128)S(1)}, f32[4,512]{1,0:T(4,128)S(1)}, f32[8,512]{1,0:T(8,128)S(1)}) custom-call(f32[8,512]{1,0:T(8,128)S(1)} %broadcast_in_dim.15.entering, f32[4,264,512]{2,1,0:T(8,128)S(1)} %collective-permute-done.scaled_far, ...), custom_call_target="tpu_custom_call" | custom-call | flops 1610612736 | bytes 4194304 | tf_op jit(solution)/shard_map/other_part/pallas_call | solution.py:388
  14.4 0.0 collective-permute-done.1.scaled_far
  14.4 2.3 %other_part.5 = (f32[4,264,512]{2,1,0:T(8,128)S(1)}, f32[4,264,512]{2,1,0:T(8,128)S(1)}, f32[4,512]{1,0:T(4,128)S(1)}, f32[8,512]{1,0:T(8,128)S(1)}) custom-call(f32[8,512]{1,0:T(8,128)S(1)} %get-tuple-element.49.entering, f32[4,264,512]{2,1,0:T(8,128)S(1)} %collective-permute-done.1.scaled_far, ...), custom_call_target="tpu_custom_call" | custom-call | flops 1610612736 | bytes 4194304 | tf_op jit(solution)/shard_map/other_part/pallas_call | solution.py:388
  16.7 0.0 collective-permute-done.2.scaled_far
  16.7 1.7 %other_part.6 = (f32[3,264,512]{2,1,0:T(8,128)S(1)}, f32[3,264,512]{2,1,0:T(8,128)S(1)}, f32[3,512]{1,0:T(4,128)S(1)}, f32[8,512]{1,0:T(8,128)S(1)}) custom-call(f32[8,512]{1,0:T(8,128)S(1)} %get-tuple-element.53.entering, f32[3,264,512]{2,1,0:T(8,128)S(1)} %collective-permute-done.2.scaled_far, ...), custom_call_target="tpu_custom_call" | custom-call | flops 1207959552 | bytes 3145728 | tf_op jit(solution)/shard_map/other_part/pallas_call | solution.py:388
  18.4 0.0 collective-permute-done.3.scaled_far
  18.4 0.7 %other_part.7 = (f32[1,264,512]{2,1,0:T(8,128)S(1)}, f32[1,264,512]{2,1,0:T(8,128)S(1)}, f32[1,512]{1,0:T(1,128)S(1)}, f32[8,512]{1,0:T(8,128)S(1)}) custom-call(f32[8,512]{1,0:T(8,128)S(1)} %get-tuple-element.57.entering, f32[1,264,512]{2,1,0:T(8,128)S(1)} %collective-permute-done.3.scaled_far, ...), custom_call_target="tpu_custom_call" | custom-call | flops 402653184 | bytes 1048576 | tf_op jit(solution)/shard_map/other_part/pallas_call | solution.py:388
  19.1 0.7 %collective-permute-start.4 = (f32[8,512]{1,0:T(8,128)S(1)}, f32[8,512]{1,0:T(8,128)S(1)}, u32[]{:S(2)}, u32[]{:S(2)}) collective-permute-start(f32[8,512]{1,0:T(8,128)S(1)} %get-tuple-element.61), channel_id=1, source_target_pairs={{0,8},{1,9},{2,10},{3,11},{4,12},{5,13},{6,14},{7,15}} | collective-permute-start | bytes 49160 | tf_op jit(solution)/shard_map/ppermute | solution.py:406
  19.8 0.0 collective-permute-done.4.entering
  19.9 0.7 %collective-permute-start.5 = (f32[8,512]{1,0:T(8,128)S(1)}, f32[8,512]{1,0:T(8,128)S(1)}, u32[]{:S(2)}, u32[]{:S(2)}) collective-permute-start(f32[8,512]{1,0:T(8,128)S(1)} %get-tuple-element.79), channel_id=1, source_target_pairs={{8,16},{9,17},{10,18},{11,19},{12,20},{13,21},{14,22},{15,23}} | collective-permute-start | bytes 49160 | tf_op jit(solution)/shard_map/ppermute | solution.py:406
  20.5 0.0 collective-permute-done.5.entering
  20.6 1.3 %collective-permute-start.6 = (f32[8,512]{1,0:T(8,128)S(1)}, f32[8,512]{1,0:T(8,128)S(1)}, u32[]{:S(2)}, u32[]{:S(2)}) collective-permute-start(f32[8,512]{1,0:T(8,128)S(1)} %get-tuple-element.81), channel_id=1, source_target_pairs={{16,24},{17,25},{18,26},{19,27},{20,28},{21,29},{22,30},{23,31}} | collective-permute-start | bytes 49160 | tf_op jit(solution)/shard_map/ppermute | solution.py:406
  21.9 9.9 %collective-permute-done.6.entering = f32[8,512]{1,0:T(8,128)S(1)} collective-permute-done((f32[8,512]{1,0:T(8,128)S(1)}, f32[8,512]{1,0:T(8,128)S(1)}, u32[]{:S(2)}, u32[]{:S(2)}) %collective-permute-start.6) | collective-permute-done | bytes 16416 | tf_op jit(solution)/shard_map/ppermute | solution.py:406
  31.8 3.3 %last_chain.1 = (f32[12,128]{1,0:T(8,128)}, f32[12,256]{1,0:T(8,128)}) custom-call(f32[12,512]{1,0:T(8,128)S(1)} %get-tuple-element.80.before, f32[8,512]{1,0:T(8,128)S(1)} %collective-permute-done.6.entering, f32[2,8,512]{2,1,0:T(8,128)S(1)} %get-tuple-element.45.parts, f32[512,512]{1,0:T(8,128)S(1)} %copy-done, ...), custom_call_target="tpu_custom_call" | custom-call | flops 4831838208 | tf_op jit(solution)/shard_map/last_chain/pallas_call | solution.py:416
  (4 shorter events, 0.1 us)
Async XLA Ops:
  0.6 2.3 %copy-start = (f32[512,512]{1,0:T(8,128)S(1)}, f32[512,512]{1,0:T(8,128)}, u32[]{:S(2)}) copy-start(f32[512,512]{1,0:T(8,128)} %blend.15) | copy-start | bytes 3145732
  0.6 2.3 %copy-start.1 = (s32[256]{0:T(256)S(1)}, s32[256]{0:T(256)}, u32[]{:S(2)}) copy-start(s32[256]{0:T(256)} %param.14) | copy-start | bytes 3076
  0.7 2.3 %copy-start.2 = (f32[4]{0:T(128)S(1)}, f32[4]{0:T(128)}, u32[]{:S(2)}) copy-start(f32[4]{0:T(128)} %param.13) | copy-start | bytes 52
  2.8 9.4 %collective-permute-start = (f32[4,264,512]{2,1,0:T(8,128)S(1)}, f32[4,264,512]{2,1,0:T(8,128)S(1)}, u32[]{:S(2)}, u32[]{:S(2)}) collective-permute-start(f32[4,264,512]{2,1,0:T(8,128)S(1)} %get-tuple-element.42), channel_id=1, source_target_pairs={{0,1},{1,0},{2,3},{3,2},{4,5},{5,4},{6,7},{7,6},{8,9},{9,8},{10,11... | collective-permute-start | bytes 6488072 | tf_op jit(solution)/shard_map/ppermute | solution.py:397
  4.8 9.6 %collective-permute-start.1 = (f32[4,264,512]{2,1,0:T(8,128)S(1)}, f32[4,264,512]{2,1,0:T(8,128)S(1)}, u32[]{:S(2)}, u32[]{:S(2)}) collective-permute-start(f32[4,264,512]{2,1,0:T(8,128)S(1)} %get-tuple-element.50), channel_id=1, source_target_pairs={{0,1},{1,0},{2,3},{3,2},{4,5},{5,4},{6,7},{7,6},{8,9},{9,8},{10,11... | collective-permute-start | bytes 6488072 | tf_op jit(solution)/shard_map/ppermute | solution.py:397
  8.0 8.8 %collective-permute-start.2 = (f32[3,264,512]{2,1,0:T(8,128)S(1)}, f32[3,264,512]{2,1,0:T(8,128)S(1)}, u32[]{:S(2)}, u32[]{:S(2)}) collective-permute-start(f32[3,264,512]{2,1,0:T(8,128)S(1)} %get-tuple-element.54), channel_id=1, source_target_pairs={{0,1},{1,0},{2,3},{3,2},{4,5},{5,4},{6,7},{7,6},{8,9},{9,8},{10,11... | collective-permute-start | bytes 4866056 | tf_op jit(solution)/shard_map/ppermute | solution.py:397
  8.1 10.3 %collective-permute-start.3 = (f32[1,264,512]{2,1,0:T(8,128)S(1)}, f32[1,264,512]{2,1,0:T(8,128)S(1)}, u32[]{:S(2)}, u32[]{:S(2)}) collective-permute-start(f32[1,264,512]{2,1,0:T(8,128)S(1)} %get-tuple-element.58), channel_id=1, source_target_pairs={{0,1},{1,0},{2,3},{3,2},{4,5},{5,4},{6,7},{7,6},{8,9},{9,8},{10,11... | collective-permute-start | bytes 1622024 | tf_op jit(solution)/shard_map/ppermute | solution.py:397
  8.5 3.6 %copy-start.3 = (f32[512]{0:T(512)S(1)}, f32[512]{0:T(512)}, u32[]{:S(2)}) copy-start(f32[512]{0:T(512)} %param.15) | copy-start | bytes 6148
  19.1 0.7 %collective-permute-start.4 = (f32[8,512]{1,0:T(8,128)S(1)}, f32[8,512]{1,0:T(8,128)S(1)}, u32[]{:S(2)}, u32[]{:S(2)}) collective-permute-start(f32[8,512]{1,0:T(8,128)S(1)} %get-tuple-element.61), channel_id=1, source_target_pairs={{0,8},{1,9},{2,10},{3,11},{4,12},{5,13},{6,14},{7,15}} | collective-permute-start | bytes 49160 | tf_op jit(solution)/shard_map/ppermute | solution.py:406
  19.9 0.7 %collective-permute-start.5 = (f32[8,512]{1,0:T(8,128)S(1)}, f32[8,512]{1,0:T(8,128)S(1)}, u32[]{:S(2)}, u32[]{:S(2)}) collective-permute-start(f32[8,512]{1,0:T(8,128)S(1)} %get-tuple-element.79), channel_id=1, source_target_pairs={{8,16},{9,17},{10,18},{11,19},{12,20},{13,21},{14,22},{15,23}} | collective-permute-start | bytes 49160 | tf_op jit(solution)/shard_map/ppermute | solution.py:406
  20.6 11.2 %collective-permute-start.6 = (f32[8,512]{1,0:T(8,128)S(1)}, f32[8,512]{1,0:T(8,128)S(1)}, u32[]{:S(2)}, u32[]{:S(2)}) collective-permute-start(f32[8,512]{1,0:T(8,128)S(1)} %get-tuple-element.81), channel_id=1, source_target_pairs={{16,24},{17,25},{18,26},{19,27},{20,28},{21,29},{22,30},{23,31}} | collective-permute-start | bytes 49160 | tf_op jit(solution)/shard_map/ppermute | solution.py:406

commit v3 on v2

--- a/solution.py
+++ b/solution.py
@@ -11,7 +11,8 @@
 VMEM_LIMIT = 8 * 2**20
 LAST_PART = 1
 PARTS = 4
-SECOND_GAINS = 5
+GAIN_STEPS = (0, 8, 10)
+EARLY_STEPS = (0, 4, 2)
 WHOLE = pl.BlockSpec(memory_space=pltpu.VMEM)
 FAR = pl.BlockSpec(memory_space=pl.ANY)
 
@@ -52,7 +53,7 @@
 
 def part_sizes(steps):
     rest = steps - LAST_PART
-    sizes = [rest // (PARTS - 1) + (i < rest % (PARTS - 1)) for i in range(PARTS - 1)]
+    sizes = [(rest + PARTS - 2 - i) // (PARTS - 1) for i in range(PARTS - 1)]
     return sizes + [LAST_PART]
 
 
@@ -128,33 +129,39 @@
 
 
 def gain_limit(block, steps):
-    return (0, min(SECOND_GAINS, steps), steps)[min(block, 2)]
+    return min(GAIN_STEPS[block], steps) if block < len(GAIN_STEPS) else steps
+
+
+def early_limit(block, size):
+    return min(EARLY_STEPS[min(block, len(EARLY_STEPS) - 1)], size)
 
 
 def by_block(work, steps):
     block = lax.axis_index("tm")
-    for i in (1, 2):
-
-        @pl.when(block == 1 if i == 1 else block > 1)
+    kinds = min(len(GAIN_STEPS), lax.axis_size("tm") - 1)
+    for i in range(1, kinds + 1):
+
+        @pl.when(block == i if i < kinds else block >= i)
         def _():
-            work(gain_limit(i, steps))
-
-
-def fill_gains(limit, first, scaled, gain_high, gain_low, gained):
+            work(i, gain_limit(i, steps))
+
+
+def fill_gains(limit, first, scaled, gain_high, gain_low, gained, begin=0):
     rows = scaled.shape[1]
-    for k in range(min(scaled.shape[0], limit - first)):
+    for k in range(begin, min(scaled.shape[0], limit - first)):
         block = jnp.concatenate([scaled[k], scaled[k, rows - 8 :, :]], axis=0)
         gained[k] = times_gain(block, gain_high[...], gain_low[...])[:rows]
 
 
 def second_kernel(
-    first, steps, loads_far, columns, rates, pairs, blend,
-    loads, scaled, sent, parts, gain_high, gain_low, sems,
+    first, steps, loads_far, columns, rates, pairs, blend, mean,
+    loads, scaled, sent, parts, gain_high, gain_low, initial, sems,
 ):
     copies = fetched(loads_far, first, loads, sems)
     diagonal, cross = transition(rates, pairs, blend.shape[1])
     parts[0] = diagonal
     parts[1] = cross
+    initial[...] = jnp.broadcast_to(mean[...], initial.shape)
 
     @pl.when(lax.axis_index("tm") != 0)
     def _():
@@ -177,7 +184,7 @@
         for first, group, sem in zip(firsts, groups, sems)
     ]
 
-    def work(limit):
+    def work(block, limit):
         fill_gains(limit, 0, scaled_first, gain_high, gain_low, gained_first)
 
     by_block(work, steps)
@@ -189,7 +196,7 @@
 def gain_kernel(firsts, steps, gain_high, gain_low, *rest):
     count = len(firsts)
 
-    def work(limit):
+    def work(block, limit):
         for first, scaled, gained in zip(firsts, rest[:count], rest[count:]):
             fill_gains(limit, first, scaled, gain_high, gain_low, gained)
 
@@ -229,9 +236,10 @@
 
 
 def part_kernel(
-    first, steps, entering, scaled_far, scaled_own, parts, blend, gain_high, gain_low,
-    scaled, gained, states, leaving, sem,
+    early, steps, entering, scaled_far, scaled_own, parts, blend, gain_high, gain_low,
+    scaled, states, leaving, *rest,
 ):
+    *gained, sem = rest
     copied(scaled_far, scaled, sem).wait()
     block = lax.axis_index("tm")
 
@@ -244,23 +252,42 @@
             states[k : k + 1, :] = state[0:1, :]
         leaving[...] = state
 
-    def work(limit):
-        fill_gains(limit, first, scaled, gain_high, gain_low, gained)
+    def work(block, limit):
+        fill_gains(
+            early_limit(block, scaled.shape[0]), 0, scaled, gain_high, gain_low, *gained
+        )
+
+    if early:
+        by_block(work, steps)
+
+
+def late_kernel(firsts, steps, _, gain_high, gain_low, *rest):
+    count = len(firsts)
+    parts = list(zip(firsts, rest[:count], rest[count:]))
+
+    def work(block, limit):
+        for i, (first, scaled, gained) in enumerate(parts):
+            begin = 0 if i else early_limit(block, scaled.shape[0])
+            fill_gains(limit, first, scaled, gain_high, gain_low, gained, begin)
 
     by_block(work, steps)
 
 
-def chain(limit, entering, parts, blend, operands, states):
+def chain(turn, entering, parts, blend, operands, early, states, observe=None):
+    limit = gain_limit(turn, states.shape[0])
     state = jnp.broadcast_to(entering[0:1, :], parts.shape[1:])
     at = 0
     for _, own, gained_own, scaled, gained in operands:
         for k in range(own.shape[0]):
             pair = (own.at[k], scaled.at[k])
             if at < limit:
-                state = advance(state, pair, (gained_own.at[k], gained.at[k]), parts)
+                other = early if at < early_limit(turn, early.shape[0]) else gained
+                state = advance(state, pair, (gained_own.at[k], other.at[k]), parts)
             else:
                 state = advance(state, pair, pair, parts, blend)
             states[at : at + 1, :] = state[0:1, :]
+            if observe is not None:
+                observe(at, state)
             at += 1
     return state
 
@@ -269,14 +296,13 @@
     return [refs[5 * i : 5 * i + 5] for i in range(count)], refs[5 * count :]
 
 
-def block_kernel(turn, count, before, entering, parts, blend, *refs):
+def block_kernel(turn, count, before, entering, parts, blend, early, *refs):
     operands, (states, leaving) = grouped(refs, count)
     block = lax.axis_index("tm")
 
     @pl.when(block == turn)
     def _():
-        limit = gain_limit(turn, states.shape[0])
-        leaving[...] = chain(limit, entering, parts, blend, operands, states)
+        leaving[...] = chain(turn, entering, parts, blend, operands, early, states)
 
     @pl.when(block != turn)
     def _():
@@ -284,30 +310,41 @@
         leaving[...] = jnp.zeros_like(leaving)
 
 
-def last_kernel(turn, count, before, entering, parts, blend, *refs):
+def last_kernel(turn, count, before, entering, parts, blend, early, *refs):
     operands, (own_states, predicted, states, readings) = grouped(refs, count)
     block = lax.axis_index("tm")
+    rows = [loads.at[k] for loads, *_ in operands for k in range(loads.shape[0])]
+
+    def observe(at, state):
+        outs = rows[at].shape[0]
+        for row in range(0, outs, 8):
+            product = rows[at][row : row + 8, :] * state
+            readings[row : row + 8, at : at + 1] = jnp.sum(product, axis=1, keepdims=True)
 
     @pl.when(block == turn)
     def _():
-        limit = gain_limit(turn, states.shape[0])
-        chain(limit, entering, parts, blend, operands, states)
+        chain(turn, entering, parts, blend, operands, early, states, observe)
 
     @pl.when(block != turn)
     def _():
         states[...] = before[...]
+        for at in range(states.shape[0]):
+            observe(at, jnp.broadcast_to(before[at : at + 1, :], parts.shape[1:]))
 
     share = own_states.shape[1]
     start = pl.multiple_of(lax.axis_index("state") * share, share)
     own_states[...] = states[:, pl.ds(start, share)]
-    at = 0
-    for loads, *_ in operands:
-        for k in range(loads.shape[0]):
-            readings[:, at : at + 1] = jnp.sum(
-                loads[k] * states[at : at + 1, :], axis=1, keepdims=True
-            )
-            at += 1
-    predicted[...] = readings[...].T[:at, :]
+    predicted[...] = readings[...].T[: states.shape[0], :]
+
+
+def hop_pairs(turn, blocks):
+    if 1 < turn < blocks - 1:
+        return [(i, (i + 1) % blocks) for i in range(blocks)]
+    rest = [i for i in range(blocks) if i not in (turn - 1, turn)]
+    pairs = [(turn - 1, turn), (turn, turn - 1)]
+    for i, j in zip(rest[::2], rest[1::2]):
+        pairs += [(i, j), (j, i)]
+    return pairs + [(i, i) for i in rest[len(rest) // 2 * 2 :]]
 
 
 def per_device(
@@ -325,7 +362,6 @@
     sizes = part_sizes(steps)
     count = len(sizes)
     firsts = [sum(sizes[:i]) for i in range(count)]
-    initial = jnp.broadcast_to(initial_mean[None, :], (8, width))
 
     half = 2 * 3 * outs * width * width
     vector, gain_type = kept(8, width), kept(width, width, dtype=BF16)
@@ -353,14 +389,17 @@
         ],
         moved=8 * sizes[0] * outs * width,
     )(loadings, in_hbm(observed), in_hbm(observations), in_hbm(noise_precision[None, :]))
-    *second_chunk, parts, gain_high, gain_low = call(
+    *second_chunk, parts, gain_high, gain_low, initial = call(
         functools.partial(second_kernel, firsts[1], steps),
         "second_part",
-        chunk(sizes[1]) + [kept(2, 8, width), gain_type, gain_type],
-        [FAR] + [WHOLE] * 4,
+        chunk(sizes[1]) + [kept(2, 8, width), gain_type, gain_type, vector],
+        [FAR] + [WHOLE] * 5,
         [sems((sizes[1],))],
         moved=8 * sizes[1] * outs * width,
-    )(loadings, columns, latent_rates[None, :], pair_latent[None, :], blend_matrix)
+    )(
+        loadings, columns, latent_rates[None, :], pair_latent[None, :], blend_matrix,
+        initial_mean[None, :],
+    )
     gained_first, *later = call(
         functools.partial(third_kernel, firsts[2:], steps),
         "later_parts",
@@ -383,27 +422,39 @@
     )
 
     leaving = initial
-    operands, states = [], []
+    scaled, states, early = [], [], []
     for i in range(count):
-        scaled, gained, state, leaving = call(
-            functools.partial(part_kernel, firsts[i], steps),
+        rows, state, leaving, *gained = call(
+            functools.partial(part_kernel, i == 0, steps),
             "other_part",
-            [matrices(sizes[i]), matrices(sizes[i]), kept(sizes[i], width), vector],
+            [matrices(sizes[i]), kept(sizes[i], width), vector]
+            + ([matrices(sizes[i])] if i == 0 else []),
             [WHOLE, FAR] + [WHOLE] * 5,
             [sems],
-            flops=sizes[i] * half,
+            flops=sizes[i] * half // 3,
             moved=8 * sizes[i] * outs * width,
         )(
             leaving, other(sent[i]), scaled_own[i], parts, blend_matrix, gain_high, gain_low
         )
-        operands += [loads_own[i], scaled_own[i], gained_own[i], scaled, gained]
+        scaled.append(rows)
         states.append(state)
+        early += gained
     states = jnp.concatenate(states, axis=0)
+    gained = call(
+        functools.partial(late_kernel, firsts, steps),
+        "late_gains",
+        [matrices(size) for size in sizes],
+        [FAR] + [WHOLE] * (2 + count),
+        flops=steps * half,
+    )(leaving, gain_high, gain_low, *scaled)
+    operands = [*early]
+    for group in zip(loads_own, scaled_own, gained_own, scaled, gained):
+        operands += group
 
     specs = [WHOLE] * (4 + len(operands))
     entering = leaving
     for turn in range(1, blocks):
-        entering = lax.ppermute(leaving, "tm", [(turn - 1, turn)])
+        entering = lax.ppermute(leaving, "tm", hop_pairs(turn, blocks))
         if turn < blocks - 1:
             states, leaving = call(
                 functools.partial(block_kernel, turn, count),

time: 35.3 us -> 31.4 us (0.89)
  waiting for transfers between devices: 9.9 us -> 5.46 us
  starting transfers between devices: 3.8 us -> 4.83 us
  Pallas kernels: 20.5 us -> 20 us
    ppermute x3, waiting for transfers between devices: 9.88 us -> 5.45 us  [per_device(): entering = lax.ppermute(leaving, 'tm', hop_pairs(turn, blocks))]
    ppermute x3, starting transfers between devices: 2.62 us -> 3.65 us  [per_device(): entering = lax.ppermute(leaving, 'tm', hop_pairs(turn, blocks))]
    pallas_call x4 -> x5, Pallas kernels: 6.86 us -> 6.62 us  [the longest x1 4.76 us: per_device(): call(functools.partial(late_kernel, firsts, steps), 'late_gains', [matric...]
  transfers between devices with their start and end apart: 7 -> 7, of which waited for: 1 -> 2; matrix products, arithmetic and copies ran while one was open for 0% -> 0% of each run, Pallas kernels for 41% -> 47%
where the time goes in v3:
time: 31.4 us; the launch traced here: 31.2 us
  Pallas kernels  20 us (64%)
  waiting for transfers between devices  5.46 us (17%)
  starting transfers between devices  4.83 us (15%)
  between operations  0.85 us (3%)
    ppermute x3, waiting for transfers between devices, per_device(): entering = lax.ppermute(leaving, 'tm', hop_pairs(turn, blocks))  5.45 us
    pallas_call x1, Pallas kernels, per_device(): call(functools.partial(late_kernel, firsts, steps), 'late_gains', [matric...  4.76 us
    pallas_call x1, Pallas kernels, per_device(): call(functools.partial(gain_kernel, firsts[1:], steps), 'own_gains', [mat...  3.65 us
    ppermute x3, starting transfers between devices, per_device(): entering = lax.ppermute(leaving, 'tm', hop_pairs(turn, blocks))  3.65 us
    pallas_call x1, Pallas kernels, per_device(): call(functools.partial(last_kernel, blocks - 1 if blocks > 1 else -1, cou...  3.11 us
    pallas_call x1, Pallas kernels, per_device(): call(functools.partial(third_kernel, firsts[2:], steps), 'later_parts', [...  2.62 us
    pallas_call x1, Pallas kernels, per_device(): call(stage_kernel, 'stage', chunk(sizes[0]) + [kept(outs, 128)], [FAR] *...  2.12 us
    pallas_call x1, Pallas kernels, per_device(): call(functools.partial(second_kernel, firsts[1], steps), 'second_part', c...  1.9 us
  transfers between devices with their start and end apart: 7, of which 2 were waited for; matrix products, arithmetic and copies ran while one was open for 0% of the time, Pallas kernels for 47%

profile of v3, /device:TPU:24, one launch (start us, length us, event | category | flops | bytes accessed | tf_op | source)
XLA Modules:
  0.0 31.2 jit_solution(13782046656339226542)
XLA Ops:
  0.6 0.0 copy-start
  0.6 0.0 copy-start.1
  0.7 0.0 copy-start.2
  0.7 0.0 copy-start.3
  0.7 2.1 %stage.1 = (f32[4,256,512]{2,1,0:T(8,128)S(1)}, f32[4,264,512]{2,1,0:T(8,128)S(1)}, f32[4,264,512]{2,1,0:T(8,128)S(1)}, f32[256,128]{1,0:T(8,128)S(1)}) custom-call(f32[12,256,512]{2,1,0:T(8,128)} %loads_far.5, s32[12,256]{1,0:T(8,128)} %observed_far.1, f32[12,256]{1,0:T(8,128)} %observations_far.1, f32[1,256]{1,0:T(1,128)} %bitcast.7), custom_call_target="tpu_custom_call" | custom-call | bytes 4194304 | tf_op jit(solution)/shard_map/stage/pallas_call | solution.py:377
  2.8 0.1 collective-permute-start
  2.9 0.0 copy-done
  2.9 0.0 copy-done.1
  2.9 0.0 copy-done.2
  2.9 0.0 copy-done.3
  2.9 1.9 %second_part.1 = (f32[4,256,512]{2,1,0:T(8,128)S(1)}, f32[4,264,512]{2,1,0:T(8,128)S(1)}, f32[4,264,512]{2,1,0:T(8,128)S(1)}, f32[2,8,512]{2,1,0:T(8,128)S(1)}, ...) custom-call(f32[12,256,512]{2,1,0:T(8,128)} %loads_far.5, ...), custom_call_target="tpu_custom_call" | custom-call | bytes 4194304 | tf_op jit(solution)/shard_map/second_part/pallas_call | solution.py:392
  4.8 0.5 %collective-permute-start.1 = (f32[4,264,512]{2,1,0:T(8,128)S(1)}, f32[4,264,512]{2,1,0:T(8,128)S(1)}, u32[]{:S(2)}, u32[]{:S(2)}) collective-permute-start(f32[4,264,512]{2,1,0:T(8,128)S(1)} %get-tuple-element.53), channel_id=1, source_target_pairs={{0,1},{1,0},{2,3},{3,2},{4,5},{5,4},{6,7},{7,6},{8,9},{9,8},{10,11... | collective-permute-start | bytes 6488072 | tf_op jit(solution)/shard_map/ppermute | solution.py:437
  5.4 2.6 %later_parts.1 = (f32[4,264,512]{2,1,0:T(8,128)S(1)}, f32[3,256,512]{2,1,0:T(8,128)S(1)}, f32[3,264,512]{2,1,0:T(8,128)S(1)}, f32[3,264,512]{2,1,0:T(8,128)S(1)}...) custom-call(f32[12,256,512]{2,1,0:T(8,128)} %loads_far.5, ...), custom_call_target="tpu_custom_call" | custom-call | flops 1610612736 | bytes 4194304 | tf_op jit(solution)/shard_map/later_parts/pallas_call | solution.py:403
  8.0 0.1 collective-permute-start.2
  8.1 0.5 %collective-permute-start.3 = (f32[1,264,512]{2,1,0:T(8,128)S(1)}, f32[1,264,512]{2,1,0:T(8,128)S(1)}, u32[]{:S(2)}, u32[]{:S(2)}) collective-permute-start(f32[1,264,512]{2,1,0:T(8,128)S(1)} %get-tuple-element.61), channel_id=1, source_target_pairs={{0,1},{1,0},{2,3},{3,2},{4,5},{5,4},{6,7},{7,6},{8,9},{9,8},{10,11... | collective-permute-start | bytes 1622024 | tf_op jit(solution)/shard_map/ppermute | solution.py:437
  8.6 3.7 %own_gains.1 = (f32[4,264,512]{2,1,0:T(8,128)S(1)}, f32[3,264,512]{2,1,0:T(8,128)S(1)}, f32[1,264,512]{2,1,0:T(8,128)S(1)}) custom-call(bf16[512,512]{1,0:T(8,128)(2,1)S(1)} %get-tuple-element.49.gain_high, bf16[512,512]{1,0:T(8,128)(2,1)S(1)} %get-tuple-element.50.gain_low, f32[4,264,512]{2,1,0:T(8,128)S(1)} %get-tuple-element.54.scaled_own.rest_0_.refs_6_, ...), custom_call_target="tpu_custom_call" | custom-call | flops 3221225472 | tf_op jit(solution)/shard_map/own_gains/pallas_call | solution.py:415
  12.2 0.0 collective-permute-done.scaled_far
  12.2 1.3 %other_part.4 = (f32[4,264,512]{2,1,0:T(8,128)S(1)}, f32[4,512]{1,0:T(4,128)S(1)}, f32[8,512]{1,0:T(8,128)S(1)}, f32[4,264,512]{2,1,0:T(8,128)S(1)}) custom-call(f32[8,512]{1,0:T(8,128)S(1)} %get-tuple-element.45.entering, f32[4,264,512]{2,1,0:T(8,128)S(1)} %collective-permute-done.scaled_far, ...), custom_call_target="tpu_custom_call" | custom-call | flops 536870912 | bytes 4194304 | tf_op jit(solution)/shard_map/other_part/pallas_call | solution.py:427
  13.6 0.0 collective-permute-done.1.scaled_far
  13.6 0.3 other_part.5
  13.8 0.0 collective-permute-done.2.scaled_far
  13.8 0.2 other_part.6
  14.1 0.0 collective-permute-done.3.scaled_far
  14.1 0.1 other_part.7
  14.2 0.1 collective-permute-start.4
  14.2 4.8 %late_gains.1 = (f32[4,264,512]{2,1,0:T(8,128)S(1)}, f32[4,264,512]{2,1,0:T(8,128)S(1)}, f32[3,264,512]{2,1,0:T(8,128)S(1)}, f32[1,264,512]{2,1,0:T(8,128)S(1)}) custom-call(f32[8,512]{1,0:T(8,128)S(1)} %get-tuple-element.64._, bf16[512,512]{1,0:T(8,128)(2,1)S(1)} %get-tuple-element.49.gain_high, bf16[512,512]{1,0:T(8,128)(2,1)S(1)} %get-tuple-element.50.gain_low, ...), custom_call_target="tpu_custom_call" | custom-call | flops 4831838208 | tf_op jit(solution)/shard_map/late_gains/pallas_call | solution.py:443
  19.0 0.0 collective-permute-done.4.entering
  19.1 0.1 collective-permute-start.5
  19.1 3.7 %collective-permute-done.5.entering = f32[8,512]{1,0:T(8,128)S(1)} collective-permute-done((f32[8,512]{1,0:T(8,128)S(1)}, f32[8,512]{1,0:T(8,128)S(1)}, u32[]{:S(2)}, u32[]{:S(2)}) %collective-permute-start.5) | collective-permute-done | bytes 16416 | tf_op jit(solution)/shard_map/ppermute | solution.py:457
  22.9 3.5 %collective-permute-start.6 = (f32[8,512]{1,0:T(8,128)S(1)}, f32[8,512]{1,0:T(8,128)S(1)}, u32[]{:S(2)}, u32[]{:S(2)}) collective-permute-start(f32[8,512]{1,0:T(8,128)S(1)} %get-tuple-element.85), channel_id=1, source_target_pairs={{16,24},{24,16},{0,8},{8,0},{17,25},{25,17},{1,9},{9,1},{18,26},{2... | collective-permute-start | bytes 49160 | tf_op jit(solution)/shard_map/ppermute | solution.py:457
  26.4 1.7 %collective-permute-done.6.entering = f32[8,512]{1,0:T(8,128)S(1)} collective-permute-done((f32[8,512]{1,0:T(8,128)S(1)}, f32[8,512]{1,0:T(8,128)S(1)}, u32[]{:S(2)}, u32[]{:S(2)}) %collective-permute-start.6) | collective-permute-done | bytes 16416 | tf_op jit(solution)/shard_map/ppermute | solution.py:457
  28.1 3.1 %last_chain.1 = (f32[12,128]{1,0:T(8,128)}, f32[12,256]{1,0:T(8,128)}) custom-call(f32[12,512]{1,0:T(8,128)S(1)} %get-tuple-element.84.before, f32[8,512]{1,0:T(8,128)S(1)} %collective-permute-done.6.entering, f32[2,8,512]{2,1,0:T(8,128)S(1)} %get-tuple-element.48.parts, f32[512,512]{1,0:T(8,128)S(1)} %copy-done, ...), custom_call_target="tpu_custom_call" | custom-call | flops 4831838208 | tf_op jit(solution)/shard_map/last_chain/pallas_call | solution.py:467
  (3 shorter events, 0.0 us)
Async XLA Ops:
  0.6 2.2 %copy-start = (f32[512,512]{1,0:T(8,128)S(1)}, f32[512,512]{1,0:T(8,128)}, u32[]{:S(2)}) copy-start(f32[512,512]{1,0:T(8,128)} %blend.15) | copy-start | bytes 3145732
  0.6 2.2 %copy-start.1 = (f32[512]{0:T(512)S(1)}, f32[512]{0:T(512)}, u32[]{:S(2)}) copy-start(f32[512]{0:T(512)} %param.15) | copy-start | bytes 6148
  0.7 2.2 %copy-start.2 = (s32[256]{0:T(256)S(1)}, s32[256]{0:T(256)}, u32[]{:S(2)}) copy-start(s32[256]{0:T(256)} %param.14) | copy-start | bytes 3076
  0.7 2.2 %copy-start.3 = (f32[4]{0:T(128)S(1)}, f32[4]{0:T(128)}, u32[]{:S(2)}) copy-start(f32[4]{0:T(128)} %param.13) | copy-start | bytes 52
  2.8 9.4 %collective-permute-start = (f32[4,264,512]{2,1,0:T(8,128)S(1)}, f32[4,264,512]{2,1,0:T(8,128)S(1)}, u32[]{:S(2)}, u32[]{:S(2)}) collective-permute-start(f32[4,264,512]{2,1,0:T(8,128)S(1)} %get-tuple-element.46), channel_id=1, source_target_pairs={{0,1},{1,0},{2,3},{3,2},{4,5},{5,4},{6,7},{7,6},{8,9},{9,8},{10,11... | collective-permute-start | bytes 6488072 | tf_op jit(solution)/shard_map/ppermute | solution.py:437
  4.8 8.7 %collective-permute-start.1 = (f32[4,264,512]{2,1,0:T(8,128)S(1)}, f32[4,264,512]{2,1,0:T(8,128)S(1)}, u32[]{:S(2)}, u32[]{:S(2)}) collective-permute-start(f32[4,264,512]{2,1,0:T(8,128)S(1)} %get-tuple-element.53), channel_id=1, source_target_pairs={{0,1},{1,0},{2,3},{3,2},{4,5},{5,4},{6,7},{7,6},{8,9},{9,8},{10,11... | collective-permute-start | bytes 6488072 | tf_op jit(solution)/shard_map/ppermute | solution.py:437
  8.0 5.9 %collective-permute-start.2 = (f32[3,264,512]{2,1,0:T(8,128)S(1)}, f32[3,264,512]{2,1,0:T(8,128)S(1)}, u32[]{:S(2)}, u32[]{:S(2)}) collective-permute-start(f32[3,264,512]{2,1,0:T(8,128)S(1)} %get-tuple-element.57), channel_id=1, source_target_pairs={{0,1},{1,0},{2,3},{3,2},{4,5},{5,4},{6,7},{7,6},{8,9},{9,8},{10,11... | collective-permute-start | bytes 4866056 | tf_op jit(solution)/shard_map/ppermute | solution.py:437
  8.1 6.0 %collective-permute-start.3 = (f32[1,264,512]{2,1,0:T(8,128)S(1)}, f32[1,264,512]{2,1,0:T(8,128)S(1)}, u32[]{:S(2)}, u32[]{:S(2)}) collective-permute-start(f32[1,264,512]{2,1,0:T(8,128)S(1)} %get-tuple-element.61), channel_id=1, source_target_pairs={{0,1},{1,0},{2,3},{3,2},{4,5},{5,4},{6,7},{7,6},{8,9},{9,8},{10,11... | collective-permute-start | bytes 1622024 | tf_op jit(solution)/shard_map/ppermute | solution.py:437
  14.2 4.9 %collective-permute-start.4 = (f32[8,512]{1,0:T(8,128)S(1)}, f32[8,512]{1,0:T(8,128)S(1)}, u32[]{:S(2)}, u32[]{:S(2)}) collective-permute-start(f32[8,512]{1,0:T(8,128)S(1)} %get-tuple-element.64._), channel_id=1, source_target_pairs={{0,8},{8,0},{16,24},{24,16},{1,9},{9,1},{17,25},{25,17},{2,10},{10... | collective-permute-start | bytes 49160 | tf_op jit(solution)/shard_map/ppermute | solution.py:457
  19.1 3.8 %collective-permute-start.5 = (f32[8,512]{1,0:T(8,128)S(1)}, f32[8,512]{1,0:T(8,128)S(1)}, u32[]{:S(2)}, u32[]{:S(2)}) collective-permute-start(f32[8,512]{1,0:T(8,128)S(1)} %get-tuple-element.83), channel_id=1, source_target_pairs={{0,8},{8,16},{16,24},{24,0},{1,9},{9,17},{17,25},{25,1},{2,10},{10... | collective-permute-start | bytes 49160 | tf_op jit(solution)/shard_map/ppermute | solution.py:457
  22.9 5.2 %collective-permute-start.6 = (f32[8,512]{1,0:T(8,128)S(1)}, f32[8,512]{1,0:T(8,128)S(1)}, u32[]{:S(2)}, u32[]{:S(2)}) collective-permute-start(f32[8,512]{1,0:T(8,128)S(1)} %get-tuple-element.85), channel_id=1, source_target_pairs={{16,24},{24,16},{0,8},{8,0},{17,25},{25,17},{1,9},{9,1},{18,26},{2... | collective-permute-start | bytes 49160 | tf_op jit(solution)/shard_map/ppermute | solution.py:457

commit v4 on v3

--- a/solution.py
+++ b/solution.py
@@ -11,8 +11,8 @@
 VMEM_LIMIT = 8 * 2**20
 LAST_PART = 1
 PARTS = 4
-GAIN_STEPS = (0, 8, 10)
-EARLY_STEPS = (0, 4, 2)
+GAIN_STEPS = (0, 7, 9)
+EARLY_STEPS = (0, 2, 2, 0)
 WHOLE = pl.BlockSpec(memory_space=pltpu.VMEM)
 FAR = pl.BlockSpec(memory_space=pl.ANY)
 
@@ -69,17 +69,25 @@
     ]
 
 
+def split(ref, size):
+    outs = (ref.shape[0] - 8) // size
+    return [
+        (ref.at[pl.ds(k * outs, outs), :], ref.at[pl.ds(size * outs + k, 1), :])
+        for k in range(size)
+    ]
+
+
 def scale(copies, first, steps, loads, columns, scaled, sent):
-    outs = loads.shape[1]
+    size = loads.shape[0]
+    targets = list(zip(split(scaled, size), split(sent, size)))
     for k, copy in enumerate(copies):
         at = first + k
         copy.wait()
         rows = loads[k] * columns[:, at : at + 1]
         tail = jnp.sum(columns[:, steps + at : steps + at + 1] * rows, axis=0, keepdims=True)
-        tail = jnp.broadcast_to(tail, (8, tail.shape[1]))
-        for target in (sent, scaled):
-            target[k, :outs, :] = rows
-            target[k, outs:, :] = tail
+        for target, target_tail in targets[k]:
+            target[...] = rows
+            target_tail[...] = tail
 
 
 def stage_kernel(
@@ -104,7 +112,7 @@
     root = jnp.sqrt(observed[...].astype(F32) * noise[...])
     turned[:steps, :] = root
     turned[steps : 2 * steps, :] = root * observations[...]
-    columns[...] = turned[...].T
+    columns[:, : turned.shape[0]] = turned[...].T
     scale(copies, 0, steps, loads, columns, scaled, sent)
 
 
@@ -146,35 +154,20 @@
             work(i, gain_limit(i, steps))
 
 
-def fill_gains(limit, first, scaled, gain_high, gain_low, gained, begin=0):
-    rows = scaled.shape[1]
-    for k in range(begin, min(scaled.shape[0], limit - first)):
-        block = jnp.concatenate([scaled[k], scaled[k, rows - 8 :, :]], axis=0)
-        gained[k] = times_gain(block, gain_high[...], gain_low[...])[:rows]
-
-
-def second_kernel(
-    first, steps, loads_far, columns, rates, pairs, blend, mean,
-    loads, scaled, sent, parts, gain_high, gain_low, initial, sems,
-):
-    copies = fetched(loads_far, first, loads, sems)
-    diagonal, cross = transition(rates, pairs, blend.shape[1])
-    parts[0] = diagonal
-    parts[1] = cross
-    initial[...] = jnp.broadcast_to(mean[...], initial.shape)
-
-    @pl.when(lax.axis_index("tm") != 0)
-    def _():
-        gain = blend[...]
-        gain = gain * diagonal[0:1] + swap_pairs(gain) * cross[0:1]
-        gain_high[...], gain_low[...] = halves(gain)
-
-    scale(copies, first, steps, loads, columns, scaled, sent)
-
-
-def third_kernel(
-    firsts, steps, loads_far, columns, scaled_first, gain_high, gain_low,
-    gained_first, *rest,
+def fill_gains(limit, first, size, scaled, gain_high, gain_low, gained, begin=0):
+    tails = scaled[scaled.shape[0] - 8 :, :]
+    sources, targets = split(scaled, size), split(gained, size)
+    for k in range(begin, min(size, limit - first)):
+        rows = jnp.concatenate([sources[k][0][...], tails, tails], axis=0)
+        rows = times_gain(rows, gain_high[...], gain_low[...])
+        outs = rows.shape[0] - 16
+        targets[k][0][...] = rows[:outs]
+        targets[k][1][...] = rows[outs + k : outs + k + 1]
+
+
+def rest_kernel(
+    firsts, steps, loads_far, columns, rates, pairs, blend, mean,
+    parts, gain_high, gain_low, initial, *rest,
 ):
     count = len(firsts)
     groups = [rest[3 * i : 3 * i + 3] for i in range(count)]
@@ -183,22 +176,28 @@
         fetched(loads_far, first, group[0], sem)
         for first, group, sem in zip(firsts, groups, sems)
     ]
-
-    def work(block, limit):
-        fill_gains(limit, 0, scaled_first, gain_high, gain_low, gained_first)
-
-    by_block(work, steps)
+    diagonal, cross = transition(rates, pairs, blend.shape[1])
+    parts[0] = diagonal
+    parts[1] = cross
+    initial[...] = jnp.broadcast_to(mean[...], initial.shape)
+
+    @pl.when(lax.axis_index("tm") != 0)
+    def _():
+        gain = blend[...]
+        gain = gain * diagonal[0:1] + swap_pairs(gain) * cross[0:1]
+        gain_high[...], gain_low[...] = halves(gain)
+
     for first, group, copy in zip(firsts, groups, copies):
         loads, scaled, sent = group
         scale(copy, first, steps, loads, columns, scaled, sent)
 
 
-def gain_kernel(firsts, steps, gain_high, gain_low, *rest):
+def gain_kernel(firsts, sizes, steps, gain_high, gain_low, *rest):
     count = len(firsts)
 
     def work(block, limit):
-        for first, scaled, gained in zip(firsts, rest[:count], rest[count:]):
-            fill_gains(limit, first, scaled, gain_high, gain_low, gained)
+        for first, size, scaled, gained in zip(firsts, sizes, rest[:count], rest[count:]):
+            fill_gains(limit, first, size, scaled, gain_high, gain_low, gained)
 
     by_block(work, steps)
 
@@ -222,53 +221,53 @@
 
 def advance(state, scaled, gained, parts, blend=None):
     pull = 0.0
-    for rows, gains in zip(scaled, gained):
-        outs = rows.shape[0] - 8
+    for (rows, _), (gains, shift) in zip(scaled, gained):
         total = jnp.zeros_like(state)
-        for row in range(0, outs, 8):
+        for row in range(0, rows.shape[0], 8):
             block = rows[row : row + 8, :]
             reading = jnp.sum(block * state, axis=1, keepdims=True)
             total = total + reading * (block if blend is not None else gains[row : row + 8, :])
-        pull += jnp.sum(total, axis=0, keepdims=True) - gains[outs : outs + 1, :]
+        pull += jnp.sum(total, axis=0, keepdims=True) - shift[...]
     if blend is not None:
         state, pull = reflected(state, pull, blend), 0.0
     return state * parts[0] + swap_pairs(state) * parts[1] - pull
 
 
 def part_kernel(
-    early, steps, entering, scaled_far, scaled_own, parts, blend, gain_high, gain_low,
+    early, size, steps, entering, arrived, scaled_own, parts, blend, gain_high, gain_low,
     scaled, states, leaving, *rest,
 ):
     *gained, sem = rest
-    copied(scaled_far, scaled, sem).wait()
     block = lax.axis_index("tm")
 
     @pl.when(block == 0)
     def _():
         state = jnp.broadcast_to(entering[0:1, :], parts.shape[1:])
-        for k in range(scaled.shape[0]):
-            pair = (scaled_own.at[k], scaled.at[k])
+        for k, pair in enumerate(zip(split(scaled_own, size), split(arrived, size))):
             state = advance(state, pair, pair, parts, blend)
             states[k : k + 1, :] = state[0:1, :]
         leaving[...] = state
 
+    @pl.when(block != 0)
+    def _():
+        copied(arrived, scaled, sem).wait()
+
     def work(block, limit):
-        fill_gains(
-            early_limit(block, scaled.shape[0]), 0, scaled, gain_high, gain_low, *gained
-        )
+        limit = early_limit(block, size)
+        fill_gains(limit, 0, size, arrived, gain_high, gain_low, *gained)
 
     if early:
         by_block(work, steps)
 
 
-def late_kernel(firsts, steps, _, gain_high, gain_low, *rest):
+def late_kernel(firsts, sizes, steps, _, gain_high, gain_low, *rest):
     count = len(firsts)
-    parts = list(zip(firsts, rest[:count], rest[count:]))
+    parts = list(zip(firsts, sizes, rest[:count], rest[count:]))
 
     def work(block, limit):
-        for i, (first, scaled, gained) in enumerate(parts):
-            begin = 0 if i else early_limit(block, scaled.shape[0])
-            fill_gains(limit, first, scaled, gain_high, gain_low, gained, begin)
+        for i, (first, size, scaled, gained) in enumerate(parts):
+            begin = 0 if i else early_limit(block, size)
+            fill_gains(limit, first, size, scaled, gain_high, gain_low, gained, begin)
 
     by_block(work, steps)
 
@@ -277,12 +276,17 @@
     limit = gain_limit(turn, states.shape[0])
     state = jnp.broadcast_to(entering[0:1, :], parts.shape[1:])
     at = 0
-    for _, own, gained_own, scaled, gained in operands:
-        for k in range(own.shape[0]):
-            pair = (own.at[k], scaled.at[k])
+    for loads, *refs in operands:
+        size = loads.shape[0]
+        early_gains = split(early, size) if at == 0 else []
+        for k, (own, gained_own, other, gained) in enumerate(
+            zip(*[split(ref, size) for ref in refs])
+        ):
+            pair = (own, other)
             if at < limit:
-                other = early if at < early_limit(turn, early.shape[0]) else gained
-                state = advance(state, pair, (gained_own.at[k], other.at[k]), parts)
+                if at < early_limit(turn, len(early_gains)):
+                    gained = early_gains[k]
+                state = advance(state, pair, (gained_own, gained), parts)
             else:
                 state = advance(state, pair, pair, parts, blend)
             states[at : at + 1, :] = state[0:1, :]
@@ -310,9 +314,7 @@
         leaving[...] = jnp.zeros_like(leaving)
 
 
-def last_kernel(turn, count, before, entering, parts, blend, early, *refs):
-    operands, (own_states, predicted, states, readings) = grouped(refs, count)
-    block = lax.axis_index("tm")
+def observation(operands, readings):
     rows = [loads.at[k] for loads, *_ in operands for k in range(loads.shape[0])]
 
     def observe(at, state):
@@ -321,20 +323,41 @@
             product = rows[at][row : row + 8, :] * state
             readings[row : row + 8, at : at + 1] = jnp.sum(product, axis=1, keepdims=True)
 
-    @pl.when(block == turn)
-    def _():
-        chain(turn, entering, parts, blend, operands, early, states, observe)
-
-    @pl.when(block != turn)
-    def _():
-        states[...] = before[...]
-        for at in range(states.shape[0]):
-            observe(at, jnp.broadcast_to(before[at : at + 1, :], parts.shape[1:]))
-
+    return observe
+
+
+def report(states, readings, own_states, predicted):
     share = own_states.shape[1]
     start = pl.multiple_of(lax.axis_index("state") * share, share)
     own_states[...] = states[:, pl.ds(start, share)]
     predicted[...] = readings[...].T[: states.shape[0], :]
+
+
+def finished_kernel(turn, count, states, *refs):
+    loads, (own_states, predicted, readings) = refs[:count], refs[count:]
+
+    @pl.when(lax.axis_index("tm") != turn)
+    def _():
+        observe = observation([(load,) for load in loads], readings)
+        for at in range(states.shape[0]):
+            observe(at, jnp.broadcast_to(states[at : at + 1, :], (8, states.shape[1])))
+        report(states, readings, own_states, predicted)
+
+
+def last_kernel(turn, count, ready_states, ready, entering, parts, blend, early, *refs):
+    operands, (own_states, predicted, states, readings) = grouped(refs, count)
+    block = lax.axis_index("tm")
+
+    @pl.when(block == turn)
+    def _():
+        observe = observation(operands, readings)
+        chain(turn, entering, parts, blend, operands, early, states, observe)
+        report(states, readings, own_states, predicted)
+
+    @pl.when(block != turn)
+    def _():
+        own_states[...] = ready_states[...]
+        predicted[...] = ready[...]
 
 
 def hop_pairs(turn, blocks):
@@ -368,7 +391,7 @@
     sems = pltpu.SemaphoreType.DMA
 
     def matrices(size):
-        return kept(size, outs + 8, width)
+        return kept(size * outs + 8, width)
 
     def chunk(size):
         return [kept(size, outs, width), matrices(size), matrices(size)]
@@ -383,53 +406,43 @@
             pltpu.VMEM(small, observed.dtype),
             pltpu.VMEM(small, F32),
             pltpu.VMEM((1, outs), F32),
-            pltpu.VMEM((128, outs), F32),
+            pltpu.VMEM((-(-2 * steps // 8) * 8, outs), F32),
             sems((sizes[0],)),
             sems((3,)),
         ],
         moved=8 * sizes[0] * outs * width,
     )(loadings, in_hbm(observed), in_hbm(observations), in_hbm(noise_precision[None, :]))
-    *second_chunk, parts, gain_high, gain_low, initial = call(
-        functools.partial(second_kernel, firsts[1], steps),
-        "second_part",
-        chunk(sizes[1]) + [kept(2, 8, width), gain_type, gain_type, vector],
+    parts, gain_high, gain_low, initial, *later = call(
+        functools.partial(rest_kernel, firsts[1:], steps),
+        "rest",
+        [kept(2, 8, width), gain_type, gain_type, vector]
+        + sum([chunk(size) for size in sizes[1:]], []),
         [FAR] + [WHOLE] * 5,
-        [sems((sizes[1],))],
-        moved=8 * sizes[1] * outs * width,
+        [sems((size,)) for size in sizes[1:]],
+        moved=8 * sum(sizes[1:]) * outs * width,
     )(
         loadings, columns, latent_rates[None, :], pair_latent[None, :], blend_matrix,
         initial_mean[None, :],
     )
-    gained_first, *later = call(
-        functools.partial(third_kernel, firsts[2:], steps),
-        "later_parts",
-        [matrices(sizes[0])] + sum([chunk(size) for size in sizes[2:]], []),
-        [FAR] + [WHOLE] * 4,
-        [sems((size,)) for size in sizes[2:]],
-        flops=sizes[0] * half,
-        moved=8 * sum(sizes[2:]) * outs * width,
-    )(loadings, columns, first_chunk[1], gain_high, gain_low)
-    chunks = [first_chunk, second_chunk] + [later[i : i + 3] for i in range(0, len(later), 3)]
+    chunks = [first_chunk] + [later[i : i + 3] for i in range(0, len(later), 3)]
     loads_own, scaled_own, sent = zip(*chunks)
-    gained_own = [gained_first] + list(
-        call(
-            functools.partial(gain_kernel, firsts[1:], steps),
-            "own_gains",
-            [matrices(size) for size in sizes[1:]],
-            [WHOLE] * (1 + count),
-            flops=sum(sizes[1:]) * half,
-        )(gain_high, gain_low, *scaled_own[1:])
-    )
+    gained_own = call(
+        functools.partial(gain_kernel, firsts, sizes, steps),
+        "own_gains",
+        [matrices(size) for size in sizes],
+        [WHOLE] * (2 + count),
+        flops=steps * half,
+    )(gain_high, gain_low, *scaled_own)
 
     leaving = initial
     scaled, states, early = [], [], []
     for i in range(count):
         rows, state, leaving, *gained = call(
-            functools.partial(part_kernel, i == 0, steps),
+            functools.partial(part_kernel, i == 0, sizes[i], steps),
             "other_part",
             [matrices(sizes[i]), kept(sizes[i], width), vector]
             + ([matrices(sizes[i])] if i == 0 else []),
-            [WHOLE, FAR] + [WHOLE] * 5,
+            [WHOLE] * 7,
             [sems],
             flops=sizes[i] * half // 3,
             moved=8 * sizes[i] * outs * width,
@@ -441,7 +454,7 @@
         early += gained
     states = jnp.concatenate(states, axis=0)
     gained = call(
-        functools.partial(late_kernel, firsts, steps),
+        functools.partial(late_kernel, firsts, sizes, steps),
         "late_gains",
         [matrices(size) for size in sizes],
         [FAR] + [WHOLE] * (2 + count),
@@ -463,18 +476,27 @@
                 specs,
                 flops=steps * half,
             )(states, entering, parts, blend_matrix, *operands)
+    last = blocks - 1 if blocks > 1 else -1
+    ready = call(
+        functools.partial(finished_kernel, last, count),
+        "finished",
+        [kept(steps, share), kept(steps, outs)],
+        [WHOLE] * (1 + count),
+        [pltpu.VMEM((outs, 128), F32)],
+        flops=steps * half,
+    )(states, *loads_own)
     return tuple(
         call(
-            functools.partial(last_kernel, blocks - 1 if blocks > 1 else -1, count),
+            functools.partial(last_kernel, last, count),
             "last_chain",
             [
                 jax.ShapeDtypeStruct((steps, share), F32),
                 jax.ShapeDtypeStruct((steps, outs), F32),
             ],
-            specs,
+            [WHOLE] * (5 + len(operands)),
             [pltpu.VMEM((steps, width), F32), pltpu.VMEM((outs, 128), F32)],
             flops=steps * half,
-        )(states, entering, parts, blend_matrix, *operands)
+        )(*ready, entering, parts, blend_matrix, *operands)
     )
 
 

time: 31.4 us -> 30.7 us (0.978)
  Pallas kernels: 20 us -> 19.5 us
  starting transfers between devices: 4.83 us -> 4.38 us
    pallas_call x9, Pallas kernels: 17.9 us -> 17.3 us  [the longest x1 5.34 us: per_device(): call(functools.partial(late_kernel, firsts, sizes, steps), 'late_gains',...]
    ppermute x3, starting transfers between devices: 3.65 us -> 3.26 us  [per_device(): entering = lax.ppermute(leaving, 'tm', hop_pairs(turn, blocks))]
  transfers between devices with their start and end apart: 7 -> 7, of which waited for: 2 -> 3; matrix products, arithmetic and copies ran while one was open for 0% -> 0% of each run, Pallas kernels for 47% -> 47%
where the time goes in v4:
time: 30.7 us; the launch traced here: 30.4 us
  Pallas kernels  19.5 us (64%)
  waiting for transfers between devices  5.69 us (19%)
  starting transfers between devices  4.38 us (14%)
  between operations  0.83 us (3%)
    ppermute x3, waiting for transfers between devices, per_device(): entering = lax.ppermute(leaving, 'tm', hop_pairs(turn, blocks))  5.45 us
    pallas_call x1, Pallas kernels, per_device(): call(functools.partial(late_kernel, firsts, sizes, steps), 'late_gains',...  5.34 us
    pallas_call x1, Pallas kernels, per_device(): call(functools.partial(gain_kernel, firsts, sizes, steps), 'own_gains', [...  5.34 us
    ppermute x3, starting transfers between devices, per_device(): entering = lax.ppermute(leaving, 'tm', hop_pairs(turn, blocks))  3.26 us
    pallas_call x1, Pallas kernels, per_device(): call(functools.partial(last_kernel, last, count), 'last_chain', [jax.Shap...  3.1 us
    pallas_call x1, Pallas kernels, per_device(): call(functools.partial(rest_kernel, firsts[1:], steps), 'rest', [kept(2,...  2.76 us
    pallas_call x1, Pallas kernels, per_device(): call(stage_kernel, 'stage', chunk(sizes[0]) + [kept(outs, 128)], [FAR] *...  2.12 us
    ppermute x4, starting transfers between devices, per_device(): other(sent[i])  1.12 us
  transfers between devices with their start and end apart: 7, of which 3 were waited for; matrix products, arithmetic and copies ran while one was open for 0% of the time, Pallas kernels for 47%

profile of v4, /device:TPU:24, one launch (start us, length us, event | category | flops | bytes accessed | tf_op | source)
XLA Modules:
  0.0 30.4 jit_solution(15594104492885005876)
XLA Ops:
  0.6 0.0 copy-start
  0.6 0.0 copy-start.1
  0.7 0.0 copy-start.2
  0.7 0.0 copy-start.3
  0.7 2.1 %stage.1 = (f32[4,256,512]{2,1,0:T(8,128)S(1)}, f32[1032,512]{1,0:T(8,128)S(1)}, f32[1032,512]{1,0:T(8,128)S(1)}, f32[256,128]{1,0:T(8,128)S(1)}) custom-call(f32[12,256,512]{2,1,0:T(8,128)} %loads_far.3, s32[12,256]{1,0:T(8,128)} %observed_far.1, f32[12,256]{1,0:T(8,128)} %observations_far.1, f32[1,256]{1,0:T(1,128)} %bitcast.7), custom_call_target="tpu_custom_call" | custom-call | bytes 4194304 | tf_op jit(solution)/shard_map/stage/pallas_call | solution.py:400
  2.8 0.1 collective-permute-start
  2.9 0.0 copy-done
  2.9 0.0 copy-done.1
  2.9 0.0 copy-done.2
  2.9 0.0 copy-done.3
  2.9 2.8 %rest.1 = (f32[2,8,512]{2,1,0:T(8,128)S(1)}, bf16[512,512]{1,0:T(8,128)(2,1)S(1)}, bf16[512,512]{1,0:T(8,128)(2,1)S(1)}, f32[8,512]{1,0:T(8,128)S(1)}, f32[4,256...) custom-call(f32[12,256,512]{2,1,0:T(8,128)} %loads_far.3, ...), custom_call_target="tpu_custom_call" | custom-call | bytes 8388608 | tf_op jit(solution)/shard_map/rest/pallas_call | solution.py:415
  5.7 0.5 %collective-permute-start.1 = (f32[1032,512]{1,0:T(8,128)S(1)}, f32[1032,512]{1,0:T(8,128)S(1)}, u32[]{:S(2)}, u32[]{:S(2)}) collective-permute-start(f32[1032,512]{1,0:T(8,128)S(1)} %get-tuple-element.55), channel_id=1, source_target_pairs={{0,1},{1,0},{2,3},{3,2},{4,5},{5,4},{6,7},{7,6},{8,9},{9,8},{10,11... | collective-permute-start | bytes 6340616 | tf_op jit(solution)/shard_map/ppermute | solution.py:450
  6.2 0.1 collective-permute-start.2
  6.3 0.4 %collective-permute-start.3 = (f32[264,512]{1,0:T(8,128)S(1)}, f32[264,512]{1,0:T(8,128)S(1)}, u32[]{:S(2)}, u32[]{:S(2)}) collective-permute-start(f32[264,512]{1,0:T(8,128)S(1)} %get-tuple-element.63), channel_id=1, source_target_pairs={{0,1},{1,0},{2,3},{3,2},{4,5},{5,4},{6,7},{7,6},{8,9},{9,8},{10,11... | collective-permute-start | bytes 1622024 | tf_op jit(solution)/shard_map/ppermute | solution.py:450
  6.7 5.3 %own_gains.1 = (f32[1032,512]{1,0:T(8,128)S(1)}, f32[1032,512]{1,0:T(8,128)S(1)}, f32[776,512]{1,0:T(8,128)S(1)}, f32[264,512]{1,0:T(8,128)S(1)}) custom-call(bf16[512,512]{1,0:T(8,128)(2,1)S(1)} %get-tuple-element.51.gain_high, bf16[512,512]{1,0:T(8,128)(2,1)S(1)} %get-tuple-element.52.gain_low, ...), custom_call_target="tpu_custom_call" | custom-call | flops 4831838208 | tf_op jit(solution)/shard_map/own_gains/pallas_call | solution.py:429
  12.1 0.0 collective-permute-done.arrived
  12.1 0.4 %other_part.4 = (f32[1032,512]{1,0:T(8,128)S(1)}, f32[4,512]{1,0:T(4,128)S(1)}, f32[8,512]{1,0:T(8,128)S(1)}, f32[1032,512]{1,0:T(8,128)S(1)}) custom-call(f32[8,512]{1,0:T(8,128)S(1)} %get-tuple-element.47.entering, f32[1032,512]{1,0:T(8,128)S(1)} %collective-permute-done.arrived, f32[1032,512]{1,0:T(8,128)S(1)} %get-tuple-element.49.scaled_own.rest_0_.refs_1_, ...), custom_call_target="tpu_custom_call" | custom-call | flops 536870912 | bytes 4194304 | tf_op jit(solution)/shard_map/other_part/pallas_call | solution.py:440
  12.5 0.0 collective-permute-done.1.arrived
  12.5 0.2 other_part.5
  12.7 0.0 collective-permute-done.2.arrived
  12.7 0.2 other_part.6
  12.9 0.2 collective-permute-done.3.arrived
  13.1 0.1 other_part.7
  13.2 0.5 %collective-permute-start.4 = (f32[8,512]{1,0:T(8,128)S(1)}, f32[8,512]{1,0:T(8,128)S(1)}, u32[]{:S(2)}, u32[]{:S(2)}) collective-permute-start(f32[8,512]{1,0:T(8,128)S(1)} %get-tuple-element.66._), channel_id=1, source_target_pairs={{0,8},{8,0},{16,24},{24,16},{1,9},{9,1},{17,25},{25,17},{2,10},{10... | collective-permute-start | bytes 49160 | tf_op jit(solution)/shard_map/ppermute | solution.py:470
  13.7 5.3 %late_gains.1 = (f32[1032,512]{1,0:T(8,128)S(1)}, f32[1032,512]{1,0:T(8,128)S(1)}, f32[776,512]{1,0:T(8,128)S(1)}, f32[264,512]{1,0:T(8,128)S(1)}) custom-call(f32[8,512]{1,0:T(8,128)S(1)} %get-tuple-element.66._, bf16[512,512]{1,0:T(8,128)(2,1)S(1)} %get-tuple-element.51.gain_high, bf16[512,512]{1,0:T(8,128)(2,1)S(1)} %get-tuple-element.52.gain_low, ...), custom_call_target="tpu_custom_call" | custom-call | flops 4831838208 | tf_op jit(solution)/shard_map/late_gains/pallas_call | solution.py:456
  19.1 0.0 collective-permute-done.4.entering
  19.1 0.1 collective-permute-start.5
  19.2 3.7 %collective-permute-done.5.entering = f32[8,512]{1,0:T(8,128)S(1)} collective-permute-done((f32[8,512]{1,0:T(8,128)S(1)}, f32[8,512]{1,0:T(8,128)S(1)}, u32[]{:S(2)}, u32[]{:S(2)}) %collective-permute-start.5) | collective-permute-done | bytes 16416 | tf_op jit(solution)/shard_map/ppermute | solution.py:470
  22.9 2.7 %collective-permute-start.6 = (f32[8,512]{1,0:T(8,128)S(1)}, f32[8,512]{1,0:T(8,128)S(1)}, u32[]{:S(2)}, u32[]{:S(2)}) collective-permute-start(f32[8,512]{1,0:T(8,128)S(1)} %get-tuple-element.89), channel_id=1, source_target_pairs={{16,24},{24,16},{0,8},{8,0},{17,25},{25,17},{1,9},{9,1},{18,26},{2... | collective-permute-start | bytes 49160 | tf_op jit(solution)/shard_map/ppermute | solution.py:470
  25.6 1.7 %collective-permute-done.6.entering = f32[8,512]{1,0:T(8,128)S(1)} collective-permute-done((f32[8,512]{1,0:T(8,128)S(1)}, f32[8,512]{1,0:T(8,128)S(1)}, u32[]{:S(2)}, u32[]{:S(2)}) %collective-permute-start.6) | collective-permute-done | bytes 16416 | tf_op jit(solution)/shard_map/ppermute | solution.py:470
  27.3 3.1 %last_chain.1 = (f32[12,128]{1,0:T(8,128)}, f32[12,256]{1,0:T(8,128)}) custom-call(f32[12,128]{1,0:T(8,128)S(1)} %get-tuple-element.87.ready_states, f32[12,256]{1,0:T(8,128)S(1)} %get-tuple-element.88.ready, f32[8,512]{1,0:T(8,128)S(1)} %collective-permute-done.6.entering, f32[2,8,512]{2,1,0:T(8,128)S(1)} %get-tuple-element.50.parts, ...), custom_call_target="tpu_custom_call" | custom-call | flops 4831838208 | tf_op jit(solution)/shard_map/last_chain/pallas_call | solution.py:489
  (4 shorter events, 0.1 us)
Async XLA Ops:
  0.6 2.2 %copy-start = (f32[512,512]{1,0:T(8,128)S(1)}, f32[512,512]{1,0:T(8,128)}, u32[]{:S(2)}) copy-start(f32[512,512]{1,0:T(8,128)} %blend.15) | copy-start | bytes 3145732
  0.6 2.2 %copy-start.1 = (f32[512]{0:T(512)S(1)}, f32[512]{0:T(512)}, u32[]{:S(2)}) copy-start(f32[512]{0:T(512)} %param.15) | copy-start | bytes 6148
  0.7 2.2 %copy-start.2 = (s32[256]{0:T(256)S(1)}, s32[256]{0:T(256)}, u32[]{:S(2)}) copy-start(s32[256]{0:T(256)} %param.14) | copy-start | bytes 3076
  0.7 2.2 %copy-start.3 = (f32[4]{0:T(128)S(1)}, f32[4]{0:T(128)}, u32[]{:S(2)}) copy-start(f32[4]{0:T(128)} %param.13) | copy-start | bytes 52
  2.8 9.3 %collective-permute-start = (f32[1032,512]{1,0:T(8,128)S(1)}, f32[1032,512]{1,0:T(8,128)S(1)}, u32[]{:S(2)}, u32[]{:S(2)}) collective-permute-start(f32[1032,512]{1,0:T(8,128)S(1)} %get-tuple-element.48), channel_id=1, source_target_pairs={{0,1},{1,0},{2,3},{3,2},{4,5},{5,4},{6,7},{7,6},{8,9},{9,8},{10,11... | collective-permute-start | bytes 6340616 | tf_op jit(solution)/shard_map/ppermute | solution.py:450
  5.7 6.8 %collective-permute-start.1 = (f32[1032,512]{1,0:T(8,128)S(1)}, f32[1032,512]{1,0:T(8,128)S(1)}, u32[]{:S(2)}, u32[]{:S(2)}) collective-permute-start(f32[1032,512]{1,0:T(8,128)S(1)} %get-tuple-element.55), channel_id=1, source_target_pairs={{0,1},{1,0},{2,3},{3,2},{4,5},{5,4},{6,7},{7,6},{8,9},{9,8},{10,11... | collective-permute-start | bytes 6340616 | tf_op jit(solution)/shard_map/ppermute | solution.py:450
  6.2 6.5 %collective-permute-start.2 = (f32[776,512]{1,0:T(8,128)S(1)}, f32[776,512]{1,0:T(8,128)S(1)}, u32[]{:S(2)}, u32[]{:S(2)}) collective-permute-start(f32[776,512]{1,0:T(8,128)S(1)} %get-tuple-element.59), channel_id=1, source_target_pairs={{0,1},{1,0},{2,3},{3,2},{4,5},{5,4},{6,7},{7,6},{8,9},{9,8},{10,11... | collective-permute-start | bytes 4767752 | tf_op jit(solution)/shard_map/ppermute | solution.py:450
  6.3 6.8 %collective-permute-start.3 = (f32[264,512]{1,0:T(8,128)S(1)}, f32[264,512]{1,0:T(8,128)S(1)}, u32[]{:S(2)}, u32[]{:S(2)}) collective-permute-start(f32[264,512]{1,0:T(8,128)S(1)} %get-tuple-element.63), channel_id=1, source_target_pairs={{0,1},{1,0},{2,3},{3,2},{4,5},{5,4},{6,7},{7,6},{8,9},{9,8},{10,11... | collective-permute-start | bytes 1622024 | tf_op jit(solution)/shard_map/ppermute | solution.py:450
  13.2 5.9 %collective-permute-start.4 = (f32[8,512]{1,0:T(8,128)S(1)}, f32[8,512]{1,0:T(8,128)S(1)}, u32[]{:S(2)}, u32[]{:S(2)}) collective-permute-start(f32[8,512]{1,0:T(8,128)S(1)} %get-tuple-element.66._), channel_id=1, source_target_pairs={{0,8},{8,0},{16,24},{24,16},{1,9},{9,1},{17,25},{25,17},{2,10},{10... | collective-permute-start | bytes 49160 | tf_op jit(solution)/shard_map/ppermute | solution.py:470
  19.1 3.8 %collective-permute-start.5 = (f32[8,512]{1,0:T(8,128)S(1)}, f32[8,512]{1,0:T(8,128)S(1)}, u32[]{:S(2)}, u32[]{:S(2)}) collective-permute-start(f32[8,512]{1,0:T(8,128)S(1)} %get-tuple-element.85), channel_id=1, source_target_pairs={{0,8},{8,16},{16,24},{24,0},{1,9},{9,17},{17,25},{25,1},{2,10},{10... | collective-permute-start | bytes 49160 | tf_op jit(solution)/shard_map/ppermute | solution.py:470
  22.9 4.4 %collective-permute-start.6 = (f32[8,512]{1,0:T(8,128)S(1)}, f32[8,512]{1,0:T(8,128)S(1)}, u32[]{:S(2)}, u32[]{:S(2)}) collective-permute-start(f32[8,512]{1,0:T(8,128)S(1)} %get-tuple-element.89), channel_id=1, source_target_pairs={{16,24},{24,16},{0,8},{8,0},{17,25},{25,17},{1,9},{9,1},{18,26},{2... | collective-permute-start | bytes 49160 | tf_op jit(solution)/shard_map/ppermute | solution.py:470

commit v5 on v4

--- a/solution.py
+++ b/solution.py
@@ -11,18 +11,19 @@
 VMEM_LIMIT = 8 * 2**20
 LAST_PART = 1
 PARTS = 4
-GAIN_STEPS = (0, 7, 9)
-EARLY_STEPS = (0, 2, 2, 0)
+GAIN_STEPS = (0, 8, 10)
+EARLY_STEPS = (0, 4, 2, 0)
 WHOLE = pl.BlockSpec(memory_space=pltpu.VMEM)
 FAR = pl.BlockSpec(memory_space=pl.ANY)
 
 
-def call(kernel, name, outs, in_specs, scratch=(), flops=0, moved=0):
+def call(kernel, name, outs, in_specs, scratch=(), flops=0, moved=0, out_spec=WHOLE, aliases=()):
     return pl.pallas_call(
         kernel,
         out_shape=outs,
         in_specs=in_specs,
-        out_specs=[WHOLE] * len(outs),
+        out_specs=[out_spec] * len(outs),
+        input_output_aliases=dict(aliases),
         scratch_shapes=scratch,
         compiler_params=pltpu.CompilerParams(vmem_limit_bytes=VMEM_LIMIT),
         cost_estimate=pl.CostEstimate(flops=flops, bytes_accessed=moved, transcendentals=0),
@@ -155,14 +156,19 @@
 
 
 def fill_gains(limit, first, size, scaled, gain_high, gain_low, gained, begin=0):
-    tails = scaled[scaled.shape[0] - 8 :, :]
     sources, targets = split(scaled, size), split(gained, size)
-    for k in range(begin, min(size, limit - first)):
-        rows = jnp.concatenate([sources[k][0][...], tails, tails], axis=0)
+    end = min(size, limit - first)
+    for k in range(begin, end):
+        rows = sources[k][0][...]
+        outs = rows.shape[0]
+        if k == begin:
+            tails = scaled[scaled.shape[0] - 8 :, :]
+            rows = jnp.concatenate([rows, tails, tails], axis=0)
         rows = times_gain(rows, gain_high[...], gain_low[...])
-        outs = rows.shape[0] - 16
         targets[k][0][...] = rows[:outs]
-        targets[k][1][...] = rows[outs + k : outs + k + 1]
+        if k == begin:
+            for j in range(begin, end):
+                targets[j][1][...] = rows[outs + j : outs + j + 1]
 
 
 def rest_kernel(
@@ -209,25 +215,32 @@
     )
     turned = []
     for start in range(0, state.shape[1], 128):
-        total = jnp.zeros((8, 128), F32)
+        totals = [jnp.zeros((8, 128), F32) for _ in range(2)]
         for row in range(0, 128, 8):
             blended = blend[start + row : start + row + 8, :] * pull
-            total = total + jnp.where(
+            i = row // 8 % len(totals)
+            totals[i] = totals[i] + jnp.where(
                 place == row, jnp.sum(blended, axis=1, keepdims=True), 0.0
             )
-        turned.append(jnp.sum(total, axis=0, keepdims=True))
+        turned.append(jnp.sum(sum(totals[1:], totals[0]), axis=0, keepdims=True))
     return state - jnp.concatenate(turned, axis=1)
 
 
-def advance(state, scaled, gained, parts, blend=None):
-    pull = 0.0
-    for (rows, _), (gains, shift) in zip(scaled, gained):
-        total = jnp.zeros_like(state)
+def advance(state, scaled, gained, parts, blend=None, beside=None):
+    sides = []
+    for (rows, _), (gains, _) in zip(scaled, gained):
+        totals = [jnp.zeros_like(state), jnp.zeros_like(state)]
         for row in range(0, rows.shape[0], 8):
             block = rows[row : row + 8, :]
             reading = jnp.sum(block * state, axis=1, keepdims=True)
-            total = total + reading * (block if blend is not None else gains[row : row + 8, :])
-        pull += jnp.sum(total, axis=0, keepdims=True) - shift[...]
+            if blend is None:
+                block = gains[row : row + 8, :]
+            totals[row // 8 % 2] = totals[row // 8 % 2] + reading * block
+            if beside is not None and not sides:
+                beside(row)
+        sides.append(totals[0] + totals[1])
+    pull = jnp.sum(sides[0] + sides[1], axis=0, keepdims=True)
+    pull = pull - (gained[0][1][...] + gained[1][1][...])
     if blend is not None:
         state, pull = reflected(state, pull, blend), 0.0
     return state * parts[0] + swap_pairs(state) * parts[1] - pull
@@ -283,16 +296,20 @@
             zip(*[split(ref, size) for ref in refs])
         ):
             pair = (own, other)
+            beside = None
+            if observe is not None and at > 0:
+                beside = functools.partial(observe, at - 1, state)
             if at < limit:
                 if at < early_limit(turn, len(early_gains)):
                     gained = early_gains[k]
-                state = advance(state, pair, (gained_own, gained), parts)
+                state = advance(state, pair, (gained_own, gained), parts, beside=beside)
             else:
-                state = advance(state, pair, pair, parts, blend)
+                state = advance(state, pair, pair, parts, blend, beside)
             states[at : at + 1, :] = state[0:1, :]
-            if observe is not None:
-                observe(at, state)
             at += 1
+    if observe is not None:
+        for row in range(0, operands[0][0].shape[1], 8):
+            observe(at - 1, state, row)
     return state
 
 
@@ -314,50 +331,58 @@
         leaving[...] = jnp.zeros_like(leaving)
 
 
-def observation(operands, readings):
+def observation(operands, predicted):
     rows = [loads.at[k] for loads, *_ in operands for k in range(loads.shape[0])]
-
-    def observe(at, state):
-        outs = rows[at].shape[0]
-        for row in range(0, outs, 8):
-            product = rows[at][row : row + 8, :] * state
-            readings[row : row + 8, at : at + 1] = jnp.sum(product, axis=1, keepdims=True)
+    place = lax.broadcasted_iota(jnp.int32, (8, 128), 1) - lax.broadcasted_iota(
+        jnp.int32, (8, 128), 0
+    )
+    outs = predicted.shape[1]
+    totals = {}
+
+    def observe(at, state, row):
+        reading = jnp.sum(rows[at][row : row + 8, :] * state, axis=1, keepdims=True)
+        kept_rows = jnp.where(place == row % 128, reading, 0.0)
+        key = (at, row // 128)
+        totals[key] = totals[key] + kept_rows if key in totals else kept_rows
+        if row == outs - 8:
+            for start in range(0, outs, 128):
+                total = jnp.sum(totals[(at, start // 128)], axis=0, keepdims=True)
+                predicted[at : at + 1, start : start + 128] = total
 
     return observe
 
 
-def report(states, readings, own_states, predicted):
-    share = own_states.shape[1]
+def own_share(states, share):
     start = pl.multiple_of(lax.axis_index("state") * share, share)
-    own_states[...] = states[:, pl.ds(start, share)]
-    predicted[...] = readings[...].T[: states.shape[0], :]
+    return states[:, pl.ds(start, share)]
 
 
 def finished_kernel(turn, count, states, *refs):
-    loads, (own_states, predicted, readings) = refs[:count], refs[count:]
+    loads, (own_states, predicted) = refs[:count], refs[count:]
 
     @pl.when(lax.axis_index("tm") != turn)
     def _():
-        observe = observation([(load,) for load in loads], readings)
+        observe = observation([(load,) for load in loads], predicted)
         for at in range(states.shape[0]):
-            observe(at, jnp.broadcast_to(states[at : at + 1, :], (8, states.shape[1])))
-        report(states, readings, own_states, predicted)
+            state = jnp.broadcast_to(states[at : at + 1, :], (8, states.shape[1]))
+            for row in range(0, loads[0].shape[1], 8):
+                observe(at, state, row)
+        own_states[...] = own_share(states, own_states.shape[1])
 
 
 def last_kernel(turn, count, ready_states, ready, entering, parts, blend, early, *refs):
-    operands, (own_states, predicted, states, readings) = grouped(refs, count)
-    block = lax.axis_index("tm")
-
-    @pl.when(block == turn)
-    def _():
-        observe = observation(operands, readings)
+    operands, rest = grouped(refs, count)
+    own_far, predicted_far, own_states, predicted, states, sems = rest
+
+    @pl.when(lax.axis_index("tm") == turn)
+    def _():
+        observe = observation(operands, predicted)
         chain(turn, entering, parts, blend, operands, early, states, observe)
-        report(states, readings, own_states, predicted)
-
-    @pl.when(block != turn)
-    def _():
-        own_states[...] = ready_states[...]
-        predicted[...] = ready[...]
+        own_states[...] = own_share(states, own_states.shape[1])
+        first = copied(own_states, own_far, sems.at[0])
+        second = copied(predicted, predicted_far, sems.at[1])
+        first.wait()
+        second.wait()
 
 
 def hop_pairs(turn, blocks):
@@ -477,25 +502,32 @@
                 flops=steps * half,
             )(states, entering, parts, blend_matrix, *operands)
     last = blocks - 1 if blocks > 1 else -1
+    outputs = [
+        jax.ShapeDtypeStruct((steps, share), F32),
+        jax.ShapeDtypeStruct((steps, outs), F32),
+    ]
     ready = call(
         functools.partial(finished_kernel, last, count),
         "finished",
-        [kept(steps, share), kept(steps, outs)],
+        outputs,
         [WHOLE] * (1 + count),
-        [pltpu.VMEM((outs, 128), F32)],
         flops=steps * half,
     )(states, *loads_own)
     return tuple(
         call(
             functools.partial(last_kernel, last, count),
             "last_chain",
+            outputs,
+            [FAR] * 2 + [WHOLE] * (3 + len(operands)),
             [
-                jax.ShapeDtypeStruct((steps, share), F32),
-                jax.ShapeDtypeStruct((steps, outs), F32),
+                pltpu.VMEM((steps, share), F32),
+                pltpu.VMEM((steps, outs), F32),
+                pltpu.VMEM((steps, width), F32),
+                sems((2,)),
             ],
-            [WHOLE] * (5 + len(operands)),
-            [pltpu.VMEM((steps, width), F32), pltpu.VMEM((outs, 128), F32)],
             flops=steps * half,
+            out_spec=FAR,
+            aliases=((0, 0), (1, 1)),
         )(*ready, entering, parts, blend_matrix, *operands)
     )
 

time: 30.7 us -> 30.4 us (level)
  waiting for transfers between devices: 5.69 us -> 5.29 us
    ppermute x3, waiting for transfers between devices: 5.45 us -> 4.84 us  [per_device(): entering = lax.ppermute(leaving, 'tm', hop_pairs(turn, blocks))]
    pallas_call x2, Pallas kernels: 3.11 us -> 3.66 us  [the longest x1 3.05 us: per_device(): call(functools.partial(last_kernel, last, count), 'last_chain', outputs,...]
where the time goes in v5:
time: 30.4 us; the launch traced here: 30.3 us
  Pallas kernels  19.6 us (64%)
  waiting for transfers between devices  5.29 us (17%)
  starting transfers between devices  4.3 us (14%)
  between operations  1.01 us (3%)
    pallas_call x1, Pallas kernels, per_device(): call(functools.partial(late_kernel, firsts, sizes, steps), 'late_gains',...  5.14 us
    pallas_call x1, Pallas kernels, per_device(): call(functools.partial(gain_kernel, firsts, sizes, steps), 'own_gains', [...  5.13 us
    ppermute x3, waiting for transfers between devices, per_device(): entering = lax.ppermute(leaving, 'tm', hop_pairs(turn, blocks))  4.84 us
    ppermute x3, starting transfers between devices, per_device(): entering = lax.ppermute(leaving, 'tm', hop_pairs(turn, blocks))  3.19 us
    pallas_call x1, Pallas kernels, per_device(): call(functools.partial(last_kernel, last, count), 'last_chain', outputs,...  3.05 us
    pallas_call x1, Pallas kernels, per_device(): call(functools.partial(rest_kernel, firsts[1:], steps), 'rest', [kept(2,...  2.76 us
    pallas_call x1, Pallas kernels, per_device(): call(stage_kernel, 'stage', chunk(sizes[0]) + [kept(outs, 128)], [FAR] *...  2.12 us
    ppermute x4, starting transfers between devices, per_device(): other(sent[i])  1.12 us
  transfers between devices with their start and end apart: 7, of which 3 were waited for; matrix products, arithmetic and copies ran while one was open for 0% of the time, Pallas kernels for 47%

profile of v5, /device:TPU:24, one launch (start us, length us, event | category | flops | bytes accessed | tf_op | source)
XLA Modules:
  0.0 30.3 jit_solution(9521218383356338356)
XLA Ops:
  0.6 0.0 copy-start
  0.6 0.0 copy-start.1
  0.7 0.0 copy-start.2
  0.7 0.0 copy-start.3
  0.7 2.1 %stage.1 = (f32[4,256,512]{2,1,0:T(8,128)S(1)}, f32[1032,512]{1,0:T(8,128)S(1)}, f32[1032,512]{1,0:T(8,128)S(1)}, f32[256,128]{1,0:T(8,128)S(1)}) custom-call(f32[12,256,512]{2,1,0:T(8,128)} %loads_far.3, s32[12,256]{1,0:T(8,128)} %observed_far.1, f32[12,256]{1,0:T(8,128)} %observations_far.1, f32[1,256]{1,0:T(1,128)} %bitcast.7), custom_call_target="tpu_custom_call" | custom-call | bytes 4194304 | tf_op jit(solution)/shard_map/stage/pallas_call | solution.py:425
  2.8 0.1 collective-permute-start
  2.9 0.0 copy-done
  2.9 0.0 copy-done.1
  2.9 0.0 copy-done.2
  2.9 0.0 copy-done.3
  2.9 2.8 %rest.1 = (f32[2,8,512]{2,1,0:T(8,128)S(1)}, bf16[512,512]{1,0:T(8,128)(2,1)S(1)}, bf16[512,512]{1,0:T(8,128)(2,1)S(1)}, f32[8,512]{1,0:T(8,128)S(1)}, f32[4,256...) custom-call(f32[12,256,512]{2,1,0:T(8,128)} %loads_far.3, ...), custom_call_target="tpu_custom_call" | custom-call | bytes 8388608 | tf_op jit(solution)/shard_map/rest/pallas_call | solution.py:440
  5.7 0.5 %collective-permute-start.1 = (f32[1032,512]{1,0:T(8,128)S(1)}, f32[1032,512]{1,0:T(8,128)S(1)}, u32[]{:S(2)}, u32[]{:S(2)}) collective-permute-start(f32[1032,512]{1,0:T(8,128)S(1)} %get-tuple-element.55), channel_id=1, source_target_pairs={{0,1},{1,0},{2,3},{3,2},{4,5},{5,4},{6,7},{7,6},{8,9},{9,8},{10,11... | collective-permute-start | bytes 6340616 | tf_op jit(solution)/shard_map/ppermute | solution.py:475
  6.2 0.1 collective-permute-start.2
  6.3 0.4 %collective-permute-start.3 = (f32[264,512]{1,0:T(8,128)S(1)}, f32[264,512]{1,0:T(8,128)S(1)}, u32[]{:S(2)}, u32[]{:S(2)}) collective-permute-start(f32[264,512]{1,0:T(8,128)S(1)} %get-tuple-element.63), channel_id=1, source_target_pairs={{0,1},{1,0},{2,3},{3,2},{4,5},{5,4},{6,7},{7,6},{8,9},{9,8},{10,11... | collective-permute-start | bytes 1622024 | tf_op jit(solution)/shard_map/ppermute | solution.py:475
  6.7 5.1 %own_gains.1 = (f32[1032,512]{1,0:T(8,128)S(1)}, f32[1032,512]{1,0:T(8,128)S(1)}, f32[776,512]{1,0:T(8,128)S(1)}, f32[264,512]{1,0:T(8,128)S(1)}) custom-call(bf16[512,512]{1,0:T(8,128)(2,1)S(1)} %get-tuple-element.51.gain_high, bf16[512,512]{1,0:T(8,128)(2,1)S(1)} %get-tuple-element.52.gain_low, ...), custom_call_target="tpu_custom_call" | custom-call | flops 4831838208 | tf_op jit(solution)/shard_map/own_gains/pallas_call | solution.py:454
  11.9 0.0 collective-permute-done.arrived
  11.9 0.4 %other_part.4 = (f32[1032,512]{1,0:T(8,128)S(1)}, f32[4,512]{1,0:T(4,128)S(1)}, f32[8,512]{1,0:T(8,128)S(1)}, f32[1032,512]{1,0:T(8,128)S(1)}) custom-call(f32[8,512]{1,0:T(8,128)S(1)} %get-tuple-element.47.entering, f32[1032,512]{1,0:T(8,128)S(1)} %collective-permute-done.arrived, f32[1032,512]{1,0:T(8,128)S(1)} %get-tuple-element.49.scaled_own.rest_0_.refs_1_, ...), custom_call_target="tpu_custom_call" | custom-call | flops 536870912 | bytes 4194304 | tf_op jit(solution)/shard_map/other_part/pallas_call | solution.py:465
  12.3 0.0 collective-permute-done.1.arrived
  12.3 0.2 other_part.5
  12.5 0.0 collective-permute-done.2.arrived
  12.5 0.2 other_part.6
  12.7 0.4 %collective-permute-done.3.arrived = f32[264,512]{1,0:T(8,128)S(1)} collective-permute-done((f32[264,512]{1,0:T(8,128)S(1)}, f32[264,512]{1,0:T(8,128)S(1)}, u32[]{:S(2)}, u32[]{:S(2)}) %collective-permute-start.3) | collective-permute-done | bytes 540704 | tf_op jit(solution)/shard_map/ppermute | solution.py:475
  13.1 0.1 other_part.7
  13.2 0.5 %collective-permute-start.4 = (f32[8,512]{1,0:T(8,128)S(1)}, f32[8,512]{1,0:T(8,128)S(1)}, u32[]{:S(2)}, u32[]{:S(2)}) collective-permute-start(f32[8,512]{1,0:T(8,128)S(1)} %get-tuple-element.66._), channel_id=1, source_target_pairs={{0,8},{8,0},{16,24},{24,16},{1,9},{9,1},{17,25},{25,17},{2,10},{10... | collective-permute-start | bytes 49160 | tf_op jit(solution)/shard_map/ppermute | solution.py:495
  13.7 5.1 %late_gains.1 = (f32[1032,512]{1,0:T(8,128)S(1)}, f32[1032,512]{1,0:T(8,128)S(1)}, f32[776,512]{1,0:T(8,128)S(1)}, f32[264,512]{1,0:T(8,128)S(1)}) custom-call(f32[8,512]{1,0:T(8,128)S(1)} %get-tuple-element.66._, bf16[512,512]{1,0:T(8,128)(2,1)S(1)} %get-tuple-element.51.gain_high, bf16[512,512]{1,0:T(8,128)(2,1)S(1)} %get-tuple-element.52.gain_low, ...), custom_call_target="tpu_custom_call" | custom-call | flops 4831838208 | tf_op jit(solution)/shard_map/late_gains/pallas_call | solution.py:481
  18.9 0.0 collective-permute-done.4.entering
  18.9 0.1 collective-permute-start.5
  19.0 3.7 %collective-permute-done.5.entering = f32[8,512]{1,0:T(8,128)S(1)} collective-permute-done((f32[8,512]{1,0:T(8,128)S(1)}, f32[8,512]{1,0:T(8,128)S(1)}, u32[]{:S(2)}, u32[]{:S(2)}) %collective-permute-start.5) | collective-permute-done | bytes 16416 | tf_op jit(solution)/shard_map/ppermute | solution.py:495
  22.7 2.6 %collective-permute-start.6 = (f32[8,512]{1,0:T(8,128)S(1)}, f32[8,512]{1,0:T(8,128)S(1)}, u32[]{:S(2)}, u32[]{:S(2)}) collective-permute-start(f32[8,512]{1,0:T(8,128)S(1)} %get-tuple-element.89), channel_id=1, source_target_pairs={{16,24},{24,16},{0,8},{8,0},{17,25},{25,17},{1,9},{9,1},{18,26},{2... | collective-permute-start | bytes 49160 | tf_op jit(solution)/shard_map/ppermute | solution.py:495
  25.3 0.6 %finished.1 = (f32[12,128]{1,0:T(8,128)}, f32[12,256]{1,0:T(8,128)}) custom-call(f32[12,512]{1,0:T(8,128)S(1)} %get-tuple-element.86.states, f32[4,256,512]{2,1,0:T(8,128)S(1)} %get-tuple-element.68.refs_0_, f32[4,256,512]{2,1,0:T(8,128)S(1)} %get-tuple-element.75.refs_5_.refs_1_, f32[3,256,512]{2,1,0:T(8,128)S(1)} %get-tuple-element.78.refs_10_.refs_2_, ...), custom_call_target="tpu_custom_call" | custom-call | flops 4831838208 | tf_op jit(solution)/shard_map/finished/pallas_call | solution.py:509
  25.9 1.1 %collective-permute-done.6.entering = f32[8,512]{1,0:T(8,128)S(1)} collective-permute-done((f32[8,512]{1,0:T(8,128)S(1)}, f32[8,512]{1,0:T(8,128)S(1)}, u32[]{:S(2)}, u32[]{:S(2)}) %collective-permute-start.6) | collective-permute-done | bytes 16416 | tf_op jit(solution)/shard_map/ppermute | solution.py:495
  27.1 3.0 %last_chain.1 = (f32[12,128]{1,0:T(8,128)}, f32[12,256]{1,0:T(8,128)}) custom-call(f32[12,128]{1,0:T(8,128)} %get-tuple-element.87.ready_states, f32[12,256]{1,0:T(8,128)} %get-tuple-element.88.ready, f32[8,512]{1,0:T(8,128)S(1)} %collective-permute-done.6.entering, ...), custom_call_target="tpu_custom_call", output_to_operand_aliasing={{0}: (0, {}), {1}: (1, {})} | custom-call | flops 4831838208 | tf_op jit(solution)/shard_map/last_chain/pallas_call | solution.py:517
  (3 shorter events, 0.0 us)
Async XLA Ops:
  0.6 2.2 %copy-start = (f32[512,512]{1,0:T(8,128)S(1)}, f32[512,512]{1,0:T(8,128)}, u32[]{:S(2)}) copy-start(f32[512,512]{1,0:T(8,128)} %blend.15) | copy-start | bytes 3145732
  0.6 2.2 %copy-start.1 = (f32[512]{0:T(512)S(1)}, f32[512]{0:T(512)}, u32[]{:S(2)}) copy-start(f32[512]{0:T(512)} %param.15) | copy-start | bytes 6148
  0.7 2.2 %copy-start.2 = (s32[256]{0:T(256)S(1)}, s32[256]{0:T(256)}, u32[]{:S(2)}) copy-start(s32[256]{0:T(256)} %param.14) | copy-start | bytes 3076
  0.7 2.2 %copy-start.3 = (f32[4]{0:T(128)S(1)}, f32[4]{0:T(128)}, u32[]{:S(2)}) copy-start(f32[4]{0:T(128)} %param.13) | copy-start | bytes 52
  2.8 9.1 %collective-permute-start = (f32[1032,512]{1,0:T(8,128)S(1)}, f32[1032,512]{1,0:T(8,128)S(1)}, u32[]{:S(2)}, u32[]{:S(2)}) collective-permute-start(f32[1032,512]{1,0:T(8,128)S(1)} %get-tuple-element.48), channel_id=1, source_target_pairs={{0,1},{1,0},{2,3},{3,2},{4,5},{5,4},{6,7},{7,6},{8,9},{9,8},{10,11... | collective-permute-start | bytes 6340616 | tf_op jit(solution)/shard_map/ppermute | solution.py:475
  5.7 6.6 %collective-permute-start.1 = (f32[1032,512]{1,0:T(8,128)S(1)}, f32[1032,512]{1,0:T(8,128)S(1)}, u32[]{:S(2)}, u32[]{:S(2)}) collective-permute-start(f32[1032,512]{1,0:T(8,128)S(1)} %get-tuple-element.55), channel_id=1, source_target_pairs={{0,1},{1,0},{2,3},{3,2},{4,5},{5,4},{6,7},{7,6},{8,9},{9,8},{10,11... | collective-permute-start | bytes 6340616 | tf_op jit(solution)/shard_map/ppermute | solution.py:475
  6.2 6.3 %collective-permute-start.2 = (f32[776,512]{1,0:T(8,128)S(1)}, f32[776,512]{1,0:T(8,128)S(1)}, u32[]{:S(2)}, u32[]{:S(2)}) collective-permute-start(f32[776,512]{1,0:T(8,128)S(1)} %get-tuple-element.59), channel_id=1, source_target_pairs={{0,1},{1,0},{2,3},{3,2},{4,5},{5,4},{6,7},{7,6},{8,9},{9,8},{10,11... | collective-permute-start | bytes 4767752 | tf_op jit(solution)/shard_map/ppermute | solution.py:475
  6.3 6.8 %collective-permute-start.3 = (f32[264,512]{1,0:T(8,128)S(1)}, f32[264,512]{1,0:T(8,128)S(1)}, u32[]{:S(2)}, u32[]{:S(2)}) collective-permute-start(f32[264,512]{1,0:T(8,128)S(1)} %get-tuple-element.63), channel_id=1, source_target_pairs={{0,1},{1,0},{2,3},{3,2},{4,5},{5,4},{6,7},{7,6},{8,9},{9,8},{10,11... | collective-permute-start | bytes 1622024 | tf_op jit(solution)/shard_map/ppermute | solution.py:475
  13.2 5.7 %collective-permute-start.4 = (f32[8,512]{1,0:T(8,128)S(1)}, f32[8,512]{1,0:T(8,128)S(1)}, u32[]{:S(2)}, u32[]{:S(2)}) collective-permute-start(f32[8,512]{1,0:T(8,128)S(1)} %get-tuple-element.66._), channel_id=1, source_target_pairs={{0,8},{8,0},{16,24},{24,16},{1,9},{9,1},{17,25},{25,17},{2,10},{10... | collective-permute-start | bytes 49160 | tf_op jit(solution)/shard_map/ppermute | solution.py:495
  18.9 3.8 %collective-permute-start.5 = (f32[8,512]{1,0:T(8,128)S(1)}, f32[8,512]{1,0:T(8,128)S(1)}, u32[]{:S(2)}, u32[]{:S(2)}) collective-permute-start(f32[8,512]{1,0:T(8,128)S(1)} %get-tuple-element.85), channel_id=1, source_target_pairs={{0,8},{8,16},{16,24},{24,0},{1,9},{9,17},{17,25},{25,1},{2,10},{10... | collective-permute-start | bytes 49160 | tf_op jit(solution)/shard_map/ppermute | solution.py:495
  22.7 4.3 %collective-permute-start.6 = (f32[8,512]{1,0:T(8,128)S(1)}, f32[8,512]{1,0:T(8,128)S(1)}, u32[]{:S(2)}, u32[]{:S(2)}) collective-permute-start(f32[8,512]{1,0:T(8,128)S(1)} %get-tuple-element.89), channel_id=1, source_target_pairs={{16,24},{24,16},{0,8},{8,0},{17,25},{25,17},{1,9},{9,1},{18,26},{2... | collective-permute-start | bytes 49160 | tf_op jit(solution)/shard_map/ppermute | solution.py:495

commit v6 on v5

--- a/solution.py
+++ b/solution.py
@@ -12,7 +12,7 @@
 LAST_PART = 1
 PARTS = 4
 GAIN_STEPS = (0, 8, 10)
-EARLY_STEPS = (0, 4, 2, 0)
+EARLY_STEPS = (0, 4, 3, 0)
 WHOLE = pl.BlockSpec(memory_space=pltpu.VMEM)
 FAR = pl.BlockSpec(memory_space=pl.ANY)
 

time: 30.4 us -> 30.2 us (level)
  transfers between devices with their start and end apart: 7 -> 7, of which waited for: 3 -> 3; matrix products, arithmetic and copies ran while one was open for 0% -> 0% of each run, Pallas kernels for 47% -> 48%
where the time goes in v6:
time: 30.2 us; the launch traced here: 30 us
  Pallas kernels  19.6 us (65%)
  waiting for transfers between devices  5.29 us (18%)
  starting transfers between devices  4.06 us (13%)
  between operations  1.01 us (3%)
    pallas_call x1, Pallas kernels, per_device(): call(functools.partial(late_kernel, firsts, sizes, steps), 'late_gains',...  5.13 us
    pallas_call x1, Pallas kernels, per_device(): call(functools.partial(gain_kernel, firsts, sizes, steps), 'own_gains', [...  5.13 us
    ppermute x3, waiting for transfers between devices, per_device(): entering = lax.ppermute(leaving, 'tm', hop_pairs(turn, blocks))  4.84 us
    pallas_call x1, Pallas kernels, per_device(): call(functools.partial(last_kernel, last, count), 'last_chain', outputs,...  3.05 us
    ppermute x3, starting transfers between devices, per_device(): entering = lax.ppermute(leaving, 'tm', hop_pairs(turn, blocks))  2.94 us
    pallas_call x1, Pallas kernels, per_device(): call(functools.partial(rest_kernel, firsts[1:], steps), 'rest', [kept(2,...  2.76 us
    pallas_call x1, Pallas kernels, per_device(): call(stage_kernel, 'stage', chunk(sizes[0]) + [kept(outs, 128)], [FAR] *...  2.12 us
    ppermute x4, starting transfers between devices, per_device(): other(sent[i])  1.12 us
  transfers between devices with their start and end apart: 7, of which 3 were waited for; matrix products, arithmetic and copies ran while one was open for 0% of the time, Pallas kernels for 48%

profile of v6, /device:TPU:24, one launch (start us, length us, event | category | flops | bytes accessed | tf_op | source)
XLA Modules:
  0.0 30.0 jit_solution(15374503474129512169)
XLA Ops:
  0.6 0.0 copy-start
  0.6 0.0 copy-start.1
  0.7 0.0 copy-start.2
  0.7 0.0 copy-start.3
  0.7 2.1 %stage.1 = (f32[4,256,512]{2,1,0:T(8,128)S(1)}, f32[1032,512]{1,0:T(8,128)S(1)}, f32[1032,512]{1,0:T(8,128)S(1)}, f32[256,128]{1,0:T(8,128)S(1)}) custom-call(f32[12,256,512]{2,1,0:T(8,128)} %loads_far.3, s32[12,256]{1,0:T(8,128)} %observed_far.1, f32[12,256]{1,0:T(8,128)} %observations_far.1, f32[1,256]{1,0:T(1,128)} %bitcast.7), custom_call_target="tpu_custom_call" | custom-call | bytes 4194304 | tf_op jit(solution)/shard_map/stage/pallas_call | solution.py:425
  2.8 0.1 collective-permute-start
  2.9 0.0 copy-done
  2.9 0.0 copy-done.1
  2.9 0.0 copy-done.2
  2.9 0.0 copy-done.3
  2.9 2.8 %rest.1 = (f32[2,8,512]{2,1,0:T(8,128)S(1)}, bf16[512,512]{1,0:T(8,128)(2,1)S(1)}, bf16[512,512]{1,0:T(8,128)(2,1)S(1)}, f32[8,512]{1,0:T(8,128)S(1)}, f32[4,256...) custom-call(f32[12,256,512]{2,1,0:T(8,128)} %loads_far.3, ...), custom_call_target="tpu_custom_call" | custom-call | bytes 8388608 | tf_op jit(solution)/shard_map/rest/pallas_call | solution.py:440
  5.7 0.5 %collective-permute-start.1 = (f32[1032,512]{1,0:T(8,128)S(1)}, f32[1032,512]{1,0:T(8,128)S(1)}, u32[]{:S(2)}, u32[]{:S(2)}) collective-permute-start(f32[1032,512]{1,0:T(8,128)S(1)} %get-tuple-element.55), channel_id=1, source_target_pairs={{0,1},{1,0},{2,3},{3,2},{4,5},{5,4},{6,7},{7,6},{8,9},{9,8},{10,11... | collective-permute-start | bytes 6340616 | tf_op jit(solution)/shard_map/ppermute | solution.py:475
  6.2 0.1 collective-permute-start.2
  6.3 0.4 %collective-permute-start.3 = (f32[264,512]{1,0:T(8,128)S(1)}, f32[264,512]{1,0:T(8,128)S(1)}, u32[]{:S(2)}, u32[]{:S(2)}) collective-permute-start(f32[264,512]{1,0:T(8,128)S(1)} %get-tuple-element.63), channel_id=1, source_target_pairs={{0,1},{1,0},{2,3},{3,2},{4,5},{5,4},{6,7},{7,6},{8,9},{9,8},{10,11... | collective-permute-start | bytes 1622024 | tf_op jit(solution)/shard_map/ppermute | solution.py:475
  6.7 5.1 %own_gains.1 = (f32[1032,512]{1,0:T(8,128)S(1)}, f32[1032,512]{1,0:T(8,128)S(1)}, f32[776,512]{1,0:T(8,128)S(1)}, f32[264,512]{1,0:T(8,128)S(1)}) custom-call(bf16[512,512]{1,0:T(8,128)(2,1)S(1)} %get-tuple-element.51.gain_high, bf16[512,512]{1,0:T(8,128)(2,1)S(1)} %get-tuple-element.52.gain_low, ...), custom_call_target="tpu_custom_call" | custom-call | flops 4831838208 | tf_op jit(solution)/shard_map/own_gains/pallas_call | solution.py:454
  11.9 0.0 collective-permute-done.arrived
  11.9 0.4 %other_part.4 = (f32[1032,512]{1,0:T(8,128)S(1)}, f32[4,512]{1,0:T(4,128)S(1)}, f32[8,512]{1,0:T(8,128)S(1)}, f32[1032,512]{1,0:T(8,128)S(1)}) custom-call(f32[8,512]{1,0:T(8,128)S(1)} %get-tuple-element.47.entering, f32[1032,512]{1,0:T(8,128)S(1)} %collective-permute-done.arrived, f32[1032,512]{1,0:T(8,128)S(1)} %get-tuple-element.49.scaled_own.rest_0_.refs_1_, ...), custom_call_target="tpu_custom_call" | custom-call | flops 536870912 | bytes 4194304 | tf_op jit(solution)/shard_map/other_part/pallas_call | solution.py:465
  12.3 0.0 collective-permute-done.1.arrived
  12.3 0.2 other_part.5
  12.5 0.0 collective-permute-done.2.arrived
  12.5 0.2 other_part.6
  12.7 0.4 %collective-permute-done.3.arrived = f32[264,512]{1,0:T(8,128)S(1)} collective-permute-done((f32[264,512]{1,0:T(8,128)S(1)}, f32[264,512]{1,0:T(8,128)S(1)}, u32[]{:S(2)}, u32[]{:S(2)}) %collective-permute-start.3) | collective-permute-done | bytes 540704 | tf_op jit(solution)/shard_map/ppermute | solution.py:475
  13.1 0.1 other_part.7
  13.2 0.7 %collective-permute-start.4 = (f32[8,512]{1,0:T(8,128)S(1)}, f32[8,512]{1,0:T(8,128)S(1)}, u32[]{:S(2)}, u32[]{:S(2)}) collective-permute-start(f32[8,512]{1,0:T(8,128)S(1)} %get-tuple-element.66._), channel_id=1, source_target_pairs={{0,8},{8,0},{16,24},{24,16},{1,9},{9,1},{17,25},{25,17},{2,10},{10... | collective-permute-start | bytes 49160 | tf_op jit(solution)/shard_map/ppermute | solution.py:495
  13.9 5.1 %late_gains.1 = (f32[1032,512]{1,0:T(8,128)S(1)}, f32[1032,512]{1,0:T(8,128)S(1)}, f32[776,512]{1,0:T(8,128)S(1)}, f32[264,512]{1,0:T(8,128)S(1)}) custom-call(f32[8,512]{1,0:T(8,128)S(1)} %get-tuple-element.66._, bf16[512,512]{1,0:T(8,128)(2,1)S(1)} %get-tuple-element.51.gain_high, bf16[512,512]{1,0:T(8,128)(2,1)S(1)} %get-tuple-element.52.gain_low, ...), custom_call_target="tpu_custom_call" | custom-call | flops 4831838208 | tf_op jit(solution)/shard_map/late_gains/pallas_call | solution.py:481
  19.0 0.0 collective-permute-done.4.entering
  19.1 0.1 collective-permute-start.5
  19.2 3.7 %collective-permute-done.5.entering = f32[8,512]{1,0:T(8,128)S(1)} collective-permute-done((f32[8,512]{1,0:T(8,128)S(1)}, f32[8,512]{1,0:T(8,128)S(1)}, u32[]{:S(2)}, u32[]{:S(2)}) %collective-permute-start.5) | collective-permute-done | bytes 16416 | tf_op jit(solution)/shard_map/ppermute | solution.py:495
  22.9 2.2 %collective-permute-start.6 = (f32[8,512]{1,0:T(8,128)S(1)}, f32[8,512]{1,0:T(8,128)S(1)}, u32[]{:S(2)}, u32[]{:S(2)}) collective-permute-start(f32[8,512]{1,0:T(8,128)S(1)} %get-tuple-element.89), channel_id=1, source_target_pairs={{16,24},{24,16},{0,8},{8,0},{17,25},{25,17},{1,9},{9,1},{18,26},{2... | collective-permute-start | bytes 49160 | tf_op jit(solution)/shard_map/ppermute | solution.py:495
  25.1 0.6 %finished.1 = (f32[12,128]{1,0:T(8,128)}, f32[12,256]{1,0:T(8,128)}) custom-call(f32[12,512]{1,0:T(8,128)S(1)} %get-tuple-element.86.states, f32[4,256,512]{2,1,0:T(8,128)S(1)} %get-tuple-element.68.refs_0_, f32[4,256,512]{2,1,0:T(8,128)S(1)} %get-tuple-element.75.refs_5_.refs_1_, f32[3,256,512]{2,1,0:T(8,128)S(1)} %get-tuple-element.78.refs_10_.refs_2_, ...), custom_call_target="tpu_custom_call" | custom-call | flops 4831838208 | tf_op jit(solution)/shard_map/finished/pallas_call | solution.py:509
  25.7 1.1 %collective-permute-done.6.entering = f32[8,512]{1,0:T(8,128)S(1)} collective-permute-done((f32[8,512]{1,0:T(8,128)S(1)}, f32[8,512]{1,0:T(8,128)S(1)}, u32[]{:S(2)}, u32[]{:S(2)}) %collective-permute-start.6) | collective-permute-done | bytes 16416 | tf_op jit(solution)/shard_map/ppermute | solution.py:495
  26.8 3.0 %last_chain.1 = (f32[12,128]{1,0:T(8,128)}, f32[12,256]{1,0:T(8,128)}) custom-call(f32[12,128]{1,0:T(8,128)} %get-tuple-element.87.ready_states, f32[12,256]{1,0:T(8,128)} %get-tuple-element.88.ready, f32[8,512]{1,0:T(8,128)S(1)} %collective-permute-done.6.entering, ...), custom_call_target="tpu_custom_call", output_to_operand_aliasing={{0}: (0, {}), {1}: (1, {})} | custom-call | flops 4831838208 | tf_op jit(solution)/shard_map/last_chain/pallas_call | solution.py:517
  (3 shorter events, 0.0 us)
Async XLA Ops:
  0.6 2.2 %copy-start = (f32[512,512]{1,0:T(8,128)S(1)}, f32[512,512]{1,0:T(8,128)}, u32[]{:S(2)}) copy-start(f32[512,512]{1,0:T(8,128)} %blend.15) | copy-start | bytes 3145732
  0.6 2.2 %copy-start.1 = (f32[512]{0:T(512)S(1)}, f32[512]{0:T(512)}, u32[]{:S(2)}) copy-start(f32[512]{0:T(512)} %param.15) | copy-start | bytes 6148
  0.7 2.2 %copy-start.2 = (s32[256]{0:T(256)S(1)}, s32[256]{0:T(256)}, u32[]{:S(2)}) copy-start(s32[256]{0:T(256)} %param.14) | copy-start | bytes 3076
  0.7 2.2 %copy-start.3 = (f32[4]{0:T(128)S(1)}, f32[4]{0:T(128)}, u32[]{:S(2)}) copy-start(f32[4]{0:T(128)} %param.13) | copy-start | bytes 52
  2.8 9.1 %collective-permute-start = (f32[1032,512]{1,0:T(8,128)S(1)}, f32[1032,512]{1,0:T(8,128)S(1)}, u32[]{:S(2)}, u32[]{:S(2)}) collective-permute-start(f32[1032,512]{1,0:T(8,128)S(1)} %get-tuple-element.48), channel_id=1, source_target_pairs={{0,1},{1,0},{2,3},{3,2},{4,5},{5,4},{6,7},{7,6},{8,9},{9,8},{10,11... | collective-permute-start | bytes 6340616 | tf_op jit(solution)/shard_map/ppermute | solution.py:475
  5.7 6.6 %collective-permute-start.1 = (f32[1032,512]{1,0:T(8,128)S(1)}, f32[1032,512]{1,0:T(8,128)S(1)}, u32[]{:S(2)}, u32[]{:S(2)}) collective-permute-start(f32[1032,512]{1,0:T(8,128)S(1)} %get-tuple-element.55), channel_id=1, source_target_pairs={{0,1},{1,0},{2,3},{3,2},{4,5},{5,4},{6,7},{7,6},{8,9},{9,8},{10,11... | collective-permute-start | bytes 6340616 | tf_op jit(solution)/shard_map/ppermute | solution.py:475
  6.2 6.3 %collective-permute-start.2 = (f32[776,512]{1,0:T(8,128)S(1)}, f32[776,512]{1,0:T(8,128)S(1)}, u32[]{:S(2)}, u32[]{:S(2)}) collective-permute-start(f32[776,512]{1,0:T(8,128)S(1)} %get-tuple-element.59), channel_id=1, source_target_pairs={{0,1},{1,0},{2,3},{3,2},{4,5},{5,4},{6,7},{7,6},{8,9},{9,8},{10,11... | collective-permute-start | bytes 4767752 | tf_op jit(solution)/shard_map/ppermute | solution.py:475
  6.3 6.8 %collective-permute-start.3 = (f32[264,512]{1,0:T(8,128)S(1)}, f32[264,512]{1,0:T(8,128)S(1)}, u32[]{:S(2)}, u32[]{:S(2)}) collective-permute-start(f32[264,512]{1,0:T(8,128)S(1)} %get-tuple-element.63), channel_id=1, source_target_pairs={{0,1},{1,0},{2,3},{3,2},{4,5},{5,4},{6,7},{7,6},{8,9},{9,8},{10,11... | collective-permute-start | bytes 1622024 | tf_op jit(solution)/shard_map/ppermute | solution.py:475
  13.2 5.9 %collective-permute-start.4 = (f32[8,512]{1,0:T(8,128)S(1)}, f32[8,512]{1,0:T(8,128)S(1)}, u32[]{:S(2)}, u32[]{:S(2)}) collective-permute-start(f32[8,512]{1,0:T(8,128)S(1)} %get-tuple-element.66._), channel_id=1, source_target_pairs={{0,8},{8,0},{16,24},{24,16},{1,9},{9,1},{17,25},{25,17},{2,10},{10... | collective-permute-start | bytes 49160 | tf_op jit(solution)/shard_map/ppermute | solution.py:495
  19.1 3.8 %collective-permute-start.5 = (f32[8,512]{1,0:T(8,128)S(1)}, f32[8,512]{1,0:T(8,128)S(1)}, u32[]{:S(2)}, u32[]{:S(2)}) collective-permute-start(f32[8,512]{1,0:T(8,128)S(1)} %get-tuple-element.85), channel_id=1, source_target_pairs={{0,8},{8,16},{16,24},{24,0},{1,9},{9,17},{17,25},{25,1},{2,10},{10... | collective-permute-start | bytes 49160 | tf_op jit(solution)/shard_map/ppermute | solution.py:495
  22.9 3.9 %collective-permute-start.6 = (f32[8,512]{1,0:T(8,128)S(1)}, f32[8,512]{1,0:T(8,128)S(1)}, u32[]{:S(2)}, u32[]{:S(2)}) collective-permute-start(f32[8,512]{1,0:T(8,128)S(1)} %get-tuple-element.89), channel_id=1, source_target_pairs={{16,24},{24,16},{0,8},{8,0},{17,25},{25,17},{1,9},{9,1},{18,26},{2... | collective-permute-start | bytes 49160 | tf_op jit(solution)/shard_map/ppermute | solution.py:495

commit v7 on v6

--- a/solution.py
+++ b/solution.py
@@ -11,7 +11,7 @@
 VMEM_LIMIT = 8 * 2**20
 LAST_PART = 1
 PARTS = 4
-GAIN_STEPS = (0, 8, 10)
+GAIN_STEPS = (0, 9, 10)
 EARLY_STEPS = (0, 4, 3, 0)
 WHOLE = pl.BlockSpec(memory_space=pltpu.VMEM)
 FAR = pl.BlockSpec(memory_space=pl.ANY)

time: 30.2 us -> 30.2 us (level)
  no operation moved by 1% of the time
where the time goes in v7:
time: 30.2 us; the launch traced here: 30 us
  Pallas kernels  19.6 us (65%)
  waiting for transfers between devices  5.29 us (18%)
  starting transfers between devices  4.06 us (13%)
  between operations  1.01 us (3%)
    pallas_call x1, Pallas kernels, per_device(): call(functools.partial(late_kernel, firsts, sizes, steps), 'late_gains',...  5.13 us
    pallas_call x1, Pallas kernels, per_device(): call(functools.partial(gain_kernel, firsts, sizes, steps), 'own_gains', [...  5.13 us
    ppermute x3, waiting for transfers between devices, per_device(): entering = lax.ppermute(leaving, 'tm', hop_pairs(turn, blocks))  4.84 us
    pallas_call x1, Pallas kernels, per_device(): call(functools.partial(last_kernel, last, count), 'last_chain', outputs,...  3.05 us
    ppermute x3, starting transfers between devices, per_device(): entering = lax.ppermute(leaving, 'tm', hop_pairs(turn, blocks))  2.94 us
    pallas_call x1, Pallas kernels, per_device(): call(functools.partial(rest_kernel, firsts[1:], steps), 'rest', [kept(2,...  2.76 us
    pallas_call x1, Pallas kernels, per_device(): call(stage_kernel, 'stage', chunk(sizes[0]) + [kept(outs, 128)], [FAR] *...  2.12 us
    ppermute x4, starting transfers between devices, per_device(): other(sent[i])  1.12 us
  transfers between devices with their start and end apart: 7, of which 3 were waited for; matrix products, arithmetic and copies ran while one was open for 0% of the time, Pallas kernels for 48%

profile of v7, /device:TPU:24, one launch (start us, length us, event | category | flops | bytes accessed | tf_op | source)
XLA Modules:
  0.0 30.0 jit_solution(6495118093067409862)
XLA Ops:
  0.6 0.0 copy-start
  0.6 0.0 copy-start.1
  0.7 0.0 copy-start.2
  0.7 0.0 copy-start.3
  0.7 2.1 %stage.1 = (f32[4,256,512]{2,1,0:T(8,128)S(1)}, f32[1032,512]{1,0:T(8,128)S(1)}, f32[1032,512]{1,0:T(8,128)S(1)}, f32[256,128]{1,0:T(8,128)S(1)}) custom-call(f32[12,256,512]{2,1,0:T(8,128)} %loads_far.3, s32[12,256]{1,0:T(8,128)} %observed_far.1, f32[12,256]{1,0:T(8,128)} %observations_far.1, f32[1,256]{1,0:T(1,128)} %bitcast.7), custom_call_target="tpu_custom_call" | custom-call | bytes 4194304 | tf_op jit(solution)/shard_map/stage/pallas_call | solution.py:425
  2.8 0.1 collective-permute-start
  2.9 0.0 copy-done
  2.9 0.0 copy-done.1
  2.9 0.0 copy-done.2
  2.9 0.0 copy-done.3
  2.9 2.8 %rest.1 = (f32[2,8,512]{2,1,0:T(8,128)S(1)}, bf16[512,512]{1,0:T(8,128)(2,1)S(1)}, bf16[512,512]{1,0:T(8,128)(2,1)S(1)}, f32[8,512]{1,0:T(8,128)S(1)}, f32[4,256...) custom-call(f32[12,256,512]{2,1,0:T(8,128)} %loads_far.3, ...), custom_call_target="tpu_custom_call" | custom-call | bytes 8388608 | tf_op jit(solution)/shard_map/rest/pallas_call | solution.py:440
  5.7 0.5 %collective-permute-start.1 = (f32[1032,512]{1,0:T(8,128)S(1)}, f32[1032,512]{1,0:T(8,128)S(1)}, u32[]{:S(2)}, u32[]{:S(2)}) collective-permute-start(f32[1032,512]{1,0:T(8,128)S(1)} %get-tuple-element.55), channel_id=1, source_target_pairs={{0,1},{1,0},{2,3},{3,2},{4,5},{5,4},{6,7},{7,6},{8,9},{9,8},{10,11... | collective-permute-start | bytes 6340616 | tf_op jit(solution)/shard_map/ppermute | solution.py:475
  6.2 0.1 collective-permute-start.2
  6.3 0.4 %collective-permute-start.3 = (f32[264,512]{1,0:T(8,128)S(1)}, f32[264,512]{1,0:T(8,128)S(1)}, u32[]{:S(2)}, u32[]{:S(2)}) collective-permute-start(f32[264,512]{1,0:T(8,128)S(1)} %get-tuple-element.63), channel_id=1, source_target_pairs={{0,1},{1,0},{2,3},{3,2},{4,5},{5,4},{6,7},{7,6},{8,9},{9,8},{10,11... | collective-permute-start | bytes 1622024 | tf_op jit(solution)/shard_map/ppermute | solution.py:475
  6.7 5.1 %own_gains.1 = (f32[1032,512]{1,0:T(8,128)S(1)}, f32[1032,512]{1,0:T(8,128)S(1)}, f32[776,512]{1,0:T(8,128)S(1)}, f32[264,512]{1,0:T(8,128)S(1)}) custom-call(bf16[512,512]{1,0:T(8,128)(2,1)S(1)} %get-tuple-element.51.gain_high, bf16[512,512]{1,0:T(8,128)(2,1)S(1)} %get-tuple-element.52.gain_low, ...), custom_call_target="tpu_custom_call" | custom-call | flops 4831838208 | tf_op jit(solution)/shard_map/own_gains/pallas_call | solution.py:454
  11.9 0.0 collective-permute-done.arrived
  11.9 0.4 %other_part.4 = (f32[1032,512]{1,0:T(8,128)S(1)}, f32[4,512]{1,0:T(4,128)S(1)}, f32[8,512]{1,0:T(8,128)S(1)}, f32[1032,512]{1,0:T(8,128)S(1)}) custom-call(f32[8,512]{1,0:T(8,128)S(1)} %get-tuple-element.47.entering, f32[1032,512]{1,0:T(8,128)S(1)} %collective-permute-done.arrived, f32[1032,512]{1,0:T(8,128)S(1)} %get-tuple-element.49.scaled_own.rest_0_.refs_1_, ...), custom_call_target="tpu_custom_call" | custom-call | flops 536870912 | bytes 4194304 | tf_op jit(solution)/shard_map/other_part/pallas_call | solution.py:465
  12.3 0.0 collective-permute-done.1.arrived
  12.3 0.2 other_part.5
  12.5 0.0 collective-permute-done.2.arrived
  12.5 0.2 other_part.6
  12.7 0.4 %collective-permute-done.3.arrived = f32[264,512]{1,0:T(8,128)S(1)} collective-permute-done((f32[264,512]{1,0:T(8,128)S(1)}, f32[264,512]{1,0:T(8,128)S(1)}, u32[]{:S(2)}, u32[]{:S(2)}) %collective-permute-start.3) | collective-permute-done | bytes 540704 | tf_op jit(solution)/shard_map/ppermute | solution.py:475
  13.1 0.1 other_part.7
  13.2 0.7 %collective-permute-start.4 = (f32[8,512]{1,0:T(8,128)S(1)}, f32[8,512]{1,0:T(8,128)S(1)}, u32[]{:S(2)}, u32[]{:S(2)}) collective-permute-start(f32[8,512]{1,0:T(8,128)S(1)} %get-tuple-element.66._), channel_id=1, source_target_pairs={{0,8},{8,0},{16,24},{24,16},{1,9},{9,1},{17,25},{25,17},{2,10},{10... | collective-permute-start | bytes 49160 | tf_op jit(solution)/shard_map/ppermute | solution.py:495
  13.9 5.1 %late_gains.1 = (f32[1032,512]{1,0:T(8,128)S(1)}, f32[1032,512]{1,0:T(8,128)S(1)}, f32[776,512]{1,0:T(8,128)S(1)}, f32[264,512]{1,0:T(8,128)S(1)}) custom-call(f32[8,512]{1,0:T(8,128)S(1)} %get-tuple-element.66._, bf16[512,512]{1,0:T(8,128)(2,1)S(1)} %get-tuple-element.51.gain_high, bf16[512,512]{1,0:T(8,128)(2,1)S(1)} %get-tuple-element.52.gain_low, ...), custom_call_target="tpu_custom_call" | custom-call | flops 4831838208 | tf_op jit(solution)/shard_map/late_gains/pallas_call | solution.py:481
  19.0 0.0 collective-permute-done.4.entering
  19.1 0.1 collective-permute-start.5
  19.2 3.7 %collective-permute-done.5.entering = f32[8,512]{1,0:T(8,128)S(1)} collective-permute-done((f32[8,512]{1,0:T(8,128)S(1)}, f32[8,512]{1,0:T(8,128)S(1)}, u32[]{:S(2)}, u32[]{:S(2)}) %collective-permute-start.5) | collective-permute-done | bytes 16416 | tf_op jit(solution)/shard_map/ppermute | solution.py:495
  22.9 2.2 %collective-permute-start.6 = (f32[8,512]{1,0:T(8,128)S(1)}, f32[8,512]{1,0:T(8,128)S(1)}, u32[]{:S(2)}, u32[]{:S(2)}) collective-permute-start(f32[8,512]{1,0:T(8,128)S(1)} %get-tuple-element.89), channel_id=1, source_target_pairs={{16,24},{24,16},{0,8},{8,0},{17,25},{25,17},{1,9},{9,1},{18,26},{2... | collective-permute-start | bytes 49160 | tf_op jit(solution)/shard_map/ppermute | solution.py:495
  25.1 0.6 %finished.1 = (f32[12,128]{1,0:T(8,128)}, f32[12,256]{1,0:T(8,128)}) custom-call(f32[12,512]{1,0:T(8,128)S(1)} %get-tuple-element.86.states, f32[4,256,512]{2,1,0:T(8,128)S(1)} %get-tuple-element.68.refs_0_, f32[4,256,512]{2,1,0:T(8,128)S(1)} %get-tuple-element.75.refs_5_.refs_1_, f32[3,256,512]{2,1,0:T(8,128)S(1)} %get-tuple-element.78.refs_10_.refs_2_, ...), custom_call_target="tpu_custom_call" | custom-call | flops 4831838208 | tf_op jit(solution)/shard_map/finished/pallas_call | solution.py:509
  25.7 1.1 %collective-permute-done.6.entering = f32[8,512]{1,0:T(8,128)S(1)} collective-permute-done((f32[8,512]{1,0:T(8,128)S(1)}, f32[8,512]{1,0:T(8,128)S(1)}, u32[]{:S(2)}, u32[]{:S(2)}) %collective-permute-start.6) | collective-permute-done | bytes 16416 | tf_op jit(solution)/shard_map/ppermute | solution.py:495
  26.8 3.0 %last_chain.1 = (f32[12,128]{1,0:T(8,128)}, f32[12,256]{1,0:T(8,128)}) custom-call(f32[12,128]{1,0:T(8,128)} %get-tuple-element.87.ready_states, f32[12,256]{1,0:T(8,128)} %get-tuple-element.88.ready, f32[8,512]{1,0:T(8,128)S(1)} %collective-permute-done.6.entering, ...), custom_call_target="tpu_custom_call", output_to_operand_aliasing={{0}: (0, {}), {1}: (1, {})} | custom-call | flops 4831838208 | tf_op jit(solution)/shard_map/last_chain/pallas_call | solution.py:517
  (3 shorter events, 0.0 us)
Async XLA Ops:
  0.6 2.2 %copy-start = (f32[512,512]{1,0:T(8,128)S(1)}, f32[512,512]{1,0:T(8,128)}, u32[]{:S(2)}) copy-start(f32[512,512]{1,0:T(8,128)} %blend.15) | copy-start | bytes 3145732
  0.6 2.2 %copy-start.1 = (f32[512]{0:T(512)S(1)}, f32[512]{0:T(512)}, u32[]{:S(2)}) copy-start(f32[512]{0:T(512)} %param.15) | copy-start | bytes 6148
  0.7 2.2 %copy-start.2 = (s32[256]{0:T(256)S(1)}, s32[256]{0:T(256)}, u32[]{:S(2)}) copy-start(s32[256]{0:T(256)} %param.14) | copy-start | bytes 3076
  0.7 2.2 %copy-start.3 = (f32[4]{0:T(128)S(1)}, f32[4]{0:T(128)}, u32[]{:S(2)}) copy-start(f32[4]{0:T(128)} %param.13) | copy-start | bytes 52
  2.8 9.1 %collective-permute-start = (f32[1032,512]{1,0:T(8,128)S(1)}, f32[1032,512]{1,0:T(8,128)S(1)}, u32[]{:S(2)}, u32[]{:S(2)}) collective-permute-start(f32[1032,512]{1,0:T(8,128)S(1)} %get-tuple-element.48), channel_id=1, source_target_pairs={{0,1},{1,0},{2,3},{3,2},{4,5},{5,4},{6,7},{7,6},{8,9},{9,8},{10,11... | collective-permute-start | bytes 6340616 | tf_op jit(solution)/shard_map/ppermute | solution.py:475
  5.7 6.6 %collective-permute-start.1 = (f32[1032,512]{1,0:T(8,128)S(1)}, f32[1032,512]{1,0:T(8,128)S(1)}, u32[]{:S(2)}, u32[]{:S(2)}) collective-permute-start(f32[1032,512]{1,0:T(8,128)S(1)} %get-tuple-element.55), channel_id=1, source_target_pairs={{0,1},{1,0},{2,3},{3,2},{4,5},{5,4},{6,7},{7,6},{8,9},{9,8},{10,11... | collective-permute-start | bytes 6340616 | tf_op jit(solution)/shard_map/ppermute | solution.py:475
  6.2 6.3 %collective-permute-start.2 = (f32[776,512]{1,0:T(8,128)S(1)}, f32[776,512]{1,0:T(8,128)S(1)}, u32[]{:S(2)}, u32[]{:S(2)}) collective-permute-start(f32[776,512]{1,0:T(8,128)S(1)} %get-tuple-element.59), channel_id=1, source_target_pairs={{0,1},{1,0},{2,3},{3,2},{4,5},{5,4},{6,7},{7,6},{8,9},{9,8},{10,11... | collective-permute-start | bytes 4767752 | tf_op jit(solution)/shard_map/ppermute | solution.py:475
  6.3 6.8 %collective-permute-start.3 = (f32[264,512]{1,0:T(8,128)S(1)}, f32[264,512]{1,0:T(8,128)S(1)}, u32[]{:S(2)}, u32[]{:S(2)}) collective-permute-start(f32[264,512]{1,0:T(8,128)S(1)} %get-tuple-element.63), channel_id=1, source_target_pairs={{0,1},{1,0},{2,3},{3,2},{4,5},{5,4},{6,7},{7,6},{8,9},{9,8},{10,11... | collective-permute-start | bytes 1622024 | tf_op jit(solution)/shard_map/ppermute | solution.py:475
  13.2 5.9 %collective-permute-start.4 = (f32[8,512]{1,0:T(8,128)S(1)}, f32[8,512]{1,0:T(8,128)S(1)}, u32[]{:S(2)}, u32[]{:S(2)}) collective-permute-start(f32[8,512]{1,0:T(8,128)S(1)} %get-tuple-element.66._), channel_id=1, source_target_pairs={{0,8},{8,0},{16,24},{24,16},{1,9},{9,1},{17,25},{25,17},{2,10},{10... | collective-permute-start | bytes 49160 | tf_op jit(solution)/shard_map/ppermute | solution.py:495
  19.1 3.8 %collective-permute-start.5 = (f32[8,512]{1,0:T(8,128)S(1)}, f32[8,512]{1,0:T(8,128)S(1)}, u32[]{:S(2)}, u32[]{:S(2)}) collective-permute-start(f32[8,512]{1,0:T(8,128)S(1)} %get-tuple-element.85), channel_id=1, source_target_pairs={{0,8},{8,16},{16,24},{24,0},{1,9},{9,17},{17,25},{25,1},{2,10},{10... | collective-permute-start | bytes 49160 | tf_op jit(solution)/shard_map/ppermute | solution.py:495
  22.9 3.9 %collective-permute-start.6 = (f32[8,512]{1,0:T(8,128)S(1)}, f32[8,512]{1,0:T(8,128)S(1)}, u32[]{:S(2)}, u32[]{:S(2)}) collective-permute-start(f32[8,512]{1,0:T(8,128)S(1)} %get-tuple-element.89), channel_id=1, source_target_pairs={{16,24},{24,16},{0,8},{8,0},{17,25},{25,17},{1,9},{9,1},{18,26},{2... | collective-permute-start | bytes 49160 | tf_op jit(solution)/shard_map/ppermute | solution.py:495
